TPU v7x, 128 devices: a whole 4x4x4 slice. The times are simulated.
128 devices in a mesh: region: 32 (over x, y, core), sub: 4 (over z).
Axes of the slice: x: 4, y: 4, z: 4, core: 2. Of those that a mesh axis runs over, the one named last changes fastest.
Arguments:
- interior_inverse: float32 [512, 512, 512], P(('region', 'sub')), may hold values from -0.12 to 12, as said below
- coupling: float32 [512, 4, 512, 128], P(('region', 'sub')), may hold values from -0.25 to 0.25
- interior_grad: float32 [512, 512, 128], P(('region', 'sub')), may hold values from -6 to 6
- separator_hessian_blocks: float32 [512, 128, 128], P(('region', 'sub')), may hold values from -12 to 290, as said below
- sep_grad: float32 [512, 128, 128], P(('region', 'sub')), may hold values from -384 to 384
- lists: int32 [512, 4], replicated, may hold values from 0 to 511, as said below
- owner: int32 [512], replicated, may hold values from 0 to 511, as said below
- counts: int32 [512], replicated, may hold values from 1 to 4
Outputs:
- interior_solution: float32 [512, 512, 128], P(('region', 'sub'))
- separator_solution: float32 [512, 128, 128], P(('region', 'sub'))
- separator_residual: float32 [512, 128, 128], P(('region', 'sub'))
Inputs may be any that keep to these rules, and one draw needn't show every extreme that they name: `owner`: A permutation of the 512 positions; position p lies on device p // 4 in the order region, then sub. Submap i lies on device i // 4. Each submap lists distinct tiles. Every listing names a tile owned by a device of the submap's region or of the next region (the last region's next is the first); of the 16 listings of one device, exactly 2 name tiles of each of these 8 owners. Only the first counts[i] listings of submap i are live. `interior_inverse`: symmetric positive definite. `separator_hessian_blocks`: Symmetric; with the couplings the whole system is positive definite.
All inputs are finite; a program needn't handle non-finite values.
Results may differ from a plain program's by a relative error of at most 0.0003.
Values sent between devices are 32-bit elements; how exact they have to be, the bound alone decides.
No kernel may reach another device: no remote copies, remote signals or barrier semaphores. Data moves between devices by JAX's collectives and lax.ppermute only.
A program may use at most 128 MiB of HBM per device.

v0:
```python
import jax
import jax.numpy as jnp
from jax import lax
from jax.sharding import PartitionSpec as P

CHEB = 2


TOP_ACCURACY = lax.Precision.HIGHEST


def from_behind(x, axis, by):
    count = lax.axis_size(axis)
    return lax.ppermute(x, axis, [(i, (i + by) % count) for i in range(count)])


def tile_solve(factor_tile, right_tile):
    return jax.scipy.linalg.cho_solve((factor_tile, True), right_tile)


def route_plan(device, lists, owner, counts, sub_dev, sep_dev, n_region, n_sub):
    slots = lists.shape[1]
    per_dev = sub_dev * slots
    capacity = per_dev // (2 * n_sub)
    rows_here = lax.dynamic_slice_in_dim(lists, device * sub_dev, sub_dev, 0).reshape(-1)
    count_here = lax.dynamic_slice_in_dim(counts, device * sub_dev, sub_dev, 0)
    tile_ids = jnp.arange(owner.shape[0], dtype=jnp.int32)
    matches = rows_here[:, None] == tile_ids[None, :]
    position = jnp.sum(jnp.where(matches, owner[None, :], 0), axis=1)
    owner_dev = position // sep_dev
    resident_tile = position % sep_dev
    offset = (owner_dev // n_sub - device // n_sub) % n_region
    dest = offset * n_sub + owner_dev % n_sub
    order_ids = jnp.arange(per_dev, dtype=jnp.int32)
    earlier = (dest[:, None] == dest[None, :]) & (order_ids[None, :] < order_ids[:, None])
    rank = jnp.sum(earlier.astype(jnp.int32), axis=1)
    slot_at = dest * capacity + rank
    is_live = (jnp.arange(slots, dtype=jnp.int32)[None, :] < count_here[:, None]).reshape(-1)
    return (slot_at, resident_tile, is_live)


def deliver(packed, hop_sign, n_sub):
    shaped = packed.reshape((2, n_sub, -1) + packed.shape[1:])
    block = lax.all_to_all(shaped, "sub", split_axis=1, concat_axis=1, tiled=True)
    moved = from_behind(block[1], "region", hop_sign)
    shaped = jnp.concatenate([block[:1], moved[None]], axis=0)
    return shaped.reshape(packed.shape)


def per_device(
    interior_inverse,
    coupling,
    interior_grad,
    separator_hessian_blocks,
    sep_grad,
    lists,
    owner,
    counts,
):
    sub_dev, slots, ni_size, tile_size = coupling.shape
    nrhs_size = interior_grad.shape[2]
    sep_dev = separator_hessian_blocks.shape[0]
    span_cols = slots * tile_size
    per_dev = sub_dev * slots
    n_region = lax.axis_size("region")
    n_sub = lax.axis_size("sub")
    capacity = per_dev // (2 * n_sub)
    region_here = lax.axis_index("region")
    sub_here = lax.axis_index("sub")
    device = region_here * n_sub + sub_here
    slot_at, resident_tile, is_live = route_plan(
        device, lists, owner, counts, sub_dev, sep_dev, n_region, n_sub
    )
    order_ids = jnp.arange(per_dev, dtype=jnp.int32)
    buffer_order = jnp.sum(
        order_ids[None, :] * (slot_at[None, :] == order_ids[:, None]).astype(jnp.int32), axis=1
    )
    offsets = jnp.arange(2, dtype=jnp.int32)[:, None]
    sub_ids = jnp.arange(n_sub, dtype=jnp.int32)[None, :]
    sources = ((region_here - offsets) % n_region * n_sub + sub_ids).reshape(-1)

    def plan_source(source):
        return route_plan(source, lists, owner, counts, sub_dev, sep_dev, n_region, n_sub)

    src_at, src_local, _ = jax.vmap(plan_source)(sources)
    pair_ids = jnp.arange(2 * n_sub, dtype=jnp.int32)
    targets = (pair_ids // n_sub * n_sub + sub_here)[:, None] * capacity + jnp.arange(
        capacity, dtype=jnp.int32
    )[None, :]
    hit = src_at[:, None, :] == targets[:, :, None]
    local_in = jnp.sum(jnp.where(hit, src_local[:, None, :], 0), axis=2).reshape(-1)
    collect = (local_in[None, :] == jnp.arange(sep_dev, dtype=jnp.int32)[:, None]).astype(
        jnp.float32
    )

    def to_owner(slot_contents):
        return deliver(jnp.take(slot_contents, buffer_order, axis=0), 1, n_sub)

    def to_sources(owner_data):
        arrived = deliver(owner_data, -1, n_sub)
        return jnp.take(arrived, slot_at, axis=0)

    live_mask = is_live.reshape(sub_dev, slots).astype(jnp.float32)
    masked = coupling * live_mask[:, :, None, None]
    cat_cols = jnp.transpose(masked, (0, 2, 1, 3)).reshape(sub_dev, ni_size, span_cols)
    solved = jnp.einsum("bij,bjk->bik", interior_inverse, cat_cols, precision=TOP_ACCURACY)
    schur = jnp.einsum("bji,bjk->bik", cat_cols, solved, precision=TOP_ACCURACY)
    reduced = jnp.einsum("bij,bjk->bik", interior_inverse, interior_grad, precision=TOP_ACCURACY)
    pushed = jnp.einsum("bji,bjk->bik", cat_cols, reduced, precision=TOP_ACCURACY)
    schur_five = schur.reshape(sub_dev, slots, tile_size, slots, tile_size)
    diag_tiles = jnp.stack([schur_five[:, j, :, j, :] for j in range(slots)], axis=1)
    payload = jnp.concatenate(
        [diag_tiles, pushed.reshape(sub_dev, slots, tile_size, nrhs_size)], axis=-1
    )
    incoming = to_owner(payload.reshape(per_dev, tile_size, tile_size + nrhs_size))
    summed = jnp.einsum("tk,kab->tab", collect, incoming, precision=TOP_ACCURACY)
    blockdiag = separator_hessian_blocks - summed[:, :, :tile_size]
    rhs_zero = sep_grad - summed[:, :, tile_size:]
    factors = jnp.linalg.cholesky(blockdiag)

    def precond(resid):
        return jax.vmap(tile_solve)(factors, resid)

    def schur_operator_apply(input_vector):
        outgoing = jnp.take(input_vector, local_in, axis=0)
        listed = to_sources(outgoing)
        product = jnp.einsum(
            "bij,bjk->bik",
            schur,
            listed.reshape(sub_dev, span_cols, nrhs_size),
            precision=TOP_ACCURACY,
        )
        returned = to_owner(product.reshape(per_dev, tile_size, nrhs_size))
        gathered_sum = jnp.einsum("tk,kab->tab", collect, returned, precision=TOP_ACCURACY)
        owned_portion = jnp.einsum(
            "zvl,zlo->zvo", separator_hessian_blocks, input_vector, precision=TOP_ACCURACY
        )
        return (owned_portion - gathered_sum, listed)

    z_zero = precond(rhs_zero)
    first = lax.psum(jnp.sum(rhs_zero * z_zero), ("region", "sub"))
    image, seen = schur_operator_apply(z_zero)
    resid = rhs_zero - image
    z_resid = precond(resid)
    latter_term = lax.psum(jnp.sum(resid * z_resid), ("region", "sub"))
    quotient = latter_term / first
    solution = z_zero
    direction = z_zero
    kept = seen
    gamma_prev = 1.0
    for sweep in range(CHEB):
        gamma = 1.0 / (2.0 - quotient * gamma_prev)
        direction = quotient * gamma * gamma_prev * direction + 2.0 * gamma * z_resid
        solution = solution + direction
        image, seen = schur_operator_apply(direction)
        kept = kept + seen
        resid = resid - image
        if sweep + 1 < CHEB:
            z_resid = precond(resid)
        gamma_prev = gamma
    listed_solution = to_sources(jnp.take(solution, local_in, axis=0))
    interior = reduced - jnp.einsum(
        "bij,bjk->bik",
        solved,
        listed_solution.reshape(sub_dev, span_cols, nrhs_size),
        precision=TOP_ACCURACY,
    )
    return (interior, solution, resid)


def solution(mesh):
    placed = (
        P(("region", "sub"), None, None),
        P(("region", "sub"), None, None, None),
        P(("region", "sub"), None, None),
        P(("region", "sub"), None, None),
        P(("region", "sub"), None, None),
        P(),
        P(),
        P(),
    )
    return jax.shard_map(
        per_device,
        mesh=mesh,
        in_specs=placed,
        out_specs=(
            P(("region", "sub"), None, None),
            P(("region", "sub"), None, None),
            P(("region", "sub"), None, None),
        ),
        check_vma=False,
    )
```

profile of v0, /device:TPU:0, one launch (start us, length us, event | category | flops | bytes accessed | tf_op | source)
XLA Modules:
  0.0 515.6 jit_solution(6053636207207997948)
XLA Ops:
  3.0 5.3 %copy.176 = f32[4,4,512,128]{2,3,1,0:T(8,128)} copy(f32[4,4,512,128]{3,2,1,0:T(8,128)} %param.15) | data formatting | bytes 8388608 | tf_op args[1]
  9.3 6.0 %fusion.45 = f32[4,512,128]{2,1,0:T(8,128)S(1)} fusion(f32[4,512,512]{2,1,0:T(8,128)} %param.14, f32[4,512,128]{2,1,0:T(8,128)S(1)} %copy-done), kind=kOutput, calls=%fused_computation.181 | convolution fusion | flops 1610612736 | bytes 6291456 | tf_op jit(solution)/shard_map/bij,bjk->bik/dot_general | solution.py:108
  16.0 1.5 copy-done.4
  17.5 7.1 %fusion.46 = f32[4,512,512]{2,1,0:T(8,128)S(1)} fusion(f32[4,512,512]{1,2,0:T(8,128)S(1)} %bitcast.162, f32[4,512,512]{2,1,0:T(8,128)S(1)} %copy-done.4), kind=kOutput, calls=%fused_computation.182 | convolution fusion | flops 6442450944 | bytes 12582912 | tf_op jit(solution)/shard_map/bij,bjk->bik/dot_general | solution.py:106
  24.6 3.7 fusion.48
  28.2 8.7 %fusion.47 = f32[4,512,512]{2,1,0:T(8,128)} fusion(f32[4,512,512]{1,2,0:T(8,128)S(1)} %bitcast.164, f32[4,512,512]{2,1,0:T(8,128)S(1)} %fusion.46), kind=kOutput, calls=%fused_computation.183 | convolution fusion | flops 6442450944 | bytes 12582912 | tf_op jit(solution)/shard_map/bji,bjk->bik/dot_general | solution.py:107
  36.9 5.3 %reshape.575 = f32[4,4,128,4,128]{4,3,2,1,0:T(4,128)} reshape(f32[4,512,512]{2,1,0:T(8,128)} %fusion.47) | data formatting | bytes 8388608 | tf_op jit(solution)/shard_map/reshape | solution.py:110
  42.2 3.3 fusion.44
  45.6 1.5 pad_maximum_fusion
  47.1 3.6 gather_fusion
  50.7 5.2 %copy_select_fusion = f32[2,4,2,128,256]{4,2,3,0,1:T(2,128)} fusion(f32[2,4,2,128,256]{4,3,2,1,0:T(8,128)} %bitcast.165, pred[2,4,2]{2,0,1:T(4,128)(4,1)S(1)} %copy.182), kind=kLoop, calls=%fused_computation.17 | loop fusion | flops 524288 | bytes 4194320 | tf_op jit(solution)/shard_map/jit(_take)/select_n | solution.py:97
  55.9 5.4 %all-to-all-start = ((f32[2,4,2,128,256]{4,2,3,0,1:T(2,128)}), f32[2,4,2,128,256]{4,2,3,0,1:T(2,128)}, u32[]{:S(2)}, u32[]{:S(2)}) async-start(f32[2,4,2,128,256]{4,2,3,0,1:T(2,128)} %copy_select_fusion), calls=%async_computation | async-start | bytes 4194304 | tf_op jit(solution)/shard_map/all_to_all | solution.py:44
  61.5 16.8 %while.1 = (s32[]{:T(128)}, s32[512,4]{0,1:T(4,128)}, s32[8,2]{0,1:T(2,128)S(1)}, s32[8,4,4]{2,1,0:T(4,128)S(1)}, s32[]{:T(128)}) while((s32[]{:T(128)}, s32[512,4]{0,1:T(4,128)}, s32[8,2]{0,1:T(2,128)S(1)}, s32[8,4,4]{2,1,0:T(4,128)S(1)}, s32[]{:T(128)}) %tuple.52), condition=%wide.while_cond, body=%wide.while_body.sunk | while | flops 2 | bytes 4457 | solution.py:25
  62.1 1.4 constant_dynamic-slice_fusion.6
  64.2 1.4 constant_dynamic-slice_fusion.6
  66.3 1.4 constant_dynamic-slice_fusion.6
  68.4 1.4 constant_dynamic-slice_fusion.6
  70.5 1.4 constant_dynamic-slice_fusion.6
  79.4 8.5 %all-to-all-done = f32[2,4,2,128,256]{4,2,3,0,1:T(2,128)} async-done(((f32[2,4,2,128,256]{4,2,3,0,1:T(2,128)}), f32[2,4,2,128,256]{4,2,3,0,1:T(2,128)}, u32[]{:S(2)}, u32[]{:S(2)}) %all-to-all-start) | async-done | bytes 2097184 | tf_op jit(solution)/shard_map/all_to_all | solution.py:44
  87.9 3.2 slice_bitcast_fusion.1
  91.6 17.4 %collective-permute-done = f32[4,2,128,256]{3,1,2,0:T(2,128)} collective-permute-done((f32[4,2,128,256]{3,1,2,0:T(2,128)}, f32[4,2,128,256]{3,1,2,0:T(2,128)}, u32[]{:S(2)}, u32[]{:S(2)}) %collective-permute-start) | collective-permute-done | bytes 1048608 | tf_op jit(solution)/shard_map/ppermute | solution.py:14
  109.0 2.2 pad_maximum_fusion.1
  111.2 2.6 copy.189
  113.8 4.1 reshape.576
  117.9 2.4 fusion.42
  120.9 46.9 %custom-call.9 = f32[4,128,128]{2,1,0:T(8,128)S(1)} custom-call(f32[4,128,128]{2,1,0:T(8,128)S(1)} %fusion.15), custom_call_target="Cholesky" | custom-call | tf_op jit(solution)/shard_map/jit(cholesky)/cholesky | solution.py:119
  168.1 39.3 %custom-call.12 = f32[4,1,128,128]{2,3,1,0:T(8,128)S(1)} custom-call(f32[4,1,128,128]{3,2,1,0:T(8,128)S(1)} %select_bitcast_fusion), custom_call_target="InvertDiagBlocksLowerTriangular" | custom-call | tf_op jit(solution)/shard_map/vmap(jit(_cho_solve))/triangular_solve | solution.py:18
  210.3 3.5 all-to-all-start.1
  213.8 11.4 %all-to-all-done.1 = f32[2,4,2,128,128]{4,3,2,0,1:T(8,128)S(1)} async-done(((f32[2,4,2,128,128]{4,3,2,0,1:T(8,128)}), f32[2,4,2,128,128]{4,3,2,0,1:T(8,128)S(1)}, u32[]{:S(2)}, u32[]{:S(2)}) %all-to-all-start.1) | async-done | bytes 1048608 | tf_op jit(solution)/shard_map/all_to_all | solution.py:44
  225.6 6.7 %collective-permute-done.1 = f32[4,2,128,128]{3,2,1,0:T(8,128)S(1)} collective-permute-done((f32[4,2,128,128]{3,2,1,0:T(8,128)S(1)}, f32[4,2,128,128]{3,2,1,0:T(8,128)S(1)}, u32[]{:S(2)}, u32[]{:S(2)}) %collective-permute-start.1) | collective-permute-done | bytes 524320 | tf_op jit(solution)/shard_map/ppermute | solution.py:14
  233.3 1.8 gather_fusion.2
  235.3 6.8 %fusion.50 = f32[4,512,128]{2,1,0:T(8,128)} fusion(f32[4,512,512]{2,1,0:T(8,128)} %fusion.47, f32[4,512,128]{2,1,0:T(8,128)S(1)} %bitcast.183), kind=kOutput, calls=%fused_computation.186 | convolution fusion | flops 1610612736 | bytes 6291456 | tf_op jit(solution)/shard_map/bij,bjk->bik/dot_general | solution.py:127
  242.1 1.8 gather_fusion.3
  244.9 18.1 %all_to_all.40 = f32[2,4,2,128,128]{4,2,3,0,1:T(2,128)S(1)} all-to-all(f32[2,4,2,128,128]{4,2,3,0,1:T(2,128)S(1)} %copy.201), channel_id=1, replica_groups=mesh['region'=32,'sub'=4] {'sub'}, dimensions={1} | all-to-all | bytes 2097152 | tf_op jit(solution)/shard_map/all_to_all | solution.py:44
  265.3 10.8 %collective-permute-done.2 = f32[4,2,128,128]{3,1,2,0:T(2,128)} collective-permute-done((f32[4,2,128,128]{3,1,2,0:T(2,128)}, f32[4,2,128,128]{3,1,2,0:T(2,128)}, u32[]{:S(2)}, u32[]{:S(2)}) %collective-permute-start.2) | collective-permute-done | bytes 524320 | tf_op jit(solution)/shard_map/ppermute | solution.py:14
  276.1 1.5 pad_maximum_fusion.4
  280.4 62.0 %all-reduce.1 = (f32[]{:T(128)}, f32[]{:T(128)}) all-reduce(f32[]{:T(128)} %get-tuple-element.94, f32[]{:T(128)} %get-tuple-element.93), channel_id=1, replica_groups=mesh['region'=32,'sub'=4] {'region','sub'}, use_global_device_ids=true, to_apply=%region_9.13 | all-reduce | flops 2 | bytes 16 | tf_op jit(solution)/shard_map/psum | solution.py:145
  344.7 17.9 %all_to_all.41 = f32[2,4,2,128,128]{4,3,2,0,1:T(8,128)S(1)} all-to-all(f32[2,4,2,128,128]{4,3,2,0,1:T(8,128)S(1)} %copy.211), channel_id=1, replica_groups=mesh['region'=32,'sub'=4] {'sub'}, dimensions={1} | all-to-all | bytes 2097152 | tf_op jit(solution)/shard_map/all_to_all | solution.py:44
  363.8 6.7 %collective-permute-done.3 = f32[4,2,128,128]{3,2,1,0:T(8,128)S(1)} collective-permute-done((f32[4,2,128,128]{3,2,1,0:T(8,128)S(1)}, f32[4,2,128,128]{3,2,1,0:T(8,128)S(1)}, u32[]{:S(2)}, u32[]{:S(2)}) %collective-permute-start.3) | collective-permute-done | bytes 524320 | tf_op jit(solution)/shard_map/ppermute | solution.py:14
  371.6 1.8 gather_fusion.5
  373.5 6.8 %fusion.52 = f32[4,512,128]{2,1,0:T(8,128)} fusion(f32[4,512,512]{2,1,0:T(8,128)} %fusion.47, f32[4,512,128]{2,1,0:T(8,128)S(1)} %bitcast.185), kind=kOutput, calls=%fused_computation.188 | convolution fusion | flops 1610612736 | bytes 6291456 | tf_op jit(solution)/shard_map/bij,bjk->bik/dot_general | solution.py:127
  380.4 1.8 gather_fusion.6
  383.2 17.8 %all_to_all.42 = f32[2,4,2,128,128]{4,2,3,0,1:T(2,128)S(1)} all-to-all(f32[2,4,2,128,128]{4,2,3,0,1:T(2,128)S(1)} %copy.213), channel_id=1, replica_groups=mesh['region'=32,'sub'=4] {'sub'}, dimensions={1} | all-to-all | bytes 2097152 | tf_op jit(solution)/shard_map/all_to_all | solution.py:44
  402.7 11.4 %collective-permute-done.4 = f32[4,2,128,128]{3,1,2,0:T(2,128)} collective-permute-done((f32[4,2,128,128]{3,1,2,0:T(2,128)}, f32[4,2,128,128]{3,1,2,0:T(2,128)}, u32[]{:S(2)}, u32[]{:S(2)}) %collective-permute-start.4) | collective-permute-done | bytes 524320 | tf_op jit(solution)/shard_map/ppermute | solution.py:14
  414.1 1.5 pad_maximum_fusion.6
  418.8 1.6 gather_fusion.7
  420.4 2.4 broadcast_select_fusion.2
  423.9 4.3 all-to-all-start.6
  429.2 9.9 %all-to-all-done.6 = f32[2,4,2,128,128]{4,3,2,0,1:T(8,128)} async-done(((f32[2,4,2,128,128]{4,3,2,0,1:T(8,128)}), f32[2,4,2,128,128]{4,3,2,0,1:T(8,128)}, u32[]{:S(2)}, u32[]{:S(2)}) %all-to-all-start.6) | async-done | bytes 1048608 | tf_op jit(solution)/shard_map/all_to_all | solution.py:44
  439.1 3.5 all-to-all-start.5
  442.6 2.1 slice_bitcast_fusion.5
  444.7 2.7 collective-permute-start.6
  447.4 6.0 %all-to-all-done.5 = f32[2,4,2,128,128]{4,3,2,0,1:T(8,128)S(1)} async-done(((f32[2,4,2,128,128]{4,3,2,0,1:T(8,128)}), f32[2,4,2,128,128]{4,3,2,0,1:T(8,128)S(1)}, u32[]{:S(2)}, u32[]{:S(2)}) %all-to-all-start.5) | async-done | bytes 1048608 | tf_op jit(solution)/shard_map/all_to_all | solution.py:44
  454.5 7.6 %collective-permute-start.5 = (f32[4,2,128,128]{3,2,1,0:T(8,128)}, f32[4,2,128,128]{3,2,1,0:T(8,128)}, u32[]{:S(2)}, u32[]{:S(2)}) collective-permute-start(f32[4,2,128,128]{3,2,1,0:T(8,128)} %get-tuple-element.72), channel_id=1, source_target_pairs={{0,124},{4,0},{8,4},{12,8},{16,12},{20,16},{24,20},{28,24},{32,28}... | collective-permute-start | bytes 1572872 | tf_op jit(solution)/shard_map/ppermute | solution.py:14
  463.2 1.6 gather_fusion.10
  464.8 4.3 collective-permute-done.5
  470.4 1.7 gather_fusion.8
  472.1 2.0 broadcast_select_fusion.1
  474.9 4.6 fusion.54
  479.5 2.8 gather_fusion.11
  484.6 13.3 %all_to_all.43 = f32[2,4,2,128,128]{4,2,3,0,1:T(2,128)S(1)} all-to-all(f32[2,4,2,128,128]{4,2,3,0,1:T(2,128)S(1)} %copy.225), channel_id=1, replica_groups=mesh['region'=32,'sub'=4] {'sub'}, dimensions={1} | all-to-all | bytes 2097152 | tf_op jit(solution)/shard_map/all_to_all | solution.py:44
  500.1 10.0 %convolution_subtract_fusion = f32[4,512,128]{2,1,0:T(8,128)} fusion(f32[4,512,128]{2,1,0:T(8,128)S(1)} %fusion.45, f32[4,512,512]{2,1,0:T(8,128)} %copy-done.3, f32[4,512,128]{2,1,0:T(8,128)S(1)} %bitcast.166), kind=kOutput, calls=%fused_computation.19 | convolution fusion | flops 1610874880 | bytes 7340032 | tf_op jit(solution)/shard_map/bij,bjk->bik/dot_general | solution.py:162
  510.0 1.9 collective-permute-done.7
  511.9 1.7 pad_maximum_fusion.9
  (173 shorter events, 48.0 us)
Async XLA Ops:
  0.6 8.6 %copy-start = (f32[4,512,128]{2,1,0:T(8,128)S(1)}, f32[4,512,128]{2,1,0:T(8,128)}, u32[]{:S(2)}) copy-start(f32[4,512,128]{2,1,0:T(8,128)} %param.16) | copy-start | bytes 3145732
  8.3 7.0 %copy-start.5 = (f32[4,4,512,128]{2,3,1,0:T(8,128)S(1)}, f32[4,4,512,128]{2,3,1,0:T(8,128)}, u32[]{:S(2)}) copy-start(f32[4,4,512,128]{2,3,1,0:T(8,128)} %copy.176) | copy-start | bytes 12582916
  15.3 2.2 copy-start.4
  24.6 3.7 copy-start.3
  50.7 27.6 %copy-start.7 = (f32[4,128,128]{2,1,0:T(8,128)S(1)}, f32[4,128,128]{2,1,0:T(8,128)}, u32[]{:S(2)}) copy-start(f32[4,128,128]{2,1,0:T(8,128)} %param.17) | copy-start | bytes 786436
  50.7 28.0 %copy-start.13 = (s32[512]{0:T(512)S(1)}, s32[512]{0:T(512)}, u32[]{:S(2)}) copy-start(s32[512]{0:T(512)} %param.20) | copy-start | bytes 6148
  55.9 32.0 %all-to-all-start = ((f32[2,4,2,128,256]{4,2,3,0,1:T(2,128)}), f32[2,4,2,128,256]{4,2,3,0,1:T(2,128)}, u32[]{:S(2)}, u32[]{:S(2)}) async-start(f32[2,4,2,128,256]{4,2,3,0,1:T(2,128)} %copy_select_fusion), calls=%async_computation | async-start | bytes 4194304 | tf_op jit(solution)/shard_map/all_to_all | solution.py:44
  91.2 17.9 %collective-permute-start = (f32[4,2,128,256]{3,1,2,0:T(2,128)}, f32[4,2,128,256]{3,1,2,0:T(2,128)}, u32[]{:S(2)}, u32[]{:S(2)}) collective-permute-start(f32[4,2,128,256]{3,1,2,0:T(2,128)} %get-tuple-element.66), channel_id=1, source_target_pairs={{0,4},{4,8},{8,12},{12,16},{16,20},{20,24},{24,28},{28,32},{32,36}... | collective-permute-start | bytes 3145736 | tf_op jit(solution)/shard_map/ppermute | solution.py:14
  113.8 6.5 %copy-start.12 = (f32[4,128,128]{2,1,0:T(8,128)S(1)}, f32[4,128,128]{2,1,0:T(8,128)}, u32[]{:S(2)}) copy-start(f32[4,128,128]{2,1,0:T(8,128)} %param.18) | copy-start | bytes 786436
  210.3 14.9 %all-to-all-start.1 = ((f32[2,4,2,128,128]{4,3,2,0,1:T(8,128)}), f32[2,4,2,128,128]{4,3,2,0,1:T(8,128)S(1)}, u32[]{:S(2)}, u32[]{:S(2)}) async-start(f32[2,4,2,128,128]{4,3,2,0,1:T(8,128)} %copy.199), calls=%async_computation.1 | async-start | bytes 2097152 | tf_op jit(solution)/shard_map/all_to_all | solution.py:44
  225.3 6.9 %collective-permute-start.1 = (f32[4,2,128,128]{3,2,1,0:T(8,128)S(1)}, f32[4,2,128,128]{3,2,1,0:T(8,128)S(1)}, u32[]{:S(2)}, u32[]{:S(2)}) collective-permute-start(f32[4,2,128,128]{3,2,1,0:T(8,128)S(1)} %get-tuple-element.80), channel_id=1, source_target_pairs={{0,124},{4,0},{8,4},{12,8},{16,12},{20,16},{24,20},{28,24},{32,28}... | collective-permute-start | bytes 1572872 | tf_op jit(solution)/shard_map/ppermute | solution.py:14
  263.9 12.2 %collective-permute-start.2 = (f32[4,2,128,128]{3,1,2,0:T(2,128)}, f32[4,2,128,128]{3,1,2,0:T(2,128)}, u32[]{:S(2)}, u32[]{:S(2)}) collective-permute-start(f32[4,2,128,128]{3,1,2,0:T(2,128)} %get-tuple-element.78), channel_id=1, source_target_pairs={{0,4},{4,8},{8,12},{12,16},{16,20},{20,24},{24,28},{28,32},{32,36}... | collective-permute-start | bytes 1572872 | tf_op jit(solution)/shard_map/ppermute | solution.py:14
  362.7 7.8 %collective-permute-start.3 = (f32[4,2,128,128]{3,2,1,0:T(8,128)S(1)}, f32[4,2,128,128]{3,2,1,0:T(8,128)S(1)}, u32[]{:S(2)}, u32[]{:S(2)}) collective-permute-start(f32[4,2,128,128]{3,2,1,0:T(8,128)S(1)} %get-tuple-element.76), channel_id=1, source_target_pairs={{0,124},{4,0},{8,4},{12,8},{16,12},{20,16},{24,20},{28,24},{32,28}... | collective-permute-start | bytes 1572872 | tf_op jit(solution)/shard_map/ppermute | solution.py:14
  401.9 12.2 %collective-permute-start.4 = (f32[4,2,128,128]{3,1,2,0:T(2,128)}, f32[4,2,128,128]{3,1,2,0:T(2,128)}, u32[]{:S(2)}, u32[]{:S(2)}) collective-permute-start(f32[4,2,128,128]{3,1,2,0:T(2,128)} %get-tuple-element.74), channel_id=1, source_target_pairs={{0,4},{4,8},{8,12},{12,16},{16,20},{20,24},{24,28},{28,32},{32,36}... | collective-permute-start | bytes 1572872 | tf_op jit(solution)/shard_map/ppermute | solution.py:14
  416.5 0.7 copy-start.10
  418.2 4.6 copy-start.6
  422.8 5.3 %copy-start.9 = (f32[16,128,128]{2,1,0:T(8,128)S(1)}, f32[16,128,128]{2,1,0:T(8,128)}, u32[]{:S(2)}) copy-start(f32[16,128,128]{2,1,0:T(8,128)} %get-tuple-element.88) | copy-start | bytes 3145732
  423.9 15.2 %all-to-all-start.6 = ((f32[2,4,2,128,128]{4,3,2,0,1:T(8,128)}), f32[2,4,2,128,128]{4,3,2,0,1:T(8,128)}, u32[]{:S(2)}, u32[]{:S(2)}) async-start(f32[2,4,2,128,128]{4,3,2,0,1:T(8,128)} %copy.223), calls=%async_computation.6 | async-start | bytes 2097152 | tf_op jit(solution)/shard_map/all_to_all | solution.py:44
  439.1 14.4 %all-to-all-start.5 = ((f32[2,4,2,128,128]{4,3,2,0,1:T(8,128)}), f32[2,4,2,128,128]{4,3,2,0,1:T(8,128)S(1)}, u32[]{:S(2)}, u32[]{:S(2)}) async-start(f32[2,4,2,128,128]{4,3,2,0,1:T(8,128)} %copy.218), calls=%async_computation.5 | async-start | bytes 2097152 | tf_op jit(solution)/shard_map/all_to_all | solution.py:44
  444.7 17.4 %collective-permute-start.6 = (f32[4,2,128,128]{3,2,1,0:T(8,128)}, f32[4,2,128,128]{3,2,1,0:T(8,128)}, u32[]{:S(2)}, u32[]{:S(2)}) collective-permute-start(f32[4,2,128,128]{3,2,1,0:T(8,128)} %get-tuple-element.70), channel_id=1, source_target_pairs={{0,124},{4,0},{8,4},{12,8},{16,12},{20,16},{24,20},{28,24},{32,28}... | collective-permute-start | bytes 1572872 | tf_op jit(solution)/shard_map/ppermute | solution.py:14
  454.5 14.6 %collective-permute-start.5 = (f32[4,2,128,128]{3,2,1,0:T(8,128)}, f32[4,2,128,128]{3,2,1,0:T(8,128)}, u32[]{:S(2)}, u32[]{:S(2)}) collective-permute-start(f32[4,2,128,128]{3,2,1,0:T(8,128)} %get-tuple-element.72), channel_id=1, source_target_pairs={{0,124},{4,0},{8,4},{12,8},{16,12},{20,16},{24,20},{28,24},{32,28}... | collective-permute-start | bytes 1572872 | tf_op jit(solution)/shard_map/ppermute | solution.py:14
  472.1 2.8 copy-start.2
  482.4 16.9 %copy-start.8 = (f32[4,128,128]{2,1,0:T(8,128)S(1)}, f32[4,128,128]{2,1,0:T(8,128)}, u32[]{:S(2)}) copy-start(f32[4,128,128]{2,1,0:T(8,128)} %param.17) | copy-start | bytes 786436
  499.0 12.9 %collective-permute-start.7 = (f32[4,2,128,128]{3,1,2,0:T(2,128)}, f32[4,2,128,128]{3,1,2,0:T(2,128)}, u32[]{:S(2)}, u32[]{:S(2)}) collective-permute-start(f32[4,2,128,128]{3,1,2,0:T(2,128)} %get-tuple-element.68), channel_id=1, source_target_pairs={{0,4},{4,8},{8,12},{12,16},{16,20},{20,24},{24,28},{28,32},{32,36}... | collective-permute-start | bytes 1572872 | tf_op jit(solution)/shard_map/ppermute | solution.py:14
  500.0 13.9 %copy-start.11 = (f32[4,128,128]{2,0,1:T(4,128)S(1)}, f32[4,128,128]{2,0,1:T(4,128)}, u32[]{:S(2)}) copy-start(f32[4,128,128]{2,0,1:T(4,128)} %copy-done.10) | copy-start | bytes 786436
  500.0 15.1 %copy-start.1 = (f32[4,512,128]{2,1,0:T(8,128)S(1)}, f32[4,512,128]{2,1,0:T(8,128)}, u32[]{:S(2)}) copy-start(f32[4,512,128]{2,1,0:T(8,128)} %param.16) | copy-start | bytes 3145732
where the time goes:
time: 520 us; the launch traced here: 516 us
  blocking collectives  129 us (25%)
  other arithmetic  115 us (22%)
  waiting for transfers between devices  95 us (18%)
  local copies, waits for them, and re-layouts  81.2 us (16%)
  matrix products  62.3 us (12%)
  starting transfers between devices  29.2 us (6%)
    all_to_all x4, blocking collectives, deliver(): lax.all_to_all(shaped, 'sub', split_axis=1, concat_axis=1, tiled=True)  67.1 us
    psum x1, blocking collectives, per_device(): latter_term = lax.psum(jnp.sum(resid * z_resid), ('region', 'sub'))  62 us
    ppermute x8, waiting for transfers between devices, from_behind(): return lax.ppermute(x, axis, [(i, (i + by) % count) for i in range(count)])  59.2 us
    another operation x4, other arithmetic, per_device(): factors = jnp.linalg.cholesky(blockdiag)  47.1 us
    another operation x3, other arithmetic, tile_solve(): return jax.scipy.linalg.cho_solve((factor_tile, True), right_tile)  39.4 us
    all_to_all x4, waiting for transfers between devices, deliver(): lax.all_to_all(shaped, 'sub', split_axis=1, concat_axis=1, tiled=True)  35.8 us
    unnamed x40, local copies, waits for them, and re-layouts  18.7 us
    dot_general x3, matrix products, schur_operator_apply(): jnp.einsum('bij,bjk->bik', schur, listed.reshape(sub_dev, span_cols, nrhs...  18.3 us
  transfers between devices with their start and end apart: 12, of which 11 were waited for; matrix products, arithmetic and copies ran while one was open for 7% of the time, Pallas kernels for 0%

commit v1 on v0

v1 whole, which is shorter than its diff:
```python
import jax
import jax.numpy as jnp
from jax import lax
from jax.experimental import pallas as pl
from jax.experimental.pallas import tpu as pltpu
from jax.sharding import PartitionSpec as P

F32 = jnp.float32
BF16 = jnp.bfloat16
SUB_DEV = 4
SLOTS = 4
TILE = 128
NI = 512
NRHS = 128
SEP_DEV = 4
PER_DEV = SUB_DEV * SLOTS
BLOCK = 32
VMEM_BYTES = 56 * 1024 * 1024

ROUTES = [(0, 0), (0, 1), (0, 2), (0, 3), (1, 0), (1, 1), (1, 2), (1, 3)]


def halves(x):
    high = x.astype(BF16)
    low = (x - high.astype(F32)).astype(BF16)
    return high, low


def dot3(a, b, dims=((1,), (0,))):
    (ah, al), (bh, bl) = a, b

    def one(x, y):
        return lax.dot_general(x, y, (dims, ((), ())), preferred_element_type=F32)

    return one(ah, bl) + one(al, bh) + one(ah, bh)


def params(**kw):
    return pltpu.CompilerParams(vmem_limit_bytes=VMEM_BYTES, **kw)


SMEM = pl.BlockSpec(memory_space=pltpu.SMEM)
VMEM = pl.BlockSpec(memory_space=pltpu.VMEM)


def walk_listings(place_ref, list_ref, owner_ref, count_ref, n_region, n_sub, first, last, visit):
    region = place_ref[0]

    def clear(i, carry):
        count_ref[i] = 0
        return carry

    lax.fori_loop(0, count_ref.shape[0], clear, 0)

    def step(n, carry):
        source = n // PER_DEV
        behind = 1 - source // n_sub
        pos = owner_ref[list_ref[n]]
        owner_dev = pos // SEP_DEV
        ahead = lax.rem(owner_dev // n_sub - (region - behind) + 2 * n_region, n_region)
        owner_sub = lax.rem(owner_dev, n_sub)
        key = (source * 2 + ahead) * n_sub + owner_sub
        rank = count_ref[key]
        count_ref[key] = rank + 1
        turn = lax.rem(owner_sub - lax.rem(source, n_sub) + n_sub, n_sub)
        slot = (ahead * n_sub + turn) * 2 + rank
        visit(n, source, behind, pos, ahead, owner_sub, slot)
        return carry

    lax.fori_loop(first, last, step, 0)


def plan_kernel(n_region, n_sub, place_ref, list_ref, owner_ref, target_ref, seen_ref, own_ref, count_ref):
    region, sub = place_ref[0], place_ref[1]

    def tile_at(pos):
        dev = pos // SEP_DEV
        side = lax.rem(dev // n_sub - region + 2 * n_region, n_region)
        side = jnp.where(side == 0, 0, jnp.where(side == 1, 2, 1))
        turn = lax.rem(sub - lax.rem(dev, n_sub) + n_sub, n_sub)
        return (side * n_sub + turn) * SEP_DEV + lax.rem(pos, SEP_DEV)

    def visit(n, source, behind, pos, ahead, owner_sub, slot):
        mine = (ahead == behind) & (owner_sub == sub)
        where = jnp.where(mine, slot, PER_DEV)
        target_ref[where] = lax.rem(pos, SEP_DEV)
        base = n - lax.rem(n, SLOTS)
        for k in range(1, SLOTS):
            other = owner_ref[list_ref[base + lax.rem(lax.rem(n, SLOTS) + k, SLOTS)]]
            seen_ref[where * (SLOTS - 1) + k - 1] = jnp.where(mine, tile_at(other), 0)

    walk_listings(place_ref, list_ref, owner_ref, count_ref, n_region, n_sub, 0, 2 * n_sub * PER_DEV, visit)
    begin = (n_sub + sub) * PER_DEV

    def mine(i, carry):
        own_ref[i] = tile_at(owner_ref[list_ref[begin + i]])
        return carry

    lax.fori_loop(0, PER_DEV, mine, 0)


def plan(place, near, owner, n_region, n_sub):
    shapes = (PER_DEV + 1, (PER_DEV + 1) * (SLOTS - 1), PER_DEV)
    return pl.pallas_call(
        lambda *refs: plan_kernel(n_region, n_sub, *refs),
        out_shape=tuple(jax.ShapeDtypeStruct((n,), jnp.int32) for n in shapes),
        in_specs=[SMEM] * 3,
        out_specs=(SMEM,) * 3,
        scratch_shapes=[pltpu.SMEM((4 * n_sub * n_sub,), jnp.int32)],
        compiler_params=params(),
        name="plan",
    )(place, near, owner)


def masked_cat(coupling_ref, live):
    parts = []
    for j in range(SLOTS):
        keep = (j < live).astype(F32)
        parts.append(halves(coupling_ref[0, j] * keep))
    return parts


def eliminate_kernel(
    n_region, n_sub, place_ref, list_ref, owner_ref, live_ref, inverse_ref, coupling_ref, grad_ref,
    solved_h_ref, solved_l_ref, reduced_ref, *rest
):
    chunks, (pay_ref, right_h, right_l, slot_ref, count_ref) = rest[:8], rest[8:]
    i = pl.program_id(0)
    begin = (n_sub + place_ref[1]) * PER_DEV

    @pl.when(i == 0)
    def _():
        def visit(n, source, behind, pos, ahead, owner_sub, slot):
            slot_ref[n - begin] = slot

        walk_listings(
            place_ref, list_ref, owner_ref, count_ref, n_region, n_sub, begin, begin + PER_DEV, visit
        )

    columns = masked_cat(coupling_ref, live_ref[i])
    for j in range(SLOTS):
        right_h[:, j * TILE : (j + 1) * TILE] = columns[j][0]
        right_l[:, j * TILE : (j + 1) * TILE] = columns[j][1]
    gh, gl = halves(grad_ref[0])
    right_h[:, SLOTS * TILE :] = gh
    right_l[:, SLOTS * TILE :] = gl
    left = halves(inverse_ref[0])
    both = dot3(left, (right_h[...], right_l[...]))
    reduced = both[:, SLOTS * TILE :]
    reduced_ref[0] = reduced
    rh, rl = halves(reduced)
    for j in range(SLOTS):
        sh, sl = halves(both[:, j * TILE : (j + 1) * TILE])
        solved_h_ref[0, :, j * TILE : (j + 1) * TILE] = sh
        solved_l_ref[0, :, j * TILE : (j + 1) * TILE] = sl
        pair = (jnp.concatenate([sh, rh], axis=1), jnp.concatenate([sl, rl], axis=1))
        pay_ref[slot_ref[i * SLOTS + j]] = dot3(columns[j], pair, ((0,), (0,)))

    @pl.when(i == SUB_DEV - 1)
    def _():
        for c in range(8):
            chunks[c][...] = pay_ref[2 * c : 2 * c + 2]


def eliminate(place, near, owner, live, interior_inverse, coupling, interior_grad, n_region, n_sub):
    span = SLOTS * TILE
    wide = TILE + NRHS
    step = lambda i: (i, 0, 0)
    whole = pl.BlockSpec((2, TILE, wide), lambda i: (0, 0, 0))
    return pl.pallas_call(
        lambda *refs: eliminate_kernel(n_region, n_sub, *refs),
        grid=(SUB_DEV,),
        out_shape=(
            jax.ShapeDtypeStruct((SUB_DEV, NI, span), BF16),
            jax.ShapeDtypeStruct((SUB_DEV, NI, span), BF16),
            jax.ShapeDtypeStruct((SUB_DEV, NI, NRHS), F32),
        )
        + (jax.ShapeDtypeStruct((2, TILE, wide), F32),) * 8,
        in_specs=[SMEM] * 4
        + [
            pl.BlockSpec((1, NI, NI), step),
            pl.BlockSpec((1, SLOTS, NI, TILE), lambda i: (i, 0, 0, 0)),
            pl.BlockSpec((1, NI, NRHS), step),
        ],
        out_specs=(
            pl.BlockSpec((1, NI, span), step),
            pl.BlockSpec((1, NI, span), step),
            pl.BlockSpec((1, NI, NRHS), step),
        )
        + (whole,) * 8,
        scratch_shapes=[
            pltpu.VMEM((PER_DEV, TILE, wide), F32),
            pltpu.VMEM((NI, span + NRHS), BF16),
            pltpu.VMEM((NI, span + NRHS), BF16),
            pltpu.SMEM((PER_DEV,), jnp.int32),
            pltpu.SMEM((4 * n_sub * n_sub,), jnp.int32),
        ],
        compiler_params=params(),
        name="eliminate",
    )(place, near, owner, live, interior_inverse, coupling, interior_grad)


def couple_kernel(
    n_region, n_sub, place_ref, list_ref, owner_ref, live_ref, coupling_ref, solved_h_ref, solved_l_ref, *rest
):
    chunks, (pay_ref, cat_h, cat_l, slot_ref, count_ref) = rest[:8], rest[8:]
    i = pl.program_id(0)
    begin = (n_sub + place_ref[1]) * PER_DEV

    @pl.when(i == 0)
    def _():
        def visit(n, source, behind, pos, ahead, owner_sub, slot):
            slot_ref[n - begin] = slot

        walk_listings(
            place_ref, list_ref, owner_ref, count_ref, n_region, n_sub, begin, begin + PER_DEV, visit
        )

    columns = masked_cat(coupling_ref, live_ref[i])
    for j in range(SLOTS):
        cat_h[:, j * TILE : (j + 1) * TILE] = columns[j][0]
        cat_l[:, j * TILE : (j + 1) * TILE] = columns[j][1]
    schur = dot3((cat_h[...], cat_l[...]), (solved_h_ref[0], solved_l_ref[0]), ((0,), (0,)))
    for j in range(SLOTS):
        slot = slot_ref[i * SLOTS + j]
        for k in range(1, SLOTS):
            other = (j + k) % SLOTS
            pay_ref[slot, :, (k - 1) * TILE : k * TILE] = schur[
                j * TILE : (j + 1) * TILE, other * TILE : (other + 1) * TILE
            ]

    @pl.when(i == SUB_DEV - 1)
    def _():
        for c in range(8):
            chunks[c][...] = pay_ref[2 * c : 2 * c + 2]


def couple(place, near, owner, live, coupling, solved_h, solved_l, n_region, n_sub):
    span = SLOTS * TILE
    wide = (SLOTS - 1) * TILE
    step = lambda i: (i, 0, 0)
    return pl.pallas_call(
        lambda *refs: couple_kernel(n_region, n_sub, *refs),
        grid=(SUB_DEV,),
        out_shape=(jax.ShapeDtypeStruct((2, TILE, wide), F32),) * 8,
        in_specs=[SMEM] * 4
        + [
            pl.BlockSpec((1, SLOTS, NI, TILE), lambda i: (i, 0, 0, 0)),
            pl.BlockSpec((1, NI, span), step),
            pl.BlockSpec((1, NI, span), step),
        ],
        out_specs=(pl.BlockSpec((2, TILE, wide), lambda i: (0, 0, 0)),) * 8,
        scratch_shapes=[
            pltpu.VMEM((PER_DEV, TILE, wide), F32),
            pltpu.VMEM((NI, span), BF16),
            pltpu.VMEM((NI, span), BF16),
            pltpu.SMEM((PER_DEV,), jnp.int32),
            pltpu.SMEM((4 * n_sub * n_sub,), jnp.int32),
        ],
        compiler_params=params(),
        cost_estimate=pl.CostEstimate(flops=3 * 2 * 4 * NI**3, bytes_accessed=12 << 20, transcendentals=0),
        name="couple",
    )(place, near, owner, live, coupling, solved_h, solved_l)


def lane_group(shape, axis):
    return lax.broadcasted_iota(jnp.int32, shape, axis) // BLOCK


def block_diagonal(w, kb):
    groups = TILE // BLOCK
    parts = []
    for m in range(groups):
        rows = w[m * BLOCK : (m + 1) * BLOCK]
        shift = ((m - kb) % groups) * BLOCK
        if shift:
            rows = pltpu.roll(rows, shift, 1)
        parts.append(jnp.where(lane_group(rows.shape, 1) == m, rows, 0.0))
    return parts


def packed_inverse(p):
    lane = lax.broadcasted_iota(jnp.int32, p.shape, 1)
    row_id = lax.broadcasted_iota(jnp.int32, p.shape, 0)
    group_base = lane // BLOCK * BLOCK
    for k in range(BLOCK):
        column = jnp.take_along_axis(p, group_base + k, axis=1)
        row = p[k : k + 1]
        recip = 1.0 / column[k : k + 1]
        at_k = lane == group_base + k
        new_row = jnp.where(at_k[:1], recip, row * recip)
        p = jnp.where(at_k, 0.0, p) - column * new_row
        p = jnp.where(row_id == k, new_row, p)
    return p


def batch_inverse(tiles):
    groups = TILE // BLOCK
    w = [
        jnp.concatenate([t[kb * BLOCK : (kb + 1) * BLOCK] for t in tiles], axis=0) for kb in range(groups)
    ]
    lane = lax.broadcasted_iota(jnp.int32, (TILE, TILE), 1)
    row_in = lax.broadcasted_iota(jnp.int32, (TILE, TILE), 0) % BLOCK
    for kb in range(groups):
        parts = block_diagonal(w[kb], kb)
        packed = packed_inverse(parts[0] + parts[1] + parts[2] + parts[3])
        inner = jnp.concatenate(
            [jnp.where(lane_group(packed.shape, 1) == m, packed, 0.0) for m in range(groups)], axis=0
        )
        in_block = lane // BLOCK == kb
        unit = (lane == kb * BLOCK + row_in).astype(F32)
        pivot = dot3(halves(inner), halves(jnp.where(in_block, unit, w[kb])))
        pivot_parts = halves(pivot)
        for other in range(groups):
            if other == kb:
                continue
            left = jnp.concatenate(block_diagonal(w[other], kb), axis=0)
            w[other] = jnp.where(in_block, 0.0, w[other]) - dot3(halves(left), pivot_parts)
        w[kb] = pivot
    return [
        jnp.concatenate([w[kb][m * BLOCK : (m + 1) * BLOCK] for kb in range(groups)], axis=0)
        for m in range(SEP_DEV)
    ]


def folded(x):
    return jnp.sum(x.reshape(-1, 8, x.shape[-1]), axis=0)


def start_kernel(target_ref, hess_ref, grad_ref, *rest):
    chunks, (inv_h_ref, inv_l_ref, u_ref, w_ref, norm_ref, sum_ref) = rest[:8], rest[8:]
    sum_ref[:, :, :TILE] = hess_ref[...]
    sum_ref[:, :, TILE:] = grad_ref[...]
    for a in range(PER_DEV):
        t = target_ref[a]
        sum_ref[t] = sum_ref[t] - chunks[a // 2][a % 2]
    inverses = batch_inverse([sum_ref[t, :, :TILE] for t in range(SEP_DEV)])
    norm = jnp.zeros((8, NRHS), F32)
    for t in range(SEP_DEV):
        inv_h, inv_l = halves(inverses[t])
        inv_h_ref[t] = inv_h
        inv_l_ref[t] = inv_l
        u = sum_ref[t, :, TILE:]
        w = dot3((inv_h, inv_l), halves(u))
        u_ref[t] = u
        w_ref[t] = w
        norm = norm + folded(u * w)
    norm_ref[...] = norm


def start(target, hess, grad, chunks):
    tile = jax.ShapeDtypeStruct((SEP_DEV, TILE, NRHS), F32)
    half = jax.ShapeDtypeStruct((SEP_DEV, TILE, TILE), BF16)
    return pl.pallas_call(
        start_kernel,
        out_shape=(half, half, tile, tile, jax.ShapeDtypeStruct((8, NRHS), F32)),
        in_specs=[SMEM] + [VMEM] * 10,
        out_specs=(VMEM,) * 5,
        scratch_shapes=[pltpu.VMEM((SEP_DEV, TILE, TILE + NRHS), F32)],
        compiler_params=params(),
        cost_estimate=pl.CostEstimate(flops=10**10, bytes_accessed=4 << 20, transcendentals=0),
        name="start",
    )(target, hess, grad, *chunks)


def apply_kernel(with_w, target_ref, seen_ref, inv_h_ref, inv_l_ref, *rest):
    offs, vs, outs = rest[:8], rest[8:20], rest[20:]
    u_ref = outs[0]
    v_h, v_l = outs[-2:]
    for c in range(12):
        h, l = halves(vs[c][...])
        v_h[c * SEP_DEV : (c + 1) * SEP_DEV] = h
        v_l[c * SEP_DEV : (c + 1) * SEP_DEV] = l
    u_ref[...] = jnp.zeros(u_ref.shape, F32)
    for a in range(PER_DEV):
        t = target_ref[a]
        ids = [seen_ref[a * (SLOTS - 1) + k] for k in range(SLOTS - 1)]
        right = tuple(jnp.concatenate([ref[n] for n in ids], axis=0) for ref in (v_h, v_l))
        u_ref[t] = u_ref[t] + dot3(halves(offs[a // 2][a % 2]), right)
    if with_w:
        w_ref, norm_ref = outs[1:3]
        norm = jnp.zeros((8, NRHS), F32)
        for t in range(SEP_DEV):
            u = u_ref[t]
            w = dot3((inv_h_ref[t], inv_l_ref[t]), halves(u))
            w_ref[t] = w
            norm = norm + folded(u * w)
        norm_ref[...] = norm


def apply(target, seen, inv_h, inv_l, offs, vs, with_w):
    tile = jax.ShapeDtypeStruct((SEP_DEV, TILE, NRHS), F32)
    outs = (tile, tile, jax.ShapeDtypeStruct((8, NRHS), F32)) if with_w else (tile,)
    return pl.pallas_call(
        lambda *refs: apply_kernel(with_w, *refs),
        out_shape=outs,
        in_specs=[SMEM] * 2 + [VMEM] * 22,
        out_specs=(VMEM,) * len(outs),
        scratch_shapes=[pltpu.VMEM((12 * SEP_DEV, TILE, NRHS), BF16)] * 2,
        compiler_params=params(),
        cost_estimate=pl.CostEstimate(flops=2 * 10**9, bytes_accessed=7 << 20, transcendentals=0),
        name="apply",
    )(target, seen, inv_h, inv_l, *offs, *vs)


def finish_kernel(own_ref, coef_ref, reduced_ref, solved_h_ref, solved_l_ref, u1_ref, u3_ref, *rest):
    groups, (interior_ref, x_ref, resid_ref, x_h, x_l) = rest[:24], rest[24:]
    for c in range(8):
        x = (
            coef_ref[0] * groups[c][...]
            + coef_ref[1] * groups[8 + c][...]
            + coef_ref[2] * groups[16 + c][...]
        )
        if c == 0:
            x_ref[...] = x
        h, l = halves(x)
        x_h[c * SEP_DEV : (c + 1) * SEP_DEV] = h
        x_l[c * SEP_DEV : (c + 1) * SEP_DEV] = l
    resid_ref[...] = coef_ref[3] * u3_ref[...] + coef_ref[4] * u1_ref[...]
    for i in range(SUB_DEV):
        ids = []
        for j in range(SLOTS):
            n = own_ref[i * SLOTS + j]
            ids.append(jnp.where(n >= 4 * SEP_DEV, n - 4 * SEP_DEV, n))
        right = tuple(jnp.concatenate([ref[n] for n in ids], axis=0) for ref in (x_h, x_l))
        interior_ref[i] = reduced_ref[i] - dot3((solved_h_ref[i], solved_l_ref[i]), right)


def finish(own, coefs, reduced, solved_h, solved_l, u1, u3, w0s, w1s, w2s):
    tile = jax.ShapeDtypeStruct((SEP_DEV, TILE, NRHS), F32)
    return pl.pallas_call(
        finish_kernel,
        out_shape=(jax.ShapeDtypeStruct((SUB_DEV, NI, NRHS), F32), tile, tile),
        in_specs=[SMEM] * 2 + [VMEM] * 29,
        out_specs=(VMEM,) * 3,
        scratch_shapes=[pltpu.VMEM((8 * SEP_DEV, TILE, NRHS), BF16)] * 2,
        compiler_params=params(),
        name="finish",
    )(own, coefs, reduced, solved_h, solved_l, u1, u3, *w0s, *w1s, *w2s)


def per_device(
    interior_inverse, coupling, interior_grad, separator_hessian_blocks, sep_grad, lists, owner, counts
):
    n_region = lax.axis_size("region")
    n_sub = lax.axis_size("sub")
    region = lax.axis_index("region")
    sub = lax.axis_index("sub")

    def shift(x, ahead, turn):
        pairs = [
            (r * n_sub + s, (r + ahead) % n_region * n_sub + (s + turn) % n_sub)
            for r in range(n_region)
            for s in range(n_sub)
        ]
        return lax.ppermute(x, ("region", "sub"), pairs)

    def exchange(chunks):
        return [chunks[0]] + [shift(chunks[c], *ROUTES[c]) for c in range(1, 8)]

    def spread(v):
        around = [v] + [shift(v, 0, turn) for turn in (1, 2, 3)]
        before = [shift(x, 1, 0) for x in around]
        after = [shift(x, -1, 0) for x in around]
        return around + before + after

    per_region = n_sub * SUB_DEV
    here = lax.dynamic_slice_in_dim(lists, region * per_region, per_region, 0)
    behind = lax.dynamic_slice_in_dim(lists, (region - 1) % n_region * per_region, per_region, 0)
    near = jnp.concatenate([behind, here], axis=0).reshape(-1)
    live = lax.dynamic_slice_in_dim(counts, (region * n_sub + sub) * SUB_DEV, SUB_DEV, 0)
    place = jnp.stack([region, sub]).astype(jnp.int32)
    key = (place, near, owner)

    solved_h, solved_l, reduced, *pay = eliminate(
        *key, live, interior_inverse, coupling, interior_grad, n_region, n_sub
    )
    arrived = exchange(pay)
    target, seen, own = plan(*key, n_region, n_sub)
    offs = couple(*key, live, coupling, solved_h, solved_l, n_region, n_sub)
    arrived, offs = lax.optimization_barrier((arrived, offs))
    offs = exchange(offs)
    inv_h, inv_l, u0, w0, norm0 = start(target, separator_hessian_blocks, sep_grad, arrived)
    w0s = spread(w0)
    u1, w1, norm1 = apply(target, seen, inv_h, inv_l, offs, w0s, True)
    norms = lax.all_gather(jnp.stack([jnp.sum(norm0, 0), jnp.sum(norm1, 0)]), ("region", "sub"))
    totals = jnp.sum(norms, axis=(0, 2))
    w1s = spread(w1)
    u2, w2, _ = apply(target, seen, inv_h, inv_l, offs, w1s, True)
    w2s = spread(w2)
    (u3,) = apply(target, seen, inv_h, inv_l, offs, w2s, False)
    q = totals[1] / totals[0]
    g1 = 1.0 / (2.0 - q)
    g2 = 1.0 / (2.0 - q * g1)
    back = q * g2 * g1
    coefs = jnp.stack(
        [
            1.0 + (1.0 + back) * g1 * q - 2.0 * g2 * g1 * q,
            (1.0 + back) * g1 * 2.0,
            4.0 * g2 * g1,
            4.0 * g1 * g2,
            -3.0 * q * g1 * g2,
        ]
    )
    near_parts = lambda ws: ws[:4] + ws[8:]
    return finish(
        own, coefs, reduced, solved_h, solved_l, u1, u3, near_parts(w0s), near_parts(w1s), near_parts(w2s)
    )


def solution(mesh):
    split3 = P(("region", "sub"), None, None)
    placed = (split3, P(("region", "sub"), None, None, None), split3, split3, split3, P(), P(), P())
    return jax.shard_map(
        per_device, mesh=mesh, in_specs=placed, out_specs=(split3, split3, split3), check_vma=False
    )
```

time: 520 us -> 281 us (0.54)
  other arithmetic: 115 us -> 1.02 us
  Pallas kernels: 0 us -> 80.2 us
  blocking collectives: 129 us -> 50.5 us
  local copies, waits for them, and re-layouts: 81.2 us -> 7.82 us
  matrix products: 62.3 us -> 0 us
  starting transfers between devices: 29.2 us -> 65.8 us
  waiting for transfers between devices: 95 us -> 70.8 us
    another operation x8 -> x1, other arithmetic: 86.6 us -> 0.65 us  [per_device(): place = jnp.stack([region, sub]).astype(jnp.int32)]
    pallas_call x0 -> x8, Pallas kernels: none -> 80.2 us  [the longest x3 17.3 us: apply(): pl.pallas_call(lambda *refs: apply_kernel(with_w, *refs), out_shape=outs,...]
    all_to_all x4 -> x0, blocking collectives: 67.1 us -> none  [deliver(): lax.all_to_all(shaped, 'sub', split_axis=1, concat_axis=1, tiled=True)]
    psum x1 -> x0, blocking collectives: 62 us -> none  [per_device(): latter_term = lax.psum(jnp.sum(resid * z_resid), ('region', 'sub'))]
    dot_general x15 -> x0, matrix products: 59.3 us -> none  [the longest x3 18.3 us: schur_operator_apply(): jnp.einsum('bij,bjk->bik', schur, listed.reshape(sub_dev, span_cols, nrhs...]
    ppermute x8 -> x47, starting transfers between devices: 12.6 us -> 65.8 us  [shift(): return lax.ppermute(x, ('region', 'sub'), pairs)]
    all_gather x0 -> x1, blocking collectives: none -> 50.5 us  [per_device(): lax.all_gather(jnp.stack([jnp.sum(norm0, 0), jnp.sum(norm1, 0)]), ('regio...]
    gather x53 -> x0, local copies, waits for them, and re-layouts: 37.4 us -> none
  transfers between devices with their start and end apart: 12 -> 47, of which waited for: 11 -> 17; matrix products, arithmetic and copies ran while one was open for 7% -> 1% of each run, Pallas kernels for 0% -> 8%
where the time goes in v1:
time: 281 us; the launch traced here: 279 us
  Pallas kernels  80.2 us (29%)
  waiting for transfers between devices  70.8 us (25%)
  starting transfers between devices  65.8 us (23%)
  blocking collectives  50.5 us (18%)
  local copies, waits for them, and re-layouts  7.82 us (3%)
  between operations  2.94 us (1%)
    ppermute x47, waiting for transfers between devices, shift(): return lax.ppermute(x, ('region', 'sub'), pairs)  70.8 us
    ppermute x47, starting transfers between devices, shift(): return lax.ppermute(x, ('region', 'sub'), pairs)  65.8 us
    all_gather x1, blocking collectives, per_device(): lax.all_gather(jnp.stack([jnp.sum(norm0, 0), jnp.sum(norm1, 0)]), ('regio...  50.5 us
    pallas_call x3, Pallas kernels, apply(): pl.pallas_call(lambda *refs: apply_kernel(with_w, *refs), out_shape=outs,...  17.3 us
    pallas_call x1, Pallas kernels, eliminate(): pl.pallas_call(lambda *refs: eliminate_kernel(n_region, n_sub, *refs), gr...  16.2 us
    pallas_call x1, Pallas kernels, start(): pl.pallas_call(start_kernel, out_shape=(half, half, tile, tile, jax.Shape...  15.6 us
    pallas_call x1, Pallas kernels, plan(): pl.pallas_call(lambda *refs: plan_kernel(n_region, n_sub, *refs), out_sha...  13.7 us
    pallas_call x1, Pallas kernels, couple(): pl.pallas_call(lambda *refs: couple_kernel(n_region, n_sub, *refs), grid=...  9.31 us
  transfers between devices with their start and end apart: 47, of which 17 were waited for; matrix products, arithmetic and copies ran while one was open for 1% of the time, Pallas kernels for 8%

profile of v1, /device:TPU:0, one launch (start us, length us, event | category | flops | bytes accessed | tf_op | source)
XLA Modules:
  0.0 279.1 jit_solution(3122121373406322093)
XLA Ops:
  0.7 0.8 constant_dynamic-slice_fusion.1
  1.6 0.6 reshape.10.refs_1_
  2.3 0.7 pad_add_fusion.1.refs_0_
  2.9 1.3 dynamic_slice.11.refs_3_
  4.2 16.2 %eliminate.1 = (bf16[4,512,512]{2,1,0:T(8,128)(2,1)}, bf16[4,512,512]{2,1,0:T(8,128)(2,1)}, f32[4,512,128]{2,1,0:T(8,128)}, f32[2,128,256]{2,1,0:T(8,128)}, f32[...) custom-call(s32[2]{0:T(128)} %pad_add_fusion.1.refs_0_, ...), custom_call_target="tpu_custom_call" | custom-call | tf_op jit(solution)/shard_map/eliminate/pallas_call | solution.py:170
  20.5 2.1 collective-permute-start
  22.5 3.6 %collective-permute-start.1 = (f32[2,128,256]{2,1,0:T(8,128)}, f32[2,128,256]{2,1,0:T(8,128)S(1)}, u32[]{:S(2)}, u32[]{:S(2)}) collective-permute-start(f32[2,128,256]{2,1,0:T(8,128)} %get-tuple-element.53), channel_id=1, source_target_pairs={{0,2},{1,3},{2,0},{3,1},{4,6},{5,7},{6,4},{7,5},{8,10},{9,11},{10,... | collective-permute-start | bytes 786440 | tf_op jit(solution)/shard_map/ppermute | solution.py:456
  26.1 1.0 collective-permute-start.2
  27.1 2.4 collective-permute-start.4
  29.5 13.7 %plan.1 = (s32[17]{0:T(128)}, s32[51]{0:T(128)}, s32[16]{0:T(128)}) custom-call(s32[2]{0:T(128)} %pad_add_fusion.1.refs_0_, s32[128]{0:T(128)} %reshape.10.refs_1_, s32[512]{0:T(512)} %refs_2_.5), custom_call_target="tpu_custom_call" | custom-call | tf_op jit(solution)/shard_map/plan/pallas_call | solution.py:104
  43.3 2.9 %collective-permute-start.6 = (f32[2,128,256]{2,1,0:T(8,128)}, f32[2,128,256]{2,1,0:T(8,128)S(1)}, u32[]{:S(2)}, u32[]{:S(2)}) collective-permute-start(f32[2,128,256]{2,1,0:T(8,128)} %get-tuple-element.58), channel_id=1, source_target_pairs={{0,7},{1,4},{2,5},{3,6},{4,11},{5,8},{6,9},{7,10},{8,15},{9,12},{1... | collective-permute-start | bytes 786440 | tf_op jit(solution)/shard_map/ppermute | solution.py:456
  46.2 9.3 %couple.1 = (f32[2,128,384]{2,1,0:T(8,128)}, f32[2,128,384]{2,1,0:T(8,128)}, f32[2,128,384]{2,1,0:T(8,128)}, f32[2,128,384]{2,1,0:T(8,128)}, f32[2,128,384]{2,1,...) custom-call(s32[2]{0:T(128)} %pad_add_fusion.1.refs_0_, s32[128]{0:T(128)} %reshape.10.refs_1_, ...), custom_call_target="tpu_custom_call" | custom-call | flops 3221225472 | bytes 12582912 | tf_op jit(solution)/shard_map/couple/pallas_call | solution.py:242
  55.6 3.1 %collective-permute-done.6.rest_7_ = f32[2,128,256]{2,1,0:T(8,128)S(1)} collective-permute-done((f32[2,128,256]{2,1,0:T(8,128)}, f32[2,128,256]{2,1,0:T(8,128)S(1)}, u32[]{:S(2)}, u32[]{:S(2)}) %collective-permute-start.6) | collective-permute-done | bytes 262176 | tf_op jit(solution)/shard_map/ppermute | solution.py:456
  58.8 0.7 copy-done.51
  59.5 15.6 %start.1 = (bf16[4,128,128]{2,1,0:T(8,128)(2,1)}, bf16[4,128,128]{2,1,0:T(8,128)(2,1)}, f32[4,128,128]{2,1,0:T(8,128)}, f32[4,128,128]{2,1,0:T(8,128)}, f32[8,128]{1,0:T(8,128)}) custom-call(s32[17]{0:T(128)} %get-tuple-element.50.target_ref.refs_0_, f32[4,128,128]{2,1,0:T(8,128)} %hess_ref.1, f32[4,128,128]{2,1,0:T(8,128)} %grad_ref.1, ...), custom_call_target="tpu_custom_call" | custom-call | flops 10000000000 | bytes 4194304 | tf_op jit(solution)/shard_map/start/pallas_call | solution.py:354
  75.1 4.3 %collective-permute-start.21 = (f32[4,128,128]{2,1,0:T(8,128)}, f32[4,128,128]{2,1,0:T(8,128)S(1)}, u32[]{:S(2)}, u32[]{:S(2)}) collective-permute-start(f32[4,128,128]{2,1,0:T(8,128)} %get-tuple-element.89.refs_12_.rest_0_), channel_id=1, source_target_pairs={{0,124},{1,125},{2,126},{3,127},{4,0},{5,1},{6,2},{7,3},{8,4},{9,5... | collective-permute-start | bytes 786440 | tf_op jit(solution)/shard_map/ppermute | solution.py:456
  79.4 1.6 collective-permute-start.16
  81.0 0.4 collective-permute-start.7
  81.4 1.1 collective-permute-start.8
  82.5 1.1 collective-permute-done.21.refs_20_.rest_4_
  83.6 1.4 collective-permute-start.15
  85.0 3.8 %collective-permute-done.17.refs_16_ = f32[4,128,128]{2,1,0:T(8,128)S(1)} collective-permute-done((f32[4,128,128]{2,1,0:T(8,128)}, f32[4,128,128]{2,1,0:T(8,128)S(1)}, u32[]{:S(2)}, u32[]{:S(2)}) %collective-permute-start.17) | collective-permute-done | bytes 262176 | tf_op jit(solution)/shard_map/ppermute | solution.py:456
  88.7 9.3 %collective-permute-done.16.refs_15_.rest_3_ = f32[4,128,128]{2,1,0:T(8,128)S(1)} collective-permute-done((f32[4,128,128]{2,1,0:T(8,128)}, f32[4,128,128]{2,1,0:T(8,128)S(1)}, u32[]{:S(2)}, u32[]{:S(2)}) %collective-permute-start.16) | collective-permute-done | bytes 262176 | tf_op jit(solution)/shard_map/ppermute | solution.py:456
  98.1 4.1 %collective-permute-start.9 = (f32[2,128,384]{2,1,0:T(8,128)S(1)}, f32[2,128,384]{2,1,0:T(8,128)S(1)}, u32[]{:S(2)}, u32[]{:S(2)}) collective-permute-start(f32[2,128,384]{2,1,0:T(8,128)S(1)} %copy-done.34), channel_id=1, source_target_pairs={{0,3},{1,0},{2,1},{3,2},{4,7},{5,4},{6,5},{7,6},{8,11},{9,8},{10,9... | collective-permute-start | bytes 1179656 | tf_op jit(solution)/shard_map/ppermute | solution.py:456
  102.1 4.5 %collective-permute-done.15.refs_14_.rest_2_ = f32[4,128,128]{2,1,0:T(8,128)S(1)} collective-permute-done((f32[4,128,128]{2,1,0:T(8,128)}, f32[4,128,128]{2,1,0:T(8,128)S(1)}, u32[]{:S(2)}, u32[]{:S(2)}) %collective-permute-start.15) | collective-permute-done | bytes 262176 | tf_op jit(solution)/shard_map/ppermute | solution.py:456
  106.7 4.4 %collective-permute-done.14.refs_13_.rest_1_ = f32[4,128,128]{2,1,0:T(8,128)S(1)} collective-permute-done((f32[4,128,128]{2,1,0:T(8,128)}, f32[4,128,128]{2,1,0:T(8,128)S(1)}, u32[]{:S(2)}, u32[]{:S(2)}) %collective-permute-start.14) | collective-permute-done | bytes 262176 | tf_op jit(solution)/shard_map/ppermute | solution.py:456
  111.1 1.1 collective-permute-start.12
  112.2 2.2 collective-permute-start.13
  114.4 3.4 %collective-permute-start.24 = (f32[4,128,128]{2,1,0:T(8,128)S(1)}, f32[4,128,128]{2,1,0:T(8,128)S(1)}, u32[]{:S(2)}, u32[]{:S(2)}) collective-permute-start(f32[4,128,128]{2,1,0:T(8,128)S(1)} %collective-permute-done.16.refs_15_.rest_3_), channel_id=1, source_target_pairs={{0,124},{1,125},{2,126},{3,127},{4,0},{5,1},{6,2},{7,3},{8,4},{9,5... | collective-permute-start | bytes 786440 | tf_op jit(solution)/shard_map/ppermute | solution.py:456
  117.8 6.5 %collective-permute-done.11.refs_9_ = f32[2,128,384]{2,1,0:T(8,128)S(1)} collective-permute-done((f32[2,128,384]{2,1,0:T(8,128)S(1)}, f32[2,128,384]{2,1,0:T(8,128)S(1)}, u32[]{:S(2)}, u32[]{:S(2)}) %collective-permute-start.11) | collective-permute-done | bytes 393248 | tf_op jit(solution)/shard_map/ppermute | solution.py:456
  124.3 10.6 %collective-permute-start.23 = (f32[4,128,128]{2,1,0:T(8,128)S(1)}, f32[4,128,128]{2,1,0:T(8,128)S(1)}, u32[]{:S(2)}, u32[]{:S(2)}) collective-permute-start(f32[4,128,128]{2,1,0:T(8,128)S(1)} %collective-permute-done.15.refs_14_.rest_2_), channel_id=1, source_target_pairs={{0,124},{1,125},{2,126},{3,127},{4,0},{5,1},{6,2},{7,3},{8,4},{9,5... | collective-permute-start | bytes 786440 | tf_op jit(solution)/shard_map/ppermute | solution.py:456
  134.9 5.0 %collective-permute-start.22 = (f32[4,128,128]{2,1,0:T(8,128)S(1)}, f32[4,128,128]{2,1,0:T(8,128)S(1)}, u32[]{:S(2)}, u32[]{:S(2)}) collective-permute-start(f32[4,128,128]{2,1,0:T(8,128)S(1)} %collective-permute-done.14.refs_13_.rest_1_), channel_id=1, source_target_pairs={{0,124},{1,125},{2,126},{3,127},{4,0},{5,1},{6,2},{7,3},{8,4},{9,5... | collective-permute-start | bytes 786440 | tf_op jit(solution)/shard_map/ppermute | solution.py:456
  140.0 4.0 %collective-permute-done.19.refs_18_ = f32[4,128,128]{2,1,0:T(8,128)S(1)} collective-permute-done((f32[4,128,128]{2,1,0:T(8,128)S(1)}, f32[4,128,128]{2,1,0:T(8,128)S(1)}, u32[]{:S(2)}, u32[]{:S(2)}) %collective-permute-start.19) | collective-permute-done | bytes 262176 | tf_op jit(solution)/shard_map/ppermute | solution.py:456
  144.0 5.1 %collective-permute-done.18.refs_17_ = f32[4,128,128]{2,1,0:T(8,128)S(1)} collective-permute-done((f32[4,128,128]{2,1,0:T(8,128)S(1)}, f32[4,128,128]{2,1,0:T(8,128)S(1)}, u32[]{:S(2)}, u32[]{:S(2)}) %collective-permute-start.18) | collective-permute-done | bytes 262176 | tf_op jit(solution)/shard_map/ppermute | solution.py:456
  149.2 0.5 copy-done.54
  149.8 5.8 %apply.3 = (f32[4,128,128]{2,1,0:T(8,128)}, f32[4,128,128]{2,1,0:T(8,128)}, f32[8,128]{1,0:T(8,128)}) custom-call(s32[17]{0:T(128)} %get-tuple-element.50.target_ref.refs_0_, s32[51]{0:T(128)} %get-tuple-element.78.refs_1_, bf16[4,128,128]{2,1,0:T(8,128)(2,1)} %get-tuple-element.79.refs_2_, bf16[4,128,128]{2,1,0:T(8,128)(2,1)} %get-tuple-element.80.refs_3_, ...), custom_call_target="tpu_custom_call" | custom-call | flops 2000000000 | bytes 7340032 | tf_op jit(solution)/shard_map/apply/pallas_call | solution.py:394
  155.9 0.4 collective-permute-start.28
  156.3 1.9 collective-permute-start.25
  158.2 6.7 %collective-permute-done.27.refs_15_.rest_11_ = f32[4,128,128]{2,1,0:T(8,128)S(1)} collective-permute-done((f32[4,128,128]{2,1,0:T(8,128)}, f32[4,128,128]{2,1,0:T(8,128)S(1)}, u32[]{:S(2)}, u32[]{:S(2)}) %collective-permute-start.27) | collective-permute-done | bytes 262176 | tf_op jit(solution)/shard_map/ppermute | solution.py:456
  164.9 0.5 collective-permute-start.31
  165.4 1.3 collective-permute-done.26.refs_14_.rest_10_
  166.7 3.3 %collective-permute-start.34 = (f32[4,128,128]{2,1,0:T(8,128)S(1)}, f32[4,128,128]{2,1,0:T(8,128)S(1)}, u32[]{:S(2)}, u32[]{:S(2)}) collective-permute-start(f32[4,128,128]{2,1,0:T(8,128)S(1)} %collective-permute-done.26.refs_14_.rest_10_), channel_id=1, source_target_pairs={{0,124},{1,125},{2,126},{3,127},{4,0},{5,1},{6,2},{7,3},{8,4},{9,5... | collective-permute-start | bytes 786440 | tf_op jit(solution)/shard_map/ppermute | solution.py:456
  170.1 1.8 collective-permute-done.25.refs_13_.rest_9_
  171.8 3.3 %collective-permute-start.33 = (f32[4,128,128]{2,1,0:T(8,128)S(1)}, f32[4,128,128]{2,1,0:T(8,128)S(1)}, u32[]{:S(2)}, u32[]{:S(2)}) collective-permute-start(f32[4,128,128]{2,1,0:T(8,128)S(1)} %collective-permute-done.25.refs_13_.rest_9_), channel_id=1, source_target_pairs={{0,124},{1,125},{2,126},{3,127},{4,0},{5,1},{6,2},{7,3},{8,4},{9,5... | collective-permute-start | bytes 786440 | tf_op jit(solution)/shard_map/ppermute | solution.py:456
  175.2 4.0 %collective-permute-done.30.refs_18_ = f32[4,128,128]{2,1,0:T(8,128)S(1)} collective-permute-done((f32[4,128,128]{2,1,0:T(8,128)S(1)}, f32[4,128,128]{2,1,0:T(8,128)S(1)}, u32[]{:S(2)}, u32[]{:S(2)}) %collective-permute-start.30) | collective-permute-done | bytes 262176 | tf_op jit(solution)/shard_map/ppermute | solution.py:456
  179.2 5.1 %collective-permute-done.29.refs_17_ = f32[4,128,128]{2,1,0:T(8,128)S(1)} collective-permute-done((f32[4,128,128]{2,1,0:T(8,128)S(1)}, f32[4,128,128]{2,1,0:T(8,128)S(1)}, u32[]{:S(2)}, u32[]{:S(2)}) %collective-permute-start.29) | collective-permute-done | bytes 262176 | tf_op jit(solution)/shard_map/ppermute | solution.py:456
  184.4 0.7 copy-done.55
  185.1 5.8 %apply.4 = (f32[4,128,128]{2,1,0:T(8,128)}, f32[4,128,128]{2,1,0:T(8,128)}, f32[8,128]{1,0:T(8,128)}) custom-call(s32[17]{0:T(128)} %get-tuple-element.50.target_ref.refs_0_, s32[51]{0:T(128)} %get-tuple-element.78.refs_1_, bf16[4,128,128]{2,1,0:T(8,128)(2,1)} %get-tuple-element.79.refs_2_, bf16[4,128,128]{2,1,0:T(8,128)(2,1)} %get-tuple-element.80.refs_3_, ...), custom_call_target="tpu_custom_call" | custom-call | flops 2000000000 | bytes 7340032 | tf_op jit(solution)/shard_map/apply/pallas_call | solution.py:394
  190.9 0.6 collective-permute-start.38
  191.8 1.5 collective-permute-start.37
  193.3 1.1 collective-permute-start.36
  194.4 5.4 %collective-permute-done.38.refs_15_.rest_19_ = f32[4,128,128]{2,1,0:T(8,128)S(1)} collective-permute-done((f32[4,128,128]{2,1,0:T(8,128)}, f32[4,128,128]{2,1,0:T(8,128)S(1)}, u32[]{:S(2)}, u32[]{:S(2)}) %collective-permute-start.38) | collective-permute-done | bytes 262176 | tf_op jit(solution)/shard_map/ppermute | solution.py:456
  199.9 0.6 collective-permute-start.42
  200.5 2.3 collective-permute-done.37.refs_14_.rest_18_
  202.7 2.3 collective-permute-start.45
  205.0 2.5 collective-permute-done.36.refs_13_.rest_17_
  207.6 2.5 collective-permute-start.44
  210.1 50.5 %all-gather.1 = f32[128,2,128]{2,1,0:T(2,128)S(1)} all-gather(f32[1,2,128]{2,1,0:T(2,128)S(1)} %maximum_bitcast_fusion), channel_id=2, replica_groups=mesh['region'=32,'sub'=4] {'region','sub'}, dimensions={0}, use_global_device_ids=true | all-gather | bytes 132096 | tf_op jit(solution)/shard_map/all_gather | solution.py:486
  260.9 0.6 fusion
  262.9 0.7 stack.47.coef_ref
  263.7 0.6 copy-done.39
  264.5 0.7 copy-done.41
  265.2 5.6 %apply.5.u3_ref = f32[4,128,128]{2,1,0:T(8,128)} custom-call(s32[17]{0:T(128)} %get-tuple-element.50.target_ref.refs_0_, s32[51]{0:T(128)} %get-tuple-element.78.refs_1_, bf16[4,128,128]{2,1,0:T(8,128)(2,1)} %get-tuple-element.79.refs_2_, bf16[4,128,128]{2,1,0:T(8,128)(2,1)} %get-tuple-element.80.refs_3_, f32[2,128,384]{2,1,0:T(8,128)} %get-tuple-element.81.refs_4_, ...), custom_call_target="tpu_custom_call" | custom-call | flops 2000000000 | bytes 7340032 | tf_op jit(solution)/shard_map/apply/pallas_call | solution.py:394
  270.8 8.1 %finish.1 = (f32[4,512,128]{2,1,0:T(8,128)}, f32[4,128,128]{2,1,0:T(8,128)}, f32[4,128,128]{2,1,0:T(8,128)}) custom-call(s32[16]{0:T(128)} %get-tuple-element.49.own_ref, f32[5]{0:T(128)} %stack.47.coef_ref, f32[4,512,128]{2,1,0:T(8,128)} %get-tuple-element.91.reduced_ref, bf16[4,512,512]{2,1,0:T(8,128)(2,1)} %get-tuple-element.59.refs_5_.solved_h_ref, ...), custom_call_target="tpu_custom_call" | custom-call | tf_op jit(solution)/shard_map/finish/pallas_call | solution.py:431
  (163 shorter events, 1.7 us)
Async XLA Ops:
  20.5 22.7 %collective-permute-start = (f32[2,128,256]{2,1,0:T(8,128)}, f32[2,128,256]{2,1,0:T(8,128)S(1)}, u32[]{:S(2)}, u32[]{:S(2)}) collective-permute-start(f32[2,128,256]{2,1,0:T(8,128)} %get-tuple-element.52), channel_id=1, source_target_pairs={{0,1},{1,2},{2,3},{3,0},{4,5},{5,6},{6,7},{7,4},{8,9},{9,10},{10,1... | collective-permute-start | bytes 786440 | tf_op jit(solution)/shard_map/ppermute | solution.py:456
  22.5 20.8 %collective-permute-start.1 = (f32[2,128,256]{2,1,0:T(8,128)}, f32[2,128,256]{2,1,0:T(8,128)S(1)}, u32[]{:S(2)}, u32[]{:S(2)}) collective-permute-start(f32[2,128,256]{2,1,0:T(8,128)} %get-tuple-element.53), channel_id=1, source_target_pairs={{0,2},{1,3},{2,0},{3,1},{4,6},{5,7},{6,4},{7,5},{8,10},{9,11},{10,... | collective-permute-start | bytes 786440 | tf_op jit(solution)/shard_map/ppermute | solution.py:456
  26.1 29.4 %collective-permute-start.2 = (f32[2,128,256]{2,1,0:T(8,128)}, f32[2,128,256]{2,1,0:T(8,128)S(1)}, u32[]{:S(2)}, u32[]{:S(2)}) collective-permute-start(f32[2,128,256]{2,1,0:T(8,128)} %get-tuple-element.54), channel_id=1, source_target_pairs={{0,3},{1,0},{2,1},{3,2},{4,7},{5,4},{6,5},{7,6},{8,11},{9,8},{10,9... | collective-permute-start | bytes 786440 | tf_op jit(solution)/shard_map/ppermute | solution.py:456
  27.1 28.4 %collective-permute-start.3 = (f32[2,128,256]{2,1,0:T(8,128)}, f32[2,128,256]{2,1,0:T(8,128)S(1)}, u32[]{:S(2)}, u32[]{:S(2)}) collective-permute-start(f32[2,128,256]{2,1,0:T(8,128)} %get-tuple-element.55), channel_id=1, source_target_pairs={{0,4},{1,5},{2,6},{3,7},{4,8},{5,9},{6,10},{7,11},{8,12},{9,13},{1... | collective-permute-start | bytes 786440 | tf_op jit(solution)/shard_map/ppermute | solution.py:456
  27.1 28.4 %collective-permute-start.4 = (f32[2,128,256]{2,1,0:T(8,128)}, f32[2,128,256]{2,1,0:T(8,128)S(1)}, u32[]{:S(2)}, u32[]{:S(2)}) collective-permute-start(f32[2,128,256]{2,1,0:T(8,128)} %get-tuple-element.56), channel_id=1, source_target_pairs={{0,5},{1,6},{2,7},{3,4},{4,9},{5,10},{6,11},{7,8},{8,13},{9,14},{1... | collective-permute-start | bytes 786440 | tf_op jit(solution)/shard_map/ppermute | solution.py:456
  43.2 12.4 %collective-permute-start.5 = (f32[2,128,256]{2,1,0:T(8,128)}, f32[2,128,256]{2,1,0:T(8,128)S(1)}, u32[]{:S(2)}, u32[]{:S(2)}) collective-permute-start(f32[2,128,256]{2,1,0:T(8,128)} %get-tuple-element.57), channel_id=1, source_target_pairs={{0,6},{1,7},{2,4},{3,5},{4,10},{5,11},{6,8},{7,9},{8,14},{9,15},{1... | collective-permute-start | bytes 786440 | tf_op jit(solution)/shard_map/ppermute | solution.py:456
  43.3 15.4 %collective-permute-start.6 = (f32[2,128,256]{2,1,0:T(8,128)}, f32[2,128,256]{2,1,0:T(8,128)S(1)}, u32[]{:S(2)}, u32[]{:S(2)}) collective-permute-start(f32[2,128,256]{2,1,0:T(8,128)} %get-tuple-element.58), channel_id=1, source_target_pairs={{0,7},{1,4},{2,5},{3,6},{4,11},{5,8},{6,9},{7,10},{8,15},{9,12},{1... | collective-permute-start | bytes 786440 | tf_op jit(solution)/shard_map/ppermute | solution.py:456
  59.5 38.6 %copy-start.34 = (f32[2,128,384]{2,1,0:T(8,128)S(1)}, f32[2,128,384]{2,1,0:T(8,128)}, u32[]{:S(2)}) copy-start(f32[2,128,384]{2,1,0:T(8,128)} %get-tuple-element.84) | copy-start | bytes 1179652
  59.5 47.2 %copy-start.33 = (f32[2,128,384]{2,1,0:T(8,128)S(1)}, f32[2,128,384]{2,1,0:T(8,128)}, u32[]{:S(2)}) copy-start(f32[2,128,384]{2,1,0:T(8,128)} %get-tuple-element.85) | copy-start | bytes 1179652
  59.5 51.6 %copy-start.32 = (f32[2,128,384]{2,1,0:T(8,128)S(1)}, f32[2,128,384]{2,1,0:T(8,128)}, u32[]{:S(2)}) copy-start(f32[2,128,384]{2,1,0:T(8,128)} %get-tuple-element.86) | copy-start | bytes 1179652
  59.5 51.6 %copy-start.31 = (f32[2,128,384]{2,1,0:T(8,128)S(1)}, f32[2,128,384]{2,1,0:T(8,128)}, u32[]{:S(2)}) copy-start(f32[2,128,384]{2,1,0:T(8,128)} %get-tuple-element.87) | copy-start | bytes 1179652
  59.5 52.7 %copy-start.30 = (f32[2,128,384]{2,1,0:T(8,128)S(1)}, f32[2,128,384]{2,1,0:T(8,128)}, u32[]{:S(2)}) copy-start(f32[2,128,384]{2,1,0:T(8,128)} %get-tuple-element.88) | copy-start | bytes 1179652
  75.1 8.5 %collective-permute-start.21 = (f32[4,128,128]{2,1,0:T(8,128)}, f32[4,128,128]{2,1,0:T(8,128)S(1)}, u32[]{:S(2)}, u32[]{:S(2)}) collective-permute-start(f32[4,128,128]{2,1,0:T(8,128)} %get-tuple-element.89.refs_12_.rest_0_), channel_id=1, source_target_pairs={{0,124},{1,125},{2,126},{3,127},{4,0},{5,1},{6,2},{7,3},{8,4},{9,5... | collective-permute-start | bytes 786440 | tf_op jit(solution)/shard_map/ppermute | solution.py:456
  79.4 9.3 %collective-permute-start.17 = (f32[4,128,128]{2,1,0:T(8,128)}, f32[4,128,128]{2,1,0:T(8,128)S(1)}, u32[]{:S(2)}, u32[]{:S(2)}) collective-permute-start(f32[4,128,128]{2,1,0:T(8,128)} %get-tuple-element.89.refs_12_.rest_0_), channel_id=1, source_target_pairs={{0,4},{1,5},{2,6},{3,7},{4,8},{5,9},{6,10},{7,11},{8,12},{9,13},{1... | collective-permute-start | bytes 786440 | tf_op jit(solution)/shard_map/ppermute | solution.py:456
  79.4 18.6 %collective-permute-start.16 = (f32[4,128,128]{2,1,0:T(8,128)}, f32[4,128,128]{2,1,0:T(8,128)S(1)}, u32[]{:S(2)}, u32[]{:S(2)}) collective-permute-start(f32[4,128,128]{2,1,0:T(8,128)} %get-tuple-element.89.refs_12_.rest_0_), channel_id=1, source_target_pairs={{0,3},{1,0},{2,1},{3,2},{4,7},{5,4},{6,5},{7,6},{8,11},{9,8},{10,9... | collective-permute-start | bytes 786440 | tf_op jit(solution)/shard_map/ppermute | solution.py:456
  81.0 30.1 %collective-permute-start.7 = (f32[2,128,384]{2,1,0:T(8,128)S(1)}, f32[2,128,384]{2,1,0:T(8,128)S(1)}, u32[]{:S(2)}, u32[]{:S(2)}) collective-permute-start(f32[2,128,384]{2,1,0:T(8,128)S(1)} %copy-done.36), channel_id=1, source_target_pairs={{0,1},{1,2},{2,3},{3,0},{4,5},{5,6},{6,7},{7,4},{8,9},{9,10},{10,1... | collective-permute-start | bytes 1179656 | tf_op jit(solution)/shard_map/ppermute | solution.py:456
  81.4 30.7 %collective-permute-start.8 = (f32[2,128,384]{2,1,0:T(8,128)S(1)}, f32[2,128,384]{2,1,0:T(8,128)S(1)}, u32[]{:S(2)}, u32[]{:S(2)}) collective-permute-start(f32[2,128,384]{2,1,0:T(8,128)S(1)} %copy-done.35), channel_id=1, source_target_pairs={{0,2},{1,3},{2,0},{3,1},{4,6},{5,7},{6,4},{7,5},{8,10},{9,11},{10,... | collective-permute-start | bytes 1179656 | tf_op jit(solution)/shard_map/ppermute | solution.py:456
  83.6 65.4 %copy-start = (f32[4,128,128]{2,1,0:T(8,128)}, f32[4,128,128]{2,1,0:T(8,128)S(1)}, u32[]{:S(2)}) copy-start(f32[4,128,128]{2,1,0:T(8,128)S(1)} %collective-permute-done.21.refs_20_.rest_4_) | copy-start | bytes 786436
  83.6 23.0 %collective-permute-start.15 = (f32[4,128,128]{2,1,0:T(8,128)}, f32[4,128,128]{2,1,0:T(8,128)S(1)}, u32[]{:S(2)}, u32[]{:S(2)}) collective-permute-start(f32[4,128,128]{2,1,0:T(8,128)} %get-tuple-element.89.refs_12_.rest_0_), channel_id=1, source_target_pairs={{0,2},{1,3},{2,0},{3,1},{4,6},{5,7},{6,4},{7,5},{8,10},{9,11},{10,... | collective-permute-start | bytes 786440 | tf_op jit(solution)/shard_map/ppermute | solution.py:456
  88.7 60.3 %copy-start.38 = (f32[4,128,128]{2,1,0:T(8,128)}, f32[4,128,128]{2,1,0:T(8,128)S(1)}, u32[]{:S(2)}) copy-start(f32[4,128,128]{2,1,0:T(8,128)S(1)} %collective-permute-done.17.refs_16_) | copy-start | bytes 786436
  88.7 22.3 %collective-permute-start.14 = (f32[4,128,128]{2,1,0:T(8,128)}, f32[4,128,128]{2,1,0:T(8,128)S(1)}, u32[]{:S(2)}, u32[]{:S(2)}) collective-permute-start(f32[4,128,128]{2,1,0:T(8,128)} %get-tuple-element.89.refs_12_.rest_0_), channel_id=1, source_target_pairs={{0,1},{1,2},{2,3},{3,0},{4,5},{5,6},{6,7},{7,4},{8,9},{9,10},{10,1... | collective-permute-start | bytes 786440 | tf_op jit(solution)/shard_map/ppermute | solution.py:456
  98.1 51.0 %copy-start.1 = (f32[4,128,128]{2,1,0:T(8,128)}, f32[4,128,128]{2,1,0:T(8,128)S(1)}, u32[]{:S(2)}) copy-start(f32[4,128,128]{2,1,0:T(8,128)S(1)} %collective-permute-done.16.refs_15_.rest_3_) | copy-start | bytes 786436
  98.1 16.4 %collective-permute-start.9 = (f32[2,128,384]{2,1,0:T(8,128)S(1)}, f32[2,128,384]{2,1,0:T(8,128)S(1)}, u32[]{:S(2)}, u32[]{:S(2)}) collective-permute-start(f32[2,128,384]{2,1,0:T(8,128)S(1)} %copy-done.34), channel_id=1, source_target_pairs={{0,3},{1,0},{2,1},{3,2},{4,7},{5,4},{6,5},{7,6},{8,11},{9,8},{10,9... | collective-permute-start | bytes 1179656 | tf_op jit(solution)/shard_map/ppermute | solution.py:456
  106.7 42.4 %copy-start.2 = (f32[4,128,128]{2,1,0:T(8,128)}, f32[4,128,128]{2,1,0:T(8,128)S(1)}, u32[]{:S(2)}) copy-start(f32[4,128,128]{2,1,0:T(8,128)S(1)} %collective-permute-done.15.refs_14_.rest_2_) | copy-start | bytes 786436
  106.7 11.1 %collective-permute-start.10 = (f32[2,128,384]{2,1,0:T(8,128)S(1)}, f32[2,128,384]{2,1,0:T(8,128)S(1)}, u32[]{:S(2)}, u32[]{:S(2)}) collective-permute-start(f32[2,128,384]{2,1,0:T(8,128)S(1)} %copy-done.33), channel_id=1, source_target_pairs={{0,4},{1,5},{2,6},{3,7},{4,8},{5,9},{6,10},{7,11},{8,12},{9,13},{1... | collective-permute-start | bytes 1179656 | tf_op jit(solution)/shard_map/ppermute | solution.py:456
  111.0 13.3 %collective-permute-start.11 = (f32[2,128,384]{2,1,0:T(8,128)S(1)}, f32[2,128,384]{2,1,0:T(8,128)S(1)}, u32[]{:S(2)}, u32[]{:S(2)}) collective-permute-start(f32[2,128,384]{2,1,0:T(8,128)S(1)} %copy-done.32), channel_id=1, source_target_pairs={{0,5},{1,6},{2,7},{3,4},{4,9},{5,10},{6,11},{7,8},{8,13},{9,14},{1... | collective-permute-start | bytes 1179656 | tf_op jit(solution)/shard_map/ppermute | solution.py:456
  111.1 23.8 %collective-permute-start.12 = (f32[2,128,384]{2,1,0:T(8,128)S(1)}, f32[2,128,384]{2,1,0:T(8,128)S(1)}, u32[]{:S(2)}, u32[]{:S(2)}) collective-permute-start(f32[2,128,384]{2,1,0:T(8,128)S(1)} %copy-done.31), channel_id=1, source_target_pairs={{0,6},{1,7},{2,4},{3,5},{4,10},{5,11},{6,8},{7,9},{8,14},{9,15},{1... | collective-permute-start | bytes 1179656 | tf_op jit(solution)/shard_map/ppermute | solution.py:456
  112.2 22.7 %collective-permute-start.13 = (f32[2,128,384]{2,1,0:T(8,128)S(1)}, f32[2,128,384]{2,1,0:T(8,128)S(1)}, u32[]{:S(2)}, u32[]{:S(2)}) collective-permute-start(f32[2,128,384]{2,1,0:T(8,128)S(1)} %copy-done.30), channel_id=1, source_target_pairs={{0,7},{1,4},{2,5},{3,6},{4,11},{5,8},{6,9},{7,10},{8,15},{9,12},{1... | collective-permute-start | bytes 1179656 | tf_op jit(solution)/shard_map/ppermute | solution.py:456
  114.4 25.5 %collective-permute-start.24 = (f32[4,128,128]{2,1,0:T(8,128)S(1)}, f32[4,128,128]{2,1,0:T(8,128)S(1)}, u32[]{:S(2)}, u32[]{:S(2)}) collective-permute-start(f32[4,128,128]{2,1,0:T(8,128)S(1)} %collective-permute-done.16.refs_15_.rest_3_), channel_id=1, source_target_pairs={{0,124},{1,125},{2,126},{3,127},{4,0},{5,1},{6,2},{7,3},{8,4},{9,5... | collective-permute-start | bytes 786440 | tf_op jit(solution)/shard_map/ppermute | solution.py:456
  117.8 22.1 %collective-permute-start.20 = (f32[4,128,128]{2,1,0:T(8,128)S(1)}, f32[4,128,128]{2,1,0:T(8,128)S(1)}, u32[]{:S(2)}, u32[]{:S(2)}) collective-permute-start(f32[4,128,128]{2,1,0:T(8,128)S(1)} %collective-permute-done.16.refs_15_.rest_3_), channel_id=1, source_target_pairs={{0,4},{1,5},{2,6},{3,7},{4,8},{5,9},{6,10},{7,11},{8,12},{9,13},{1... | collective-permute-start | bytes 786440 | tf_op jit(solution)/shard_map/ppermute | solution.py:456
  124.3 15.7 %collective-permute-start.23 = (f32[4,128,128]{2,1,0:T(8,128)S(1)}, f32[4,128,128]{2,1,0:T(8,128)S(1)}, u32[]{:S(2)}, u32[]{:S(2)}) collective-permute-start(f32[4,128,128]{2,1,0:T(8,128)S(1)} %collective-permute-done.15.refs_14_.rest_2_), channel_id=1, source_target_pairs={{0,124},{1,125},{2,126},{3,127},{4,0},{5,1},{6,2},{7,3},{8,4},{9,5... | collective-permute-start | bytes 786440 | tf_op jit(solution)/shard_map/ppermute | solution.py:456
  134.9 9.1 %collective-permute-start.19 = (f32[4,128,128]{2,1,0:T(8,128)S(1)}, f32[4,128,128]{2,1,0:T(8,128)S(1)}, u32[]{:S(2)}, u32[]{:S(2)}) collective-permute-start(f32[4,128,128]{2,1,0:T(8,128)S(1)} %collective-permute-done.15.refs_14_.rest_2_), channel_id=1, source_target_pairs={{0,4},{1,5},{2,6},{3,7},{4,8},{5,9},{6,10},{7,11},{8,12},{9,13},{1... | collective-permute-start | bytes 786440 | tf_op jit(solution)/shard_map/ppermute | solution.py:456
  134.9 9.1 %collective-permute-start.22 = (f32[4,128,128]{2,1,0:T(8,128)S(1)}, f32[4,128,128]{2,1,0:T(8,128)S(1)}, u32[]{:S(2)}, u32[]{:S(2)}) collective-permute-start(f32[4,128,128]{2,1,0:T(8,128)S(1)} %collective-permute-done.14.refs_13_.rest_1_), channel_id=1, source_target_pairs={{0,124},{1,125},{2,126},{3,127},{4,0},{5,1},{6,2},{7,3},{8,4},{9,5... | collective-permute-start | bytes 786440 | tf_op jit(solution)/shard_map/ppermute | solution.py:456
  139.9 9.1 %collective-permute-start.18 = (f32[4,128,128]{2,1,0:T(8,128)S(1)}, f32[4,128,128]{2,1,0:T(8,128)S(1)}, u32[]{:S(2)}, u32[]{:S(2)}) collective-permute-start(f32[4,128,128]{2,1,0:T(8,128)S(1)} %collective-permute-done.14.refs_13_.rest_1_), channel_id=1, source_target_pairs={{0,4},{1,5},{2,6},{3,7},{4,8},{5,9},{6,10},{7,11},{8,12},{9,13},{1... | collective-permute-start | bytes 786440 | tf_op jit(solution)/shard_map/ppermute | solution.py:456
  155.6 44.2 %copy-start.21 = (f32[8,128]{1,0:T(8,128)S(1)}, f32[8,128]{1,0:T(8,128)}, u32[]{:S(2)}) copy-start(f32[8,128]{1,0:T(8,128)} %get-tuple-element.77) | copy-start | bytes 12292
  155.6 44.2 %copy-start.22 = (f32[8,128]{1,0:T(8,128)S(1)}, f32[8,128]{1,0:T(8,128)}, u32[]{:S(2)}) copy-start(f32[8,128]{1,0:T(8,128)} %get-tuple-element.90) | copy-start | bytes 12292
  155.6 9.3 %collective-permute-start.27 = (f32[4,128,128]{2,1,0:T(8,128)}, f32[4,128,128]{2,1,0:T(8,128)S(1)}, u32[]{:S(2)}, u32[]{:S(2)}) collective-permute-start(f32[4,128,128]{2,1,0:T(8,128)} %get-tuple-element.93.refs_12_.rest_8_), channel_id=1, source_target_pairs={{0,3},{1,0},{2,1},{3,2},{4,7},{5,4},{6,5},{7,6},{8,11},{9,8},{10,9... | collective-permute-start | bytes 786440 | tf_op jit(solution)/shard_map/ppermute | solution.py:456
  155.8 9.1 %collective-permute-start.32 = (f32[4,128,128]{2,1,0:T(8,128)}, f32[4,128,128]{2,1,0:T(8,128)S(1)}, u32[]{:S(2)}, u32[]{:S(2)}) collective-permute-start(f32[4,128,128]{2,1,0:T(8,128)} %get-tuple-element.93.refs_12_.rest_8_), channel_id=1, source_target_pairs={{0,124},{1,125},{2,126},{3,127},{4,0},{5,1},{6,2},{7,3},{8,4},{9,5... | collective-permute-start | bytes 786440 | tf_op jit(solution)/shard_map/ppermute | solution.py:456
  155.8 10.9 %collective-permute-start.26 = (f32[4,128,128]{2,1,0:T(8,128)}, f32[4,128,128]{2,1,0:T(8,128)S(1)}, u32[]{:S(2)}, u32[]{:S(2)}) collective-permute-start(f32[4,128,128]{2,1,0:T(8,128)} %get-tuple-element.93.refs_12_.rest_8_), channel_id=1, source_target_pairs={{0,2},{1,3},{2,0},{3,1},{4,6},{5,7},{6,4},{7,5},{8,10},{9,11},{10,... | collective-permute-start | bytes 786440 | tf_op jit(solution)/shard_map/ppermute | solution.py:456
  155.9 14.2 %collective-permute-start.28 = (f32[4,128,128]{2,1,0:T(8,128)}, f32[4,128,128]{2,1,0:T(8,128)S(1)}, u32[]{:S(2)}, u32[]{:S(2)}) collective-permute-start(f32[4,128,128]{2,1,0:T(8,128)} %get-tuple-element.93.refs_12_.rest_8_), channel_id=1, source_target_pairs={{0,4},{1,5},{2,6},{3,7},{4,8},{5,9},{6,10},{7,11},{8,12},{9,13},{1... | collective-permute-start | bytes 786440 | tf_op jit(solution)/shard_map/ppermute | solution.py:456
  156.3 15.6 %collective-permute-start.25 = (f32[4,128,128]{2,1,0:T(8,128)}, f32[4,128,128]{2,1,0:T(8,128)S(1)}, u32[]{:S(2)}, u32[]{:S(2)}) collective-permute-start(f32[4,128,128]{2,1,0:T(8,128)} %get-tuple-element.93.refs_12_.rest_8_), channel_id=1, source_target_pairs={{0,1},{1,2},{2,3},{3,0},{4,5},{5,6},{6,7},{7,4},{8,9},{9,10},{10,1... | collective-permute-start | bytes 786440 | tf_op jit(solution)/shard_map/ppermute | solution.py:456
  164.9 10.2 %collective-permute-start.35 = (f32[4,128,128]{2,1,0:T(8,128)S(1)}, f32[4,128,128]{2,1,0:T(8,128)S(1)}, u32[]{:S(2)}, u32[]{:S(2)}) collective-permute-start(f32[4,128,128]{2,1,0:T(8,128)S(1)} %collective-permute-done.27.refs_15_.rest_11_), channel_id=1, source_target_pairs={{0,124},{1,125},{2,126},{3,127},{4,0},{5,1},{6,2},{7,3},{8,4},{9,5... | collective-permute-start | bytes 786440 | tf_op jit(solution)/shard_map/ppermute | solution.py:456
  164.9 10.2 %collective-permute-start.31 = (f32[4,128,128]{2,1,0:T(8,128)S(1)}, f32[4,128,128]{2,1,0:T(8,128)S(1)}, u32[]{:S(2)}, u32[]{:S(2)}) collective-permute-start(f32[4,128,128]{2,1,0:T(8,128)S(1)} %collective-permute-done.27.refs_15_.rest_11_), channel_id=1, source_target_pairs={{0,4},{1,5},{2,6},{3,7},{4,8},{5,9},{6,10},{7,11},{8,12},{9,13},{1... | collective-permute-start | bytes 786440 | tf_op jit(solution)/shard_map/ppermute | solution.py:456
  166.7 8.4 %collective-permute-start.34 = (f32[4,128,128]{2,1,0:T(8,128)S(1)}, f32[4,128,128]{2,1,0:T(8,128)S(1)}, u32[]{:S(2)}, u32[]{:S(2)}) collective-permute-start(f32[4,128,128]{2,1,0:T(8,128)S(1)} %collective-permute-done.26.refs_14_.rest_10_), channel_id=1, source_target_pairs={{0,124},{1,125},{2,126},{3,127},{4,0},{5,1},{6,2},{7,3},{8,4},{9,5... | collective-permute-start | bytes 786440 | tf_op jit(solution)/shard_map/ppermute | solution.py:456
  170.1 9.1 %collective-permute-start.30 = (f32[4,128,128]{2,1,0:T(8,128)S(1)}, f32[4,128,128]{2,1,0:T(8,128)S(1)}, u32[]{:S(2)}, u32[]{:S(2)}) collective-permute-start(f32[4,128,128]{2,1,0:T(8,128)S(1)} %collective-permute-done.26.refs_14_.rest_10_), channel_id=1, source_target_pairs={{0,4},{1,5},{2,6},{3,7},{4,8},{5,9},{6,10},{7,11},{8,12},{9,13},{1... | collective-permute-start | bytes 786440 | tf_op jit(solution)/shard_map/ppermute | solution.py:456
  171.8 7.4 %collective-permute-start.33 = (f32[4,128,128]{2,1,0:T(8,128)S(1)}, f32[4,128,128]{2,1,0:T(8,128)S(1)}, u32[]{:S(2)}, u32[]{:S(2)}) collective-permute-start(f32[4,128,128]{2,1,0:T(8,128)S(1)} %collective-permute-done.25.refs_13_.rest_9_), channel_id=1, source_target_pairs={{0,124},{1,125},{2,126},{3,127},{4,0},{5,1},{6,2},{7,3},{8,4},{9,5... | collective-permute-start | bytes 786440 | tf_op jit(solution)/shard_map/ppermute | solution.py:456
  175.2 9.1 %collective-permute-start.29 = (f32[4,128,128]{2,1,0:T(8,128)S(1)}, f32[4,128,128]{2,1,0:T(8,128)S(1)}, u32[]{:S(2)}, u32[]{:S(2)}) collective-permute-start(f32[4,128,128]{2,1,0:T(8,128)S(1)} %collective-permute-done.25.refs_13_.rest_9_), channel_id=1, source_target_pairs={{0,4},{1,5},{2,6},{3,7},{4,8},{5,9},{6,10},{7,11},{8,12},{9,13},{1... | collective-permute-start | bytes 786440 | tf_op jit(solution)/shard_map/ppermute | solution.py:456
  190.9 8.9 %collective-permute-start.38 = (f32[4,128,128]{2,1,0:T(8,128)}, f32[4,128,128]{2,1,0:T(8,128)S(1)}, u32[]{:S(2)}, u32[]{:S(2)}) collective-permute-start(f32[4,128,128]{2,1,0:T(8,128)} %get-tuple-element.94.refs_12_.rest_16_), channel_id=1, source_target_pairs={{0,3},{1,0},{2,1},{3,2},{4,7},{5,4},{6,5},{7,6},{8,11},{9,8},{10,9... | collective-permute-start | bytes 786440 | tf_op jit(solution)/shard_map/ppermute | solution.py:456
  191.5 8.4 %collective-permute-start.43 = (f32[4,128,128]{2,1,0:T(8,128)}, f32[4,128,128]{2,1,0:T(8,128)S(1)}, u32[]{:S(2)}, u32[]{:S(2)}) collective-permute-start(f32[4,128,128]{2,1,0:T(8,128)} %get-tuple-element.94.refs_12_.rest_16_), channel_id=1, source_target_pairs={{0,124},{1,125},{2,126},{3,127},{4,0},{5,1},{6,2},{7,3},{8,4},{9,5... | collective-permute-start | bytes 786440 | tf_op jit(solution)/shard_map/ppermute | solution.py:456
  191.8 10.9 %collective-permute-start.37 = (f32[4,128,128]{2,1,0:T(8,128)}, f32[4,128,128]{2,1,0:T(8,128)S(1)}, u32[]{:S(2)}, u32[]{:S(2)}) collective-permute-start(f32[4,128,128]{2,1,0:T(8,128)} %get-tuple-element.94.refs_12_.rest_16_), channel_id=1, source_target_pairs={{0,2},{1,3},{2,0},{3,1},{4,6},{5,7},{6,4},{7,5},{8,10},{9,11},{10,... | collective-permute-start | bytes 786440 | tf_op jit(solution)/shard_map/ppermute | solution.py:456
  193.3 11.7 %collective-permute-start.39 = (f32[4,128,128]{2,1,0:T(8,128)}, f32[4,128,128]{2,1,0:T(8,128)S(1)}, u32[]{:S(2)}, u32[]{:S(2)}) collective-permute-start(f32[4,128,128]{2,1,0:T(8,128)} %get-tuple-element.94.refs_12_.rest_16_), channel_id=1, source_target_pairs={{0,4},{1,5},{2,6},{3,7},{4,8},{5,9},{6,10},{7,11},{8,12},{9,13},{1... | collective-permute-start | bytes 786440 | tf_op jit(solution)/shard_map/ppermute | solution.py:456
  193.3 14.2 %collective-permute-start.36 = (f32[4,128,128]{2,1,0:T(8,128)}, f32[4,128,128]{2,1,0:T(8,128)S(1)}, u32[]{:S(2)}, u32[]{:S(2)}) collective-permute-start(f32[4,128,128]{2,1,0:T(8,128)} %get-tuple-element.94.refs_12_.rest_16_), channel_id=1, source_target_pairs={{0,1},{1,2},{2,3},{3,0},{4,5},{5,6},{6,7},{7,4},{8,9},{9,10},{10,1... | collective-permute-start | bytes 786440 | tf_op jit(solution)/shard_map/ppermute | solution.py:456
  199.8 63.8 %copy-start.14 = (f32[4,128,128]{2,1,0:T(8,128)}, f32[4,128,128]{2,1,0:T(8,128)S(1)}, u32[]{:S(2)}) copy-start(f32[4,128,128]{2,1,0:T(8,128)S(1)} %collective-permute-done.38.refs_15_.rest_19_) | copy-start | bytes 786436
  199.8 10.3 %collective-permute-start.46 = (f32[4,128,128]{2,1,0:T(8,128)S(1)}, f32[4,128,128]{2,1,0:T(8,128)S(1)}, u32[]{:S(2)}, u32[]{:S(2)}) collective-permute-start(f32[4,128,128]{2,1,0:T(8,128)S(1)} %collective-permute-done.38.refs_15_.rest_19_), channel_id=1, source_target_pairs={{0,124},{1,125},{2,126},{3,127},{4,0},{5,1},{6,2},{7,3},{8,4},{9,5... | collective-permute-start | bytes 786440 | tf_op jit(solution)/shard_map/ppermute | solution.py:456
  199.9 63.8 %copy-start.15 = (f32[4,128,128]{2,1,0:T(8,128)}, f32[4,128,128]{2,1,0:T(8,128)S(1)}, u32[]{:S(2)}) copy-start(f32[4,128,128]{2,1,0:T(8,128)S(1)} %collective-permute-done.43.refs_20_.rest_20_) | copy-start | bytes 786436
  199.9 63.7 %collective-permute-start.42 = (f32[4,128,128]{2,1,0:T(8,128)S(1)}, f32[4,128,128]{2,1,0:T(8,128)S(1)}, u32[]{:S(2)}, u32[]{:S(2)}) collective-permute-start(f32[4,128,128]{2,1,0:T(8,128)S(1)} %collective-permute-done.38.refs_15_.rest_19_), channel_id=1, source_target_pairs={{0,4},{1,5},{2,6},{3,7},{4,8},{5,9},{6,10},{7,11},{8,12},{9,13},{1... | collective-permute-start | bytes 786440 | tf_op jit(solution)/shard_map/ppermute | solution.py:456
  202.7 60.9 %copy-start.16 = (f32[4,128,128]{2,1,0:T(8,128)}, f32[4,128,128]{2,1,0:T(8,128)S(1)}, u32[]{:S(2)}) copy-start(f32[4,128,128]{2,1,0:T(8,128)S(1)} %collective-permute-done.37.refs_14_.rest_18_) | copy-start | bytes 786436
  202.7 60.8 %collective-permute-start.45 = (f32[4,128,128]{2,1,0:T(8,128)S(1)}, f32[4,128,128]{2,1,0:T(8,128)S(1)}, u32[]{:S(2)}, u32[]{:S(2)}) collective-permute-start(f32[4,128,128]{2,1,0:T(8,128)S(1)} %collective-permute-done.37.refs_14_.rest_18_), channel_id=1, source_target_pairs={{0,124},{1,125},{2,126},{3,127},{4,0},{5,1},{6,2},{7,3},{8,4},{9,5... | collective-permute-start | bytes 786440 | tf_op jit(solution)/shard_map/ppermute | solution.py:456
  205.0 58.6 %copy-start.37 = (f32[4,128,128]{2,1,0:T(8,128)}, f32[4,128,128]{2,1,0:T(8,128)S(1)}, u32[]{:S(2)}) copy-start(f32[4,128,128]{2,1,0:T(8,128)S(1)} %collective-permute-done.39.refs_16_) | copy-start | bytes 786436
  205.0 58.6 %collective-permute-start.41 = (f32[4,128,128]{2,1,0:T(8,128)S(1)}, f32[4,128,128]{2,1,0:T(8,128)S(1)}, u32[]{:S(2)}, u32[]{:S(2)}) collective-permute-start(f32[4,128,128]{2,1,0:T(8,128)S(1)} %collective-permute-done.37.refs_14_.rest_18_), channel_id=1, source_target_pairs={{0,4},{1,5},{2,6},{3,7},{4,8},{5,9},{6,10},{7,11},{8,12},{9,13},{1... | collective-permute-start | bytes 786440 | tf_op jit(solution)/shard_map/ppermute | solution.py:456
  207.6 56.1 %copy-start.17 = (f32[4,128,128]{2,1,0:T(8,128)}, f32[4,128,128]{2,1,0:T(8,128)S(1)}, u32[]{:S(2)}) copy-start(f32[4,128,128]{2,1,0:T(8,128)S(1)} %collective-permute-done.36.refs_13_.rest_17_) | copy-start | bytes 786436
  207.6 56.0 %collective-permute-start.44 = (f32[4,128,128]{2,1,0:T(8,128)S(1)}, f32[4,128,128]{2,1,0:T(8,128)S(1)}, u32[]{:S(2)}, u32[]{:S(2)}) collective-permute-start(f32[4,128,128]{2,1,0:T(8,128)S(1)} %collective-permute-done.36.refs_13_.rest_17_), channel_id=1, source_target_pairs={{0,124},{1,125},{2,126},{3,127},{4,0},{5,1},{6,2},{7,3},{8,4},{9,5... | collective-permute-start | bytes 786440 | tf_op jit(solution)/shard_map/ppermute | solution.py:456
  210.1 53.6 %copy-start.18 = (f32[4,128,128]{2,1,0:T(8,128)}, f32[4,128,128]{2,1,0:T(8,128)S(1)}, u32[]{:S(2)}) copy-start(f32[4,128,128]{2,1,0:T(8,128)S(1)} %collective-permute-done.46.refs_23_.rest_23_) | copy-start | bytes 786436
  210.1 53.5 %collective-permute-start.40 = (f32[4,128,128]{2,1,0:T(8,128)S(1)}, f32[4,128,128]{2,1,0:T(8,128)S(1)}, u32[]{:S(2)}, u32[]{:S(2)}) collective-permute-start(f32[4,128,128]{2,1,0:T(8,128)S(1)} %collective-permute-done.36.refs_13_.rest_17_), channel_id=1, source_target_pairs={{0,4},{1,5},{2,6},{3,7},{4,8},{5,9},{6,10},{7,11},{8,12},{9,13},{1... | collective-permute-start | bytes 786440 | tf_op jit(solution)/shard_map/ppermute | solution.py:456
  (39 other events, 478.1 us)

commit v2 on v1

v2 whole, which is shorter than its diff:
```python
import jax
import jax.numpy as jnp
from jax import lax
from jax.experimental import pallas as pl
from jax.experimental.pallas import tpu as pltpu
from jax.sharding import PartitionSpec as P

F32 = jnp.float32
BF16 = jnp.bfloat16
SUB_DEV = 4
SLOTS = 4
TILE = 128
NI = 512
NRHS = 128
SEP_DEV = 4
PER_DEV = SUB_DEV * SLOTS
BLOCK = 32
MIB = 1024 * 1024

PIECES = [
    [(0, 0)], [(0, 1)], [(0, 3)], [(0, 2)],
    [(1, 0)], [(1, 1), (1, 3)], [(1, 2)],
    [(2, 0), (2, 1), (2, 3), (2, 2)],
]
HALF = TILE // 2
PACKED = HALF + 8
NORM_ROWS = 8
SPREAD = SEP_DEV * TILE + NORM_ROWS


def halves(x):
    high = x.astype(BF16)
    low = (x - high.astype(F32)).astype(BF16)
    return high, low


def product(a, b):
    return lax.dot_general(a, b, (((1,), (0,)), ((), ())), preferred_element_type=F32)


def dot3(a, b):
    (ah, al), (bh, bl) = a, b
    return product(jnp.concatenate([ah, al, ah], 1), jnp.concatenate([bl, bh, bh], 0))


def dot4(stacked, paired):
    m, n = stacked.shape[0] // 2, paired.shape[1] // 2
    r = product(stacked, paired)
    return (r[m:, n:] + (r[m:, :n] + r[:m, n:])) + r[:m, :n]


def stack_halves(x):
    return jnp.concatenate(halves(x), axis=0)


def pair_halves(x):
    return jnp.concatenate(halves(x), axis=1)


def params(mib):
    return pltpu.CompilerParams(vmem_limit_bytes=mib * MIB)


SMEM = pl.BlockSpec(memory_space=pltpu.SMEM)
VMEM = pl.BlockSpec(memory_space=pltpu.VMEM)


def log2(n):
    assert n & (n - 1) == 0
    return n.bit_length() - 1


def send_slots(place_ref, list_ref, owner_ref, slot_ref, count_ref, n_region, n_sub):
    region, sub = place_ref[0], place_ref[1]
    begin = (n_sub + sub) * PER_DEV
    for c in range(2 * n_sub):
        count_ref[c] = 0

    def step(n, carry):
        dev = owner_ref[list_ref[begin + n]] >> log2(SEP_DEV)
        ahead = ((dev >> log2(n_sub)) - region) & (n_region - 1)
        turn = (dev - sub) & (n_sub - 1)
        key = ((ahead & 1) << log2(n_sub)) + turn
        rank = count_ref[key]
        count_ref[key] = rank + 1
        slot_ref[n] = key * 2 + rank
        return carry

    lax.fori_loop(0, PER_DEV, step, 0)


def plan_kernel(n_region, n_sub, place_ref, list_ref, owner_ref, target_ref, seen_ref, own_ref, next_ref):
    region, sub = place_ref[0], place_ref[1]
    me = region * n_sub + sub
    after = ((region + 1) & (n_region - 1)) * n_sub + sub

    def tile_at(pos):
        dev = pos >> log2(SEP_DEV)
        there = dev >> log2(n_sub)
        side = jnp.where(there == region, 0, jnp.where(there == (region ^ 1), 2, 1))
        turn = (sub - dev) & (n_sub - 1)
        return (side * n_sub + turn) * SEP_DEV + (pos & (SEP_DEV - 1))

    def source_step(source, carry):
        behind = 1 - (source >> log2(n_sub))
        turn = (sub - source) & (n_sub - 1)
        first = (behind * n_sub + turn) * 2

        def step(n, carry):
            slot, later = carry
            at = source * PER_DEV + n
            pos = owner_ref[list_ref[at]]
            dev = pos >> log2(SEP_DEV)
            mine = dev == me
            ahead = (dev == after) & (behind == 0)

            @pl.when(mine)
            def _():
                target_ref[slot] = pos & (SEP_DEV - 1)
                base = at & ~(SLOTS - 1)
                for k in range(1, SLOTS):
                    other = owner_ref[list_ref[base + ((n + k) & (SLOTS - 1))]]
                    seen_ref[slot * (SLOTS - 1) + k - 1] = tile_at(other)

            @pl.when(ahead)
            def _():
                next_ref[later] = pos & (SEP_DEV - 1)

            return jnp.where(mine, slot + 1, slot), jnp.where(ahead, later + 1, later)

        lax.fori_loop(0, PER_DEV, step, (first, turn * 2), unroll=4)
        return carry

    lax.fori_loop(0, 2 * n_sub, source_step, 0)
    begin = (n_sub + sub) * PER_DEV

    def mine(i, carry):
        own_ref[i] = tile_at(owner_ref[list_ref[begin + i]])
        return carry

    lax.fori_loop(0, PER_DEV, mine, 0)


def plan(place, near, owner, n_region, n_sub):
    shapes = (PER_DEV, PER_DEV * (SLOTS - 1), PER_DEV, 2 * n_sub)
    return pl.pallas_call(
        lambda *refs: plan_kernel(n_region, n_sub, *refs),
        out_shape=tuple(jax.ShapeDtypeStruct((n,), jnp.int32) for n in shapes),
        in_specs=[SMEM] * 3,
        out_specs=(SMEM,) * 4,
        compiler_params=params(2),
        cost_estimate=pl.CostEstimate(flops=2 * 10**9, bytes_accessed=8192, transcendentals=0),
        name="plan",
    )(place, near, owner)


def pack_symmetric(t):
    row = lax.broadcasted_iota(jnp.int32, (HALF, TILE), 0)
    lane = lax.broadcasted_iota(jnp.int32, (HALF, TILE), 1)
    top, low = t[:HALF], t[HALF:]
    body = jnp.where(row <= lane, top, pltpu.roll(low, HALF, 1))
    ends = jnp.sum(jnp.where(row == lane - HALF, low, 0.0), axis=0, keepdims=True)
    return jnp.concatenate([body, jnp.broadcast_to(ends, (8, TILE))], axis=0)


def unpack_symmetric(f):
    row = lax.broadcasted_iota(jnp.int32, (HALF, TILE), 0)
    lane = lax.broadcasted_iota(jnp.int32, (HALF, TILE), 1)
    body, ends = f[:HALF], f[HALF : HALF + 1]
    top = jnp.where(row < lane, body, 0.0)
    low = jnp.where((row > lane - HALF) & (lane >= HALF), pltpu.roll(body, HALF, 1), 0.0)
    part = jnp.concatenate([top, low], axis=0)
    ends = jnp.where(row == lane - HALF, ends, 0.0)
    diagonal = jnp.concatenate([jnp.where(row == lane, body, 0.0), ends], axis=0)
    return part + part.T + diagonal


def eliminate_kernel(
    n_region, n_sub, place_ref, list_ref, owner_ref, live_ref, inverse_ref, coupling_ref, grad_ref,
    solved_ref, reduced_ref, *rest
):
    chunks, (pay_ref, left_ref, right_ref, turned_ref, pair_ref, slot_ref, count_ref) = rest[:4], rest[4:]
    i = pl.program_id(0)
    span = SLOTS * TILE

    @pl.when(i == 0)
    def _():
        send_slots(place_ref, list_ref, owner_ref, slot_ref, count_ref, n_region, n_sub)

    live = live_ref[i]
    ah, al = halves(inverse_ref[0])
    left_ref[:, :NI] = ah
    left_ref[:, NI : 2 * NI] = al
    left_ref[:, 2 * NI :] = ah
    for j in range(SLOTS + 1):
        x = grad_ref[0] if j == SLOTS else coupling_ref[0, j] * (j < live).astype(F32)
        cols = slice(j * TILE, (j + 1) * TILE)
        high, low = halves(x)
        right_ref[:NI, cols] = low
        right_ref[NI : 2 * NI, cols] = high
        right_ref[2 * NI :, cols] = high
        if j < SLOTS:
            th, tl = halves(x.T)
            turned_ref[2 * j * TILE : (2 * j + 1) * TILE] = th
            turned_ref[(2 * j + 1) * TILE : (2 * j + 2) * TILE] = tl
    both = product(left_ref[...], right_ref[...])
    reduced = both[:, span:]
    reduced_ref[0] = reduced
    rh, rl = halves(reduced)
    pair_ref[:, TILE : 2 * TILE] = rh
    pair_ref[:, 3 * TILE :] = rl
    for j in range(SLOTS):
        cols = slice(j * TILE, (j + 1) * TILE)
        sh, sl = halves(both[:, cols])
        solved_ref[0, :NI, cols] = sh
        solved_ref[0, NI:, cols] = sl
        pair_ref[:, :TILE] = sh
        pair_ref[:, 2 * TILE : 3 * TILE] = sl
        result = dot4(turned_ref[2 * j * TILE : (2 * j + 2) * TILE], pair_ref[...])
        slot = slot_ref[i * SLOTS + j]
        pay_ref[slot, :PACKED] = pack_symmetric(result[:, :TILE])
        pay_ref[slot, PACKED:] = result[:, TILE:]

    @pl.when(i == SUB_DEV - 1)
    def _():
        for c in range(4):
            chunks[c][:2] = pay_ref[2 * c : 2 * c + 2]
            chunks[c][2:] = pay_ref[8 + 2 * c : 10 + 2 * c]


def eliminate(place, near, owner, live, interior_inverse, coupling, interior_grad, n_region, n_sub):
    span = SLOTS * TILE
    tall = PACKED + TILE
    step = lambda i: (i, 0, 0)
    return pl.pallas_call(
        lambda *refs: eliminate_kernel(n_region, n_sub, *refs),
        grid=(SUB_DEV,),
        out_shape=(
            jax.ShapeDtypeStruct((SUB_DEV, 2 * NI, span), BF16),
            jax.ShapeDtypeStruct((SUB_DEV, NI, NRHS), F32),
        )
        + (jax.ShapeDtypeStruct((4, tall, TILE), F32),) * 4,
        in_specs=[SMEM] * 4
        + [
            pl.BlockSpec((1, NI, NI), step),
            pl.BlockSpec((1, SLOTS, NI, TILE), lambda i: (i, 0, 0, 0)),
            pl.BlockSpec((1, NI, NRHS), step),
        ],
        out_specs=(pl.BlockSpec((1, 2 * NI, span), step), pl.BlockSpec((1, NI, NRHS), step))
        + (pl.BlockSpec((4, tall, TILE), lambda i: (0, 0, 0)),) * 4,
        scratch_shapes=[
            pltpu.VMEM((PER_DEV, tall, TILE), F32),
            pltpu.VMEM((NI, 3 * NI), BF16),
            pltpu.VMEM((3 * NI, span + NRHS), BF16),
            pltpu.VMEM((2 * span, NI), BF16),
            pltpu.VMEM((NI, 2 * (TILE + NRHS)), BF16),
            pltpu.SMEM((PER_DEV,), jnp.int32),
            pltpu.SMEM((2 * n_sub,), jnp.int32),
        ],
        compiler_params=params(56),
        name="eliminate",
    )(place, near, owner, live, interior_inverse, coupling, interior_grad)


def couple_kernel(
    n_region, n_sub, place_ref, list_ref, owner_ref, live_ref, coupling_ref, solved_ref, *rest
):
    chunks, (pay_ref, turned_ref, right_ref, slot_ref, count_ref) = rest[:8], rest[8:]
    i = pl.program_id(0)

    @pl.when(i == 0)
    def _():
        send_slots(place_ref, list_ref, owner_ref, slot_ref, count_ref, n_region, n_sub)

    live = live_ref[i]
    for j in range(SLOTS):
        rows = slice(j * TILE, (j + 1) * TILE)
        th, tl = halves((coupling_ref[0, j] * (j < live).astype(F32)).T)
        turned_ref[rows, :NI] = th
        turned_ref[rows, NI : 2 * NI] = tl
        turned_ref[rows, 2 * NI :] = th
    right_ref[:NI] = solved_ref[0, NI:]
    right_ref[NI : 2 * NI] = solved_ref[0, :NI]
    right_ref[2 * NI :] = solved_ref[0, :NI]
    schur = product(turned_ref[...], right_ref[...])
    for j in range(SLOTS):
        slot = slot_ref[i * SLOTS + j]
        for k in range(1, SLOTS):
            other = (j + k) % SLOTS
            pay_ref[slot, :, (k - 1) * TILE : k * TILE] = schur[
                j * TILE : (j + 1) * TILE, other * TILE : (other + 1) * TILE
            ]

    @pl.when(i == SUB_DEV - 1)
    def _():
        for c in range(8):
            chunks[c][...] = pay_ref[2 * c : 2 * c + 2]


def couple(place, near, owner, live, coupling, solved, n_region, n_sub):
    span = SLOTS * TILE
    wide = (SLOTS - 1) * TILE
    return pl.pallas_call(
        lambda *refs: couple_kernel(n_region, n_sub, *refs),
        grid=(SUB_DEV,),
        out_shape=(jax.ShapeDtypeStruct((2, TILE, wide), F32),) * 8,
        in_specs=[SMEM] * 4
        + [
            pl.BlockSpec((1, SLOTS, NI, TILE), lambda i: (i, 0, 0, 0)),
            pl.BlockSpec((1, 2 * NI, span), lambda i: (i, 0, 0)),
        ],
        out_specs=(pl.BlockSpec((2, TILE, wide), lambda i: (0, 0, 0)),) * 8,
        scratch_shapes=[
            pltpu.VMEM((PER_DEV, TILE, wide), F32),
            pltpu.VMEM((span, 3 * NI), BF16),
            pltpu.VMEM((3 * NI, span), BF16),
            pltpu.SMEM((PER_DEV,), jnp.int32),
            pltpu.SMEM((2 * n_sub,), jnp.int32),
        ],
        compiler_params=params(32),
        cost_estimate=pl.CostEstimate(flops=8 * 10**9, bytes_accessed=12 * MIB, transcendentals=0),
        name="couple",
    )(place, near, owner, live, coupling, solved)


def lane_group(shape, axis):
    return lax.broadcasted_iota(jnp.int32, shape, axis) // BLOCK


def block_diagonal(w, kb):
    groups = TILE // BLOCK
    parts = []
    for m in range(groups):
        rows = w[m * BLOCK : (m + 1) * BLOCK]
        shift = ((m - kb) % groups) * BLOCK
        if shift:
            rows = pltpu.roll(rows, shift, 1)
        parts.append(jnp.where(lane_group(rows.shape, 1) == m, rows, 0.0))
    return parts


def packed_inverse(p):
    lane = lax.broadcasted_iota(jnp.int32, p.shape, 1)
    row_id = lax.broadcasted_iota(jnp.int32, p.shape, 0)
    group_base = lane // BLOCK * BLOCK
    for k in range(0, BLOCK, 2):
        first = jnp.take_along_axis(p, group_base + k, axis=1)
        second = jnp.take_along_axis(p, group_base + (k + 1), axis=1)
        a, c = first[k : k + 1], first[k + 1 : k + 2]
        b, d = second[k : k + 1], second[k + 1 : k + 2]
        recip = 1.0 / (a * d - b * c)
        at_first = lane == group_base + k
        at_second = lane == group_base + (k + 1)
        row0 = jnp.where(at_first[:1], 1.0, jnp.where(at_second[:1], 0.0, p[k : k + 1]))
        row1 = jnp.where(at_first[:1], 0.0, jnp.where(at_second[:1], 1.0, p[k + 1 : k + 2]))
        new0 = (d * row0 - b * row1) * recip
        new1 = (a * row1 - c * row0) * recip
        p = jnp.where(at_first | at_second, 0.0, p) - first * new0 - second * new1
        p = jnp.where(row_id == k, new0, jnp.where(row_id == k + 1, new1, p))
    return p


def batch_inverse(tiles):
    groups = TILE // BLOCK
    w = [
        jnp.concatenate([t[kb * BLOCK : (kb + 1) * BLOCK] for t in tiles], axis=0) for kb in range(groups)
    ]
    lane = lax.broadcasted_iota(jnp.int32, (TILE, TILE), 1)
    row_in = lax.broadcasted_iota(jnp.int32, (TILE, TILE), 0) % BLOCK
    for kb in range(groups):
        parts = block_diagonal(w[kb], kb)
        packed = packed_inverse(parts[0] + parts[1] + parts[2] + parts[3])
        inner = jnp.concatenate(
            [jnp.where(lane_group(packed.shape, 1) == m, packed, 0.0) for m in range(groups)], axis=0
        )
        in_block = lane // BLOCK == kb
        unit = (lane == kb * BLOCK + row_in).astype(F32)
        pivot = dot3(halves(inner), halves(jnp.where(in_block, unit, w[kb])))
        pivot_parts = halves(pivot)
        for other in range(groups):
            if other == kb:
                continue
            left = jnp.concatenate(block_diagonal(w[other], kb), axis=0)
            w[other] = jnp.where(in_block, 0.0, w[other]) - dot3(halves(left), pivot_parts)
        w[kb] = pivot
    return [
        jnp.concatenate([w[kb][m * BLOCK : (m + 1) * BLOCK] for kb in range(groups)], axis=0)
        for m in range(SEP_DEV)
    ]


def folded(x):
    return jnp.sum(x.reshape(-1, 8, x.shape[-1]), axis=0)


def gather_kernel(target_ref, next_ref, c0, c1, c2, c3, here_ref, next_sum_ref):
    here_ref[...] = jnp.zeros(here_ref.shape, F32)
    next_sum_ref[...] = jnp.zeros(here_ref.shape, F32)
    for turn, chunk in enumerate((c0, c1, c2, c3)):
        for rank in range(2):
            t = target_ref[2 * turn + rank]
            here_ref[t] = here_ref[t] + chunk[rank]
            t = next_ref[2 * turn + rank]
            next_sum_ref[t] = next_sum_ref[t] + chunk[2 + rank]


def gather(target, later, chunks):
    total = jax.ShapeDtypeStruct((SEP_DEV, PACKED + TILE, TILE), F32)
    return pl.pallas_call(
        gather_kernel,
        out_shape=(total, total),
        in_specs=[SMEM] * 2 + [VMEM] * 4,
        out_specs=(VMEM,) * 2,
        compiler_params=params(8),
        name="gather",
    )(target, later, *chunks)


def invert_kernel(hess_ref, grad_ref, here_ref, got_ref, inv_ref, u_ref):
    tiles = []
    for t in range(SEP_DEV):
        total = here_ref[t] + got_ref[t]
        tiles.append(hess_ref[t] - unpack_symmetric(total[:PACKED]))
        u_ref[t] = grad_ref[t] - total[PACKED:]
    inverses = batch_inverse(tiles)
    for t in range(SEP_DEV):
        inv_ref[t] = stack_halves(inverses[t])


def invert(hess, grad, here, got):
    return pl.pallas_call(
        invert_kernel,
        out_shape=(
            jax.ShapeDtypeStruct((SEP_DEV, 2 * TILE, TILE), BF16),
            jax.ShapeDtypeStruct((SEP_DEV, TILE, NRHS), F32),
        ),
        in_specs=[VMEM] * 4,
        out_specs=(VMEM,) * 2,
        compiler_params=params(14),
        cost_estimate=pl.CostEstimate(flops=10**10, bytes_accessed=4 * MIB, transcendentals=0),
        name="invert",
    )(hess, grad, here, got)


def precondition(inv_ref, u_ref, earlier, w_ref):
    norm = jnp.zeros((8, NRHS), F32)
    for t in range(SEP_DEV):
        u = u_ref[t]
        w = dot4(inv_ref[t], pair_halves(u))
        w_ref[t * TILE : (t + 1) * TILE] = w
        norm = norm + folded(u * w)
    norm = jnp.sum(norm, axis=0, keepdims=True)
    row = lax.broadcasted_iota(jnp.int32, (NORM_ROWS, NRHS), 0)
    w_ref[SEP_DEV * TILE :] = jnp.where(row == 0, norm if earlier is None else earlier, jnp.where(row == 1, norm, 0.0))


WIDE = jax.ShapeDtypeStruct((SPREAD, NRHS), F32)


def begin(inv, u):
    return pl.pallas_call(
        lambda inv_ref, u_ref, w_ref: precondition(inv_ref, u_ref, None, w_ref),
        out_shape=WIDE,
        in_specs=[VMEM] * 2,
        out_specs=VMEM,
        compiler_params=params(8),
        name="begin",
    )(inv, u)


def lay_out(pieces, v_ref, sides):
    for piece, spots in zip(pieces, PIECES):
        for n, (side, turn) in enumerate(spots):
            if side not in sides:
                continue
            for t in range(SEP_DEV):
                where = (sides.index(side) * 4 + turn) * SEP_DEV + t
                rows = n * SPREAD + t * TILE
                v_ref[where] = pair_halves(piece[rows : rows + TILE])


def scatter(target_ref, seen_ref, offs, v_ref, u_ref):
    u_ref[...] = jnp.zeros(u_ref.shape, F32)
    for a in range(PER_DEV):
        t = target_ref[a]
        right = [v_ref[seen_ref[a * (SLOTS - 1) + k]] for k in range(SLOTS - 1)]
        off = offs[a // 2][a % 2] if a < 8 else offs[4][a - 8]
        u_ref[t] = u_ref[t] + dot4(stack_halves(off), jnp.concatenate(right, axis=0))


def apply_kernel(target_ref, seen_ref, inv_ref, *rest):
    offs, pieces, (u_ref, w_ref, v_ref) = rest[:5], rest[5:13], rest[13:]
    lay_out(pieces, v_ref, (0, 1, 2))
    scatter(target_ref, seen_ref, offs, v_ref, u_ref)
    precondition(inv_ref, u_ref, pieces[0][SEP_DEV * TILE : SEP_DEV * TILE + 1], w_ref)


def apply(target, seen, inv, offs, pieces):
    tile = jax.ShapeDtypeStruct((SEP_DEV, TILE, NRHS), F32)
    return pl.pallas_call(
        apply_kernel,
        out_shape=(tile, WIDE),
        in_specs=[SMEM] * 2 + [VMEM] * 14,
        out_specs=(VMEM,) * 2,
        scratch_shapes=[pltpu.VMEM((12 * SEP_DEV, TILE, 2 * NRHS), BF16)],
        compiler_params=params(16),
        cost_estimate=pl.CostEstimate(flops=2 * 10**9, bytes_accessed=7 * MIB, transcendentals=0),
        name="apply",
    )(target, seen, inv, *offs, *pieces)


def listed(own_ref, v_ref, i):
    tiles = []
    for j in range(SLOTS):
        n = own_ref[i * SLOTS + j]
        tiles.append(v_ref[n])
    return jnp.concatenate(tiles, axis=0)


def ahead_kernel(own_ref, solved_ref, *rest):
    first, second, (ya_ref, yb_ref, v_ref) = rest[:8], rest[8:16], rest[16:]
    for pieces, y_ref in ((first, ya_ref), (second, yb_ref)):
        lay_out(pieces, v_ref, (0, 1, 2))
        for i in range(SUB_DEV):
            y_ref[i] = dot4(solved_ref[i], listed(own_ref, v_ref, i))


def ahead(own, solved, w0s, w1s):
    y = jax.ShapeDtypeStruct((SUB_DEV, NI, NRHS), F32)
    return pl.pallas_call(
        ahead_kernel,
        out_shape=(y, y),
        in_specs=[SMEM] + [VMEM] * 17,
        out_specs=(VMEM,) * 2,
        scratch_shapes=[pltpu.VMEM((12 * SEP_DEV, TILE, 2 * NRHS), BF16)],
        compiler_params=params(28),
        cost_estimate=pl.CostEstimate(flops=8 * 10**9, bytes_accessed=14 * MIB, transcendentals=0),
        name="ahead",
    )(own, solved, *w0s, *w1s)


def finish_kernel(
    target_ref, seen_ref, own_ref, norm_ref, solved_ref, reduced_ref, ya_ref, yb_ref, u1_ref, w0_ref, w1_ref, *rest
):
    offs, pieces, (interior_ref, x_ref, resid_ref, v_ref, u_ref) = rest[:5], rest[5:13], rest[13:]
    whole = lambda x: jnp.sum(jnp.sum(x, axis=0, keepdims=True), axis=1, keepdims=True)
    q = whole(norm_ref[1:2]) / whole(norm_ref[:1])
    g1 = 1.0 / (2.0 - q)
    g2 = 1.0 / (2.0 - q * g1)
    back = q * g2 * g1
    c0 = 1.0 + (1.0 + back) * g1 * q - 2.0 * g2 * g1 * q
    c1 = (1.0 + back) * g1 * 2.0
    c2 = 4.0 * g2 * g1
    lay_out(pieces, v_ref, (0, 1, 2))
    for i in range(SUB_DEV):
        y = dot4(solved_ref[i], listed(own_ref, v_ref, i))
        interior_ref[i] = reduced_ref[i] - (c0 * ya_ref[i] + c1 * yb_ref[i] + c2 * y)
    scatter(target_ref, seen_ref, offs, v_ref, u_ref)
    for t in range(SEP_DEV):
        rows = slice(t * TILE, (t + 1) * TILE)
        x_ref[t] = c0 * w0_ref[rows] + c1 * w1_ref[rows] + c2 * pieces[0][rows]
        resid_ref[t] = g1 * g2 * (4.0 * u_ref[t] - 3.0 * q * u1_ref[t])


def finish(target, seen, own, norms, solved, reduced, ya, yb, u1, w0, w1, offs, w2s):
    tile = jax.ShapeDtypeStruct((SEP_DEV, TILE, NRHS), F32)
    return pl.pallas_call(
        finish_kernel,
        out_shape=(jax.ShapeDtypeStruct((SUB_DEV, NI, NRHS), F32), tile, tile),
        in_specs=[SMEM] * 3 + [VMEM] * 21,
        out_specs=(VMEM,) * 3,
        scratch_shapes=[
            pltpu.VMEM((12 * SEP_DEV, TILE, 2 * NRHS), BF16),
            pltpu.VMEM((SEP_DEV, TILE, NRHS), F32),
        ],
        compiler_params=params(30),
        name="finish",
    )(target, seen, own, norms, solved, reduced, ya, yb, u1, w0, w1, *offs, *w2s)


def per_device(
    interior_inverse, coupling, interior_grad, separator_hessian_blocks, sep_grad, lists, owner, counts
):
    n_region = lax.axis_size("region")
    n_sub = lax.axis_size("sub")
    region = lax.axis_index("region")
    sub = lax.axis_index("sub")
    both = ("region", "sub")

    def shift(x, ahead, turn):
        pairs = [
            (r * n_sub + s, (r + ahead) % n_region * n_sub + (s + turn) % n_sub)
            for r in range(n_region)
            for s in range(n_sub)
        ]
        return lax.ppermute(x, both, pairs)

    def swap(x, partner):
        pairs = [(r * n_sub + s, partner(r) * n_sub + s) for r in range(n_region) for s in range(n_sub)]
        return lax.ppermute(x, both, pairs)

    def across(x):
        return swap(x, lambda r: (r + 1 if r % 2 else r - 1) % n_region)

    def mate(x):
        return swap(x, lambda r: r ^ 1)

    def add_over(x, steps):
        for step in steps:
            x = x + swap(x, lambda r: r ^ step)
        return x

    def around(chunks):
        return [chunks[0]] + [shift(chunks[turn], 0, turn) for turn in range(1, n_sub)]

    def spread(v, small=None, steps=((), ())):
        z1, z3, z2 = (shift(v, 0, turn) for turn in (1, 3, 2))
        if small is None:
            small = sum(x[SEP_DEV * TILE :] for x in (v, z1, z3, z2))
        pair = jnp.concatenate([z1, z3], axis=0)
        pair_across = across(pair)
        if steps[0]:
            small, z2 = lax.optimization_barrier((small, z2))
            small = add_over(small, steps[0])
        z2_across = across(z2)
        all_mate = mate(jnp.concatenate([v, z1, z3, z2], axis=0))
        if steps[1]:
            small, all_mate = lax.optimization_barrier((small, all_mate))
            small = add_over(small, steps[1])
        return [v, z1, z3, z2, across(v), pair_across, z2_across, all_mate], small

    per_region = n_sub * SUB_DEV
    here = lax.dynamic_slice_in_dim(lists, region * per_region, per_region, 0)
    behind = lax.dynamic_slice_in_dim(lists, (region - 1) % n_region * per_region, per_region, 0)
    near = jnp.concatenate([behind, here], axis=0).reshape(-1)
    live = lax.dynamic_slice_in_dim(counts, (region * n_sub + sub) * SUB_DEV, SUB_DEV, 0)
    place = jnp.stack([region, sub]).astype(jnp.int32)
    key = (place, near, owner)

    solved, reduced, *pay = eliminate(*key, live, interior_inverse, coupling, interior_grad, n_region, n_sub)
    arrived = around(pay)
    target, seen, own, later = plan(*key, n_region, n_sub)
    offs = couple(*key, live, coupling, solved, n_region, n_sub)
    arrived, offs = lax.optimization_barrier((arrived, offs))
    far = around(offs[4:])
    here, following = gather(target, later, arrived)
    got = shift(following, 1, 0)
    inv, u0 = invert(separator_hessian_blocks, sep_grad, here, got)
    u0, far = lax.optimization_barrier((u0, far))
    forwarded = shift(jnp.concatenate(far, axis=0), 1, 0)
    w0 = begin(inv, u0)
    w0s, _ = spread(w0, u0[0, :NORM_ROWS])
    offs = around(offs[:4]) + [forwarded]
    u1, w1 = apply(target, seen, inv, offs, w0s)
    w1s, norms = spread(w1, None, ((), (1, 2)))
    u2, w2 = apply(target, seen, inv, offs, w1s)
    w2s, norms = spread(w2, norms, ((4,), (8, 16)))
    ya, yb = ahead(own, solved, w0s, w1s)
    return finish(target, seen, own, norms, solved, reduced, ya, yb, u1, w0, w1, offs, w2s)


def solution(mesh):
    split3 = P(("region", "sub"), None, None)
    placed = (split3, P(("region", "sub"), None, None, None), split3, split3, split3, P(), P(), P())
    return jax.shard_map(
        per_device, mesh=mesh, in_specs=placed, out_specs=(split3, split3, split3), check_vma=False
    )
```

time: 281 us -> 193 us (0.69)
  blocking collectives: 50.5 us -> 0 us
  Pallas kernels: 80.2 us -> 49.3 us
  starting transfers between devices: 65.8 us -> 59.9 us
  waiting for transfers between devices: 70.8 us -> 76.2 us
  local copies, waits for them, and re-layouts: 7.82 us -> 5.01 us
    all_gather x1 -> x0, blocking collectives: 50.5 us -> none  [per_device(): lax.all_gather(jnp.stack([jnp.sum(norm0, 0), jnp.sum(norm1, 0)]), ('regio...]
    pallas_call x4 -> x6, Pallas kernels: 32.9 us -> 18 us  [the longest x1 8.04 us: invert(): pl.pallas_call(invert_kernel, out_shape=(jax.ShapeDtypeStruct((SEP_DEV, 2...]
    pallas_call x1, Pallas kernels: 13.7 us -> 5.19 us  [plan(): pl.pallas_call(lambda *refs: plan_kernel(n_region, n_sub, *refs), out_sha...]
    ppermute x47 -> x37, starting transfers between devices: 65.8 us -> 59.9 us  [the longest x17 32.4 us: swap(): return lax.ppermute(x, both, pairs)]
    ppermute x47 -> x37, waiting for transfers between devices: 70.8 us -> 76.2 us  [the longest x20 52.8 us: shift(): return lax.ppermute(x, both, pairs)]
    pallas_call x1, Pallas kernels: 9.31 us -> 5.24 us  [couple(): pl.pallas_call(lambda *refs: couple_kernel(n_region, n_sub, *refs), grid=...]
    pallas_call x1, Pallas kernels: 8.09 us -> 4.53 us  [finish(): pl.pallas_call(finish_kernel, out_shape=(jax.ShapeDtypeStruct((SUB_DEV, N...]
  transfers between devices with their start and end apart: 47 -> 37, of which waited for: 17 -> 21; matrix products, arithmetic and copies ran while one was open for 1% -> 0% of each run, Pallas kernels for 8% -> 11%
where the time goes in v2:
time: 193 us
  waiting for transfers between devices  76.2 us (39%)
  starting transfers between devices  59.9 us (31%)
  Pallas kernels  49.3 us (26%)
  local copies, waits for them, and re-layouts  5.01 us (3%)
    ppermute x20, waiting for transfers between devices, shift(): return lax.ppermute(x, both, pairs)  52.8 us
    ppermute x17, starting transfers between devices, swap(): return lax.ppermute(x, both, pairs)  32.4 us
    ppermute x20, starting transfers between devices, shift(): return lax.ppermute(x, both, pairs)  27.6 us
    ppermute x17, waiting for transfers between devices, swap(): return lax.ppermute(x, both, pairs)  23.5 us
    pallas_call x1, Pallas kernels, eliminate(): pl.pallas_call(lambda *refs: eliminate_kernel(n_region, n_sub, *refs), gr...  16.3 us
    pallas_call x1, Pallas kernels, invert(): pl.pallas_call(invert_kernel, out_shape=(jax.ShapeDtypeStruct((SEP_DEV, 2...  8.04 us
    pallas_call x2, Pallas kernels, apply(): pl.pallas_call(apply_kernel, out_shape=(tile, WIDE), in_specs=[SMEM] * 2...  5.52 us
    pallas_call x1, Pallas kernels, couple(): pl.pallas_call(lambda *refs: couple_kernel(n_region, n_sub, *refs), grid=...  5.24 us
  transfers between devices with their start and end apart: 37, of which 21 were waited for; matrix products, arithmetic and copies ran while one was open for 0% of the time, Pallas kernels for 11%

profile of v2, /device:TPU:0, one launch (start us, length us, event | category | flops | bytes accessed | tf_op | source)
XLA Modules:
  0.0 192.6 jit_solution(11463017558511779117)
XLA Ops:
  0.7 0.8 constant_dynamic-slice_fusion.1
  1.6 0.7 reshape.9.refs_1_
  2.3 0.6 pad_add_fusion.1.refs_0_
  2.9 1.3 dynamic_slice.11.refs_3_
  4.2 16.3 %eliminate.1 = (bf16[4,1024,512]{2,1,0:T(8,128)(2,1)}, f32[4,512,128]{2,1,0:T(8,128)}, f32[4,200,128]{2,1,0:T(8,128)}, f32[4,200,128]{2,1,0:T(8,128)}, f32[4,200,128]{2,1,0:T(8,128)}, /*index=5*/f32[4,200,128]{2,1,0:T(8,128)}) custom-call(s32[2]{0:T(128)} %pad_add_fusion.1.refs_0_, s32[128]{0:T(128)} %reshape.9.refs_1_, s32[512]{0:T(512)} %refs_2_.5, ...), custom_call_target="tpu_custom_call" | custom-call | tf_op jit(solution)/shard_map/eliminate/pallas_call | solution.py:235
  20.5 2.1 %collective-permute-start = (f32[4,200,128]{2,1,0:T(8,128)}, f32[4,200,128]{2,1,0:T(8,128)S(1)}, u32[]{:S(2)}, u32[]{:S(2)}) collective-permute-start(f32[4,200,128]{2,1,0:T(8,128)} %get-tuple-element.58), channel_id=1, source_target_pairs={{0,1},{1,2},{2,3},{3,0},{4,5},{5,6},{6,7},{7,4},{8,9},{9,10},{10,1... | collective-permute-start | bytes 1228808 | tf_op jit(solution)/shard_map/ppermute | solution.py:596
  22.6 3.6 %collective-permute-start.1 = (f32[4,200,128]{2,1,0:T(8,128)}, f32[4,200,128]{2,1,0:T(8,128)S(1)}, u32[]{:S(2)}, u32[]{:S(2)}) collective-permute-start(f32[4,200,128]{2,1,0:T(8,128)} %get-tuple-element.59), channel_id=1, source_target_pairs={{0,2},{1,3},{2,0},{3,1},{4,6},{5,7},{6,4},{7,5},{8,10},{9,11},{10,... | collective-permute-start | bytes 1228808 | tf_op jit(solution)/shard_map/ppermute | solution.py:596
  26.2 1.0 collective-permute-start.2
  27.2 2.2 %copy-done.1 = bf16[4,1024,512]{2,1,0:T(8,128)(2,1)S(1)} copy-done((bf16[4,1024,512]{2,1,0:T(8,128)(2,1)S(1)}, bf16[4,1024,512]{2,1,0:T(8,128)(2,1)}, u32[]{:S(2)}) %copy-start.1) | copy-done | bytes 4194328
  29.4 5.2 %couple.1 = (f32[2,128,384]{2,1,0:T(8,128)S(1)}, f32[2,128,384]{2,1,0:T(8,128)S(1)}, f32[2,128,384]{2,1,0:T(8,128)S(1)}, f32[2,128,384]{2,1,0:T(8,128)S(1)}, f32...) custom-call(s32[2]{0:T(128)S(1)} %copy-done.7, ...), custom_call_target="tpu_custom_call" | custom-call | flops 8000000000 | bytes 12582912 | tf_op jit(solution)/shard_map/couple/pallas_call | solution.py:303
  34.7 5.2 %plan.1 = (s32[16]{0:T(128)S(1)}, s32[48]{0:T(128)S(1)}, s32[16]{0:T(128)S(1)}, s32[8]{0:T(128)S(1)}) custom-call(s32[2]{0:T(128)S(1)} %copy-done.7, s32[128]{0:T(128)S(1)} %copy-done.5, s32[512]{0:T(512)S(1)} %copy-done.6), custom_call_target="tpu_custom_call" | custom-call | flops 2000000000 | bytes 8192 | tf_op jit(solution)/shard_map/plan/pallas_call | solution.py:146
  39.9 4.5 %collective-permute-done.1.c2 = f32[4,200,128]{2,1,0:T(8,128)S(1)} collective-permute-done((f32[4,200,128]{2,1,0:T(8,128)}, f32[4,200,128]{2,1,0:T(8,128)S(1)}, u32[]{:S(2)}, u32[]{:S(2)}) %collective-permute-start.1) | collective-permute-done | bytes 409632 | tf_op jit(solution)/shard_map/ppermute | solution.py:596
  44.4 0.8 gather.1
  45.3 1.3 collective-permute-start.7
  46.6 2.4 %collective-permute-start.8 = (f32[2,128,384]{2,1,0:T(8,128)S(1)}, f32[2,128,384]{2,1,0:T(8,128)S(1)}, u32[]{:S(2)}, u32[]{:S(2)}) collective-permute-start(f32[2,128,384]{2,1,0:T(8,128)S(1)} %get-tuple-element.84), channel_id=1, source_target_pairs={{0,2},{1,3},{2,0},{3,1},{4,6},{5,7},{6,4},{7,5},{8,10},{9,11},{10,... | collective-permute-start | bytes 1179656 | tf_op jit(solution)/shard_map/ppermute | solution.py:596
  49.0 1.3 collective-permute-start.9
  50.2 5.7 %collective-permute-done.3.got_ref = f32[4,200,128]{2,1,0:T(8,128)S(1)} collective-permute-done((f32[4,200,128]{2,1,0:T(8,128)S(1)}, f32[4,200,128]{2,1,0:T(8,128)S(1)}, u32[]{:S(2)}, u32[]{:S(2)}) %collective-permute-start.3) | collective-permute-done | bytes 409632 | tf_op jit(solution)/shard_map/ppermute | solution.py:596
  56.0 8.0 %invert.1 = (bf16[4,256,128]{2,1,0:T(8,128)(2,1)S(1)}, f32[4,128,128]{2,1,0:T(8,128)S(1)}) custom-call(f32[4,128,128]{2,1,0:T(8,128)S(1)} %copy-done.9, f32[4,128,128]{2,1,0:T(8,128)S(1)} %copy-done.10, f32[4,200,128]{2,1,0:T(8,128)S(1)} %get-tuple-element.74.here_ref, f32[4,200,128]{2,1,0:T(8,128)S(1)} %collective-permute-done.3.got_ref), custom_call_target="tpu_custom_call" | custom-call | flops 10000000000 | bytes 4194304 | tf_op jit(solution)/shard_map/invert/pallas_call | solution.py:431
  64.0 2.8 %collective-permute-done.8 = f32[2,128,384]{2,1,0:T(8,128)S(1)} collective-permute-done((f32[2,128,384]{2,1,0:T(8,128)S(1)}, f32[2,128,384]{2,1,0:T(8,128)S(1)}, u32[]{:S(2)}, u32[]{:S(2)}) %collective-permute-start.8) | collective-permute-done | bytes 393248 | tf_op jit(solution)/shard_map/ppermute | solution.py:596
  66.8 0.8 collective-permute-done.9
  67.6 0.3 begin.1.rest_5_.rest_0_.w0_ref
  67.9 2.4 %collective-permute-start.13 = (f32[520,128]{1,0:T(8,128)S(1)}, f32[520,128]{1,0:T(8,128)S(1)}, u32[]{:S(2)}, u32[]{:S(2)}) collective-permute-start(f32[520,128]{1,0:T(8,128)S(1)} %begin.1.rest_5_.rest_0_.w0_ref), channel_id=1, source_target_pairs={{0,2},{1,3},{2,0},{3,1},{4,6},{5,7},{6,4},{7,5},{8,10},{9,11},{10,... | collective-permute-start | bytes 798728 | tf_op jit(solution)/shard_map/ppermute | solution.py:596
  70.2 2.3 %collective-permute-start.12 = (f32[520,128]{1,0:T(8,128)S(1)}, f32[520,128]{1,0:T(8,128)S(1)}, u32[]{:S(2)}, u32[]{:S(2)}) collective-permute-start(f32[520,128]{1,0:T(8,128)S(1)} %begin.1.rest_5_.rest_0_.w0_ref), channel_id=1, source_target_pairs={{0,3},{1,0},{2,1},{3,2},{4,7},{5,4},{6,5},{7,6},{8,11},{9,8},{10,9... | collective-permute-start | bytes 798728 | tf_op jit(solution)/shard_map/ppermute | solution.py:596
  72.7 6.0 %collective-permute-done.13.rest_8_.rest_3_ = f32[520,128]{1,0:T(8,128)S(1)} collective-permute-done((f32[520,128]{1,0:T(8,128)S(1)}, f32[520,128]{1,0:T(8,128)S(1)}, u32[]{:S(2)}, u32[]{:S(2)}) %collective-permute-start.13) | collective-permute-done | bytes 266272 | tf_op jit(solution)/shard_map/ppermute | solution.py:596
  78.7 5.2 %collective-permute-done.12.rest_7_.rest_2_ = f32[520,128]{1,0:T(8,128)S(1)} collective-permute-done((f32[520,128]{1,0:T(8,128)S(1)}, f32[520,128]{1,0:T(8,128)S(1)}, u32[]{:S(2)}, u32[]{:S(2)}) %collective-permute-start.12) | collective-permute-done | bytes 266272 | tf_op jit(solution)/shard_map/ppermute | solution.py:596
  84.0 1.7 collective-permute-start.4
  85.7 2.5 %collective-permute-start.5 = (f32[2,128,384]{2,1,0:T(8,128)S(1)}, f32[2,128,384]{2,1,0:T(8,128)S(1)}, u32[]{:S(2)}, u32[]{:S(2)}) collective-permute-start(f32[2,128,384]{2,1,0:T(8,128)S(1)} %get-tuple-element.79), channel_id=1, source_target_pairs={{0,2},{1,3},{2,0},{3,1},{4,6},{5,7},{6,4},{7,5},{8,10},{9,11},{10,... | collective-permute-start | bytes 1179656 | tf_op jit(solution)/shard_map/ppermute | solution.py:596
  88.2 0.8 collective-permute-start.6
  89.0 7.7 %collective-permute-done.4.rest_1_ = f32[2,128,384]{2,1,0:T(8,128)S(1)} collective-permute-done((f32[2,128,384]{2,1,0:T(8,128)S(1)}, f32[2,128,384]{2,1,0:T(8,128)S(1)}, u32[]{:S(2)}, u32[]{:S(2)}) %collective-permute-start.4) | collective-permute-done | bytes 393248 | tf_op jit(solution)/shard_map/ppermute | solution.py:596
  96.8 3.3 %collective-permute-start.15 = (f32[1040,128]{1,0:T(8,128)S(1)}, f32[1040,128]{1,0:T(8,128)S(1)}, u32[]{:S(2)}, u32[]{:S(2)}) collective-permute-start(f32[1040,128]{1,0:T(8,128)S(1)} %pad_maximum_fusion.4), channel_id=1, source_target_pairs={{0,124},{1,125},{2,126},{3,127},{4,8},{5,9},{6,10},{7,11},{8,4},{9... | collective-permute-start | bytes 1597448 | tf_op jit(solution)/shard_map/ppermute | solution.py:600
  100.1 6.0 %collective-permute-done.5.rest_2_ = f32[2,128,384]{2,1,0:T(8,128)S(1)} collective-permute-done((f32[2,128,384]{2,1,0:T(8,128)S(1)}, f32[2,128,384]{2,1,0:T(8,128)S(1)}, u32[]{:S(2)}, u32[]{:S(2)}) %collective-permute-start.5) | collective-permute-done | bytes 393248 | tf_op jit(solution)/shard_map/ppermute | solution.py:596
  106.1 3.3 %collective-permute-start.14 = (f32[520,128]{1,0:T(8,128)S(1)}, f32[520,128]{1,0:T(8,128)S(1)}, u32[]{:S(2)}, u32[]{:S(2)}) collective-permute-start(f32[520,128]{1,0:T(8,128)S(1)} %begin.1.rest_5_.rest_0_.w0_ref), channel_id=1, source_target_pairs={{0,124},{1,125},{2,126},{3,127},{4,8},{5,9},{6,10},{7,11},{8,4},{9... | collective-permute-start | bytes 798728 | tf_op jit(solution)/shard_map/ppermute | solution.py:600
  109.4 1.8 collective-permute-start.16
  111.1 4.1 %collective-permute-done.14.rest_9_.rest_4_ = f32[520,128]{1,0:T(8,128)S(1)} collective-permute-done((f32[520,128]{1,0:T(8,128)S(1)}, f32[520,128]{1,0:T(8,128)S(1)}, u32[]{:S(2)}, u32[]{:S(2)}) %collective-permute-start.14) | collective-permute-done | bytes 266272 | tf_op jit(solution)/shard_map/ppermute | solution.py:600
  115.2 3.3 %collective-permute-done.16.rest_11_.rest_6_ = f32[520,128]{1,0:T(8,128)S(1)} collective-permute-done((f32[520,128]{1,0:T(8,128)S(1)}, f32[520,128]{1,0:T(8,128)S(1)}, u32[]{:S(2)}, u32[]{:S(2)}) %collective-permute-start.16) | collective-permute-done | bytes 266272 | tf_op jit(solution)/shard_map/ppermute | solution.py:600
  118.5 2.6 %apply.2 = (f32[4,128,128]{2,1,0:T(8,128)S(1)}, f32[520,128]{1,0:T(8,128)S(1)}) custom-call(s32[16]{0:T(128)S(1)} %get-tuple-element.53.target_ref, s32[48]{0:T(128)S(1)} %get-tuple-element.54.seen_ref, bf16[4,256,128]{2,1,0:T(8,128)(2,1)S(1)} %get-tuple-element.76.inv_ref, f32[2,128,384]{2,1,0:T(8,128)S(1)} %get-tuple-element.77.rest_0_, ...), custom_call_target="tpu_custom_call" | custom-call | flops 2000000000 | bytes 7340032 | tf_op jit(solution)/shard_map/apply/pallas_call | solution.py:500
  121.1 1.1 collective-permute-start.20
  122.2 2.0 %collective-permute-start.18 = (f32[520,128]{1,0:T(8,128)S(1)}, f32[520,128]{1,0:T(8,128)S(1)}, u32[]{:S(2)}, u32[]{:S(2)}) collective-permute-start(f32[520,128]{1,0:T(8,128)S(1)} %get-tuple-element.91.rest_5_.rest_8_.w1_ref), channel_id=1, source_target_pairs={{0,1},{1,2},{2,3},{3,0},{4,5},{5,6},{6,7},{7,4},{8,9},{9,10},{10,1... | collective-permute-start | bytes 798728 | tf_op jit(solution)/shard_map/ppermute | solution.py:596
  124.3 6.2 %collective-permute-done.20.rest_8_.rest_11_ = f32[520,128]{1,0:T(8,128)S(1)} collective-permute-done((f32[520,128]{1,0:T(8,128)S(1)}, f32[520,128]{1,0:T(8,128)S(1)}, u32[]{:S(2)}, u32[]{:S(2)}) %collective-permute-start.20) | collective-permute-done | bytes 266272 | tf_op jit(solution)/shard_map/ppermute | solution.py:596
  130.5 2.7 %collective-permute-done.18.rest_6_.rest_9_ = f32[520,128]{1,0:T(8,128)S(1)} collective-permute-done((f32[520,128]{1,0:T(8,128)S(1)}, f32[520,128]{1,0:T(8,128)S(1)}, u32[]{:S(2)}, u32[]{:S(2)}) %collective-permute-start.18) | collective-permute-done | bytes 266272 | tf_op jit(solution)/shard_map/ppermute | solution.py:596
  133.4 4.8 %collective-permute-start.25 = (f32[1040,128]{1,0:T(8,128)S(1)}, f32[1040,128]{1,0:T(8,128)S(1)}, u32[]{:S(2)}, u32[]{:S(2)}) collective-permute-start(f32[1040,128]{1,0:T(8,128)S(1)} %pad_maximum_fusion.5), channel_id=1, source_target_pairs={{0,124},{1,125},{2,126},{3,127},{4,8},{5,9},{6,10},{7,11},{8,4},{9... | collective-permute-start | bytes 1597448 | tf_op jit(solution)/shard_map/ppermute | solution.py:600
  138.2 0.3 collective-permute-start.24
  138.6 4.7 %collective-permute-start.26 = (f32[520,128]{1,0:T(8,128)S(1)}, f32[520,128]{1,0:T(8,128)S(1)}, u32[]{:S(2)}, u32[]{:S(2)}) collective-permute-start(f32[520,128]{1,0:T(8,128)S(1)} %collective-permute-done.20.rest_8_.rest_11_), channel_id=1, source_target_pairs={{0,124},{1,125},{2,126},{3,127},{4,8},{5,9},{6,10},{7,11},{8,4},{9... | collective-permute-start | bytes 798728 | tf_op jit(solution)/shard_map/ppermute | solution.py:600
  143.3 5.0 %collective-permute-done.24.rest_9_.rest_12_ = f32[520,128]{1,0:T(8,128)S(1)} collective-permute-done((f32[520,128]{1,0:T(8,128)S(1)}, f32[520,128]{1,0:T(8,128)S(1)}, u32[]{:S(2)}, u32[]{:S(2)}) %collective-permute-start.24) | collective-permute-done | bytes 266272 | tf_op jit(solution)/shard_map/ppermute | solution.py:600
  148.4 2.9 %collective-permute-done.26.rest_11_.rest_14_ = f32[520,128]{1,0:T(8,128)S(1)} collective-permute-done((f32[520,128]{1,0:T(8,128)S(1)}, f32[520,128]{1,0:T(8,128)S(1)}, u32[]{:S(2)}, u32[]{:S(2)}) %collective-permute-start.26) | collective-permute-done | bytes 266272 | tf_op jit(solution)/shard_map/ppermute | solution.py:600
  151.2 2.9 %apply.3 = (f32[4,128,128]{2,1,0:T(8,128)}, f32[520,128]{1,0:T(8,128)S(1)}) custom-call(s32[16]{0:T(128)S(1)} %get-tuple-element.53.target_ref, s32[48]{0:T(128)S(1)} %get-tuple-element.54.seen_ref, bf16[4,256,128]{2,1,0:T(8,128)(2,1)S(1)} %get-tuple-element.76.inv_ref, f32[2,128,384]{2,1,0:T(8,128)S(1)} %get-tuple-element.77.rest_0_, ...), custom_call_target="tpu_custom_call" | custom-call | flops 2000000000 | bytes 7340032 | tf_op jit(solution)/shard_map/apply/pallas_call | solution.py:500
  154.2 1.0 collective-permute-start.27
  155.2 1.3 collective-permute-start.30
  156.4 0.8 collective-permute-start.29
  157.2 1.2 collective-permute-done.22
  158.4 3.6 %collective-permute-done.23 = f32[8,128]{1,0:T(8,128)S(1)} collective-permute-done((f32[8,128]{1,0:T(8,128)S(1)}, f32[8,128]{1,0:T(8,128)S(1)}, u32[]{:S(2)}, u32[]{:S(2)}) %collective-permute-start.23) | collective-permute-done | bytes 4128 | tf_op jit(solution)/shard_map/ppermute | solution.py:600
  162.0 2.3 %collective-permute-done.27.rest_8_ = f32[520,128]{1,0:T(8,128)S(1)} collective-permute-done((f32[520,128]{1,0:T(8,128)S(1)}, f32[520,128]{1,0:T(8,128)S(1)}, u32[]{:S(2)}, u32[]{:S(2)}) %collective-permute-start.27) | collective-permute-done | bytes 266272 | tf_op jit(solution)/shard_map/ppermute | solution.py:596
  164.3 0.8 collective-permute-done.30.rest_7_
  165.1 2.0 %collective-permute-done.29.rest_6_ = f32[520,128]{1,0:T(8,128)S(1)} collective-permute-done((f32[520,128]{1,0:T(8,128)S(1)}, f32[520,128]{1,0:T(8,128)S(1)}, u32[]{:S(2)}, u32[]{:S(2)}) %collective-permute-start.29) | collective-permute-done | bytes 266272 | tf_op jit(solution)/shard_map/ppermute | solution.py:596
  167.3 2.8 %collective-permute-start.28 = (f32[8,128]{1,0:T(8,128)S(1)}, f32[8,128]{1,0:T(8,128)S(1)}, u32[]{:S(2)}, u32[]{:S(2)}) collective-permute-start(f32[8,128]{1,0:T(8,128)S(1)} %add.50), channel_id=1, source_target_pairs={{0,16},{1,17},{2,18},{3,19},{4,20},{5,21},{6,22},{7,23},{8,24},{9,... | collective-permute-start | bytes 12296 | tf_op jit(solution)/shard_map/ppermute | solution.py:600
  170.1 3.0 %collective-permute-start.34 = (f32[520,128]{1,0:T(8,128)S(1)}, f32[520,128]{1,0:T(8,128)S(1)}, u32[]{:S(2)}, u32[]{:S(2)}) collective-permute-start(f32[520,128]{1,0:T(8,128)S(1)} %get-tuple-element.94.rest_5_), channel_id=1, source_target_pairs={{0,124},{1,125},{2,126},{3,127},{4,8},{5,9},{6,10},{7,11},{8,4},{9... | collective-permute-start | bytes 798728 | tf_op jit(solution)/shard_map/ppermute | solution.py:600
  173.2 2.0 %collective-permute-start.36 = (f32[520,128]{1,0:T(8,128)S(1)}, f32[520,128]{1,0:T(8,128)S(1)}, u32[]{:S(2)}, u32[]{:S(2)}) collective-permute-start(f32[520,128]{1,0:T(8,128)S(1)} %collective-permute-done.27.rest_8_), channel_id=1, source_target_pairs={{0,124},{1,125},{2,126},{3,127},{4,8},{5,9},{6,10},{7,11},{8,4},{9... | collective-permute-start | bytes 798728 | tf_op jit(solution)/shard_map/ppermute | solution.py:600
  175.2 0.4 collective-permute-start.32
  175.6 2.9 %collective-permute-start.35 = (f32[1040,128]{1,0:T(8,128)S(1)}, f32[1040,128]{1,0:T(8,128)S(1)}, u32[]{:S(2)}, u32[]{:S(2)}) collective-permute-start(f32[1040,128]{1,0:T(8,128)S(1)} %pad_maximum_fusion.6), channel_id=1, source_target_pairs={{0,124},{1,125},{2,126},{3,127},{4,8},{5,9},{6,10},{7,11},{8,4},{9... | collective-permute-start | bytes 1597448 | tf_op jit(solution)/shard_map/ppermute | solution.py:600
  178.5 1.6 collective-permute-done.32
  180.1 2.8 %collective-permute-start.33 = (f32[8,128]{1,0:T(8,128)S(1)}, f32[8,128]{1,0:T(8,128)S(1)}, u32[]{:S(2)}, u32[]{:S(2)}) collective-permute-start(f32[8,128]{1,0:T(8,128)S(1)} %add.52), channel_id=1, source_target_pairs={{0,64},{1,65},{2,66},{3,67},{4,68},{5,69},{6,70},{7,71},{8,72},{9,... | collective-permute-start | bytes 12296 | tf_op jit(solution)/shard_map/ppermute | solution.py:600
  182.8 3.4 %ahead.1 = (f32[4,512,128]{2,1,0:T(8,128)S(1)}, f32[4,512,128]{2,1,0:T(8,128)S(1)}) custom-call(s32[16]{0:T(128)S(1)} %get-tuple-element.55.own_ref, bf16[4,1024,512]{2,1,0:T(8,128)(2,1)S(1)} %copy-done.2, f32[520,128]{1,0:T(8,128)S(1)} %begin.1.rest_5_.rest_0_.w0_ref, f32[520,128]{1,0:T(8,128)S(1)} %collective-permute-done.11.rest_6_.rest_1_, ...), custom_call_target="tpu_custom_call" | custom-call | flops 8000000000 | bytes 14680064 | tf_op jit(solution)/shard_map/ahead/pallas_call | solution.py:530
  186.3 1.8 collective-permute-done.35.rest_10_
  188.1 4.5 %finish.1 = (f32[4,512,128]{2,1,0:T(8,128)}, f32[4,128,128]{2,1,0:T(8,128)}, f32[4,128,128]{2,1,0:T(8,128)}) custom-call(s32[16]{0:T(128)S(1)} %get-tuple-element.53.target_ref, s32[48]{0:T(128)S(1)} %get-tuple-element.54.seen_ref, s32[16]{0:T(128)S(1)} %get-tuple-element.55.own_ref, f32[8,128]{1,0:T(8,128)S(1)} %add.53.norm_ref, ...), custom_call_target="tpu_custom_call" | custom-call | tf_op jit(solution)/shard_map/finish/pallas_call | solution.py:567
  (61 shorter events, 1.1 us)
Async XLA Ops:
  4.2 23.0 %copy-start = (f32[4,4,512,128]{3,2,1,0:T(8,128)S(1)}, f32[4,4,512,128]{3,2,1,0:T(8,128)}, u32[]{:S(2)}) copy-start(f32[4,4,512,128]{3,2,1,0:T(8,128)} %refs_4_.3) | copy-start | bytes 12582916
  4.2 23.0 %copy-start.5 = (s32[128]{0:T(128)S(1)}, s32[128]{0:T(128)}, u32[]{:S(2)}) copy-start(s32[128]{0:T(128)} %reshape.9.refs_1_) | copy-start | bytes 1540
  4.2 23.0 %copy-start.6 = (s32[512]{0:T(512)S(1)}, s32[512]{0:T(512)}, u32[]{:S(2)}) copy-start(s32[512]{0:T(512)} %refs_2_.5) | copy-start | bytes 6148
  4.2 23.0 %copy-start.7 = (s32[2]{0:T(128)S(1)}, s32[2]{0:T(128)}, u32[]{:S(2)}) copy-start(s32[2]{0:T(128)} %pad_add_fusion.1.refs_0_) | copy-start | bytes 28
  4.2 23.0 %copy-start.8 = (s32[4]{0:T(128)S(1)}, s32[4]{0:T(128)}, u32[]{:S(2)}) copy-start(s32[4]{0:T(128)} %dynamic_slice.11.refs_3_) | copy-start | bytes 52
  20.5 19.3 %collective-permute-start = (f32[4,200,128]{2,1,0:T(8,128)}, f32[4,200,128]{2,1,0:T(8,128)S(1)}, u32[]{:S(2)}, u32[]{:S(2)}) collective-permute-start(f32[4,200,128]{2,1,0:T(8,128)} %get-tuple-element.58), channel_id=1, source_target_pairs={{0,1},{1,2},{2,3},{3,0},{4,5},{5,6},{6,7},{7,4},{8,9},{9,10},{10,1... | collective-permute-start | bytes 1228808 | tf_op jit(solution)/shard_map/ppermute | solution.py:596
  22.6 21.8 %collective-permute-start.1 = (f32[4,200,128]{2,1,0:T(8,128)}, f32[4,200,128]{2,1,0:T(8,128)S(1)}, u32[]{:S(2)}, u32[]{:S(2)}) collective-permute-start(f32[4,200,128]{2,1,0:T(8,128)} %get-tuple-element.59), channel_id=1, source_target_pairs={{0,2},{1,3},{2,0},{3,1},{4,6},{5,7},{6,4},{7,5},{8,10},{9,11},{10,... | collective-permute-start | bytes 1228808 | tf_op jit(solution)/shard_map/ppermute | solution.py:596
  26.2 18.2 %collective-permute-start.2 = (f32[4,200,128]{2,1,0:T(8,128)}, f32[4,200,128]{2,1,0:T(8,128)S(1)}, u32[]{:S(2)}, u32[]{:S(2)}) collective-permute-start(f32[4,200,128]{2,1,0:T(8,128)} %get-tuple-element.60), channel_id=1, source_target_pairs={{0,3},{1,0},{2,1},{3,2},{4,7},{5,4},{6,5},{7,6},{8,11},{9,8},{10,9... | collective-permute-start | bytes 1228808 | tf_op jit(solution)/shard_map/ppermute | solution.py:596
  27.2 2.2 %copy-start.1 = (bf16[4,1024,512]{2,1,0:T(8,128)(2,1)S(1)}, bf16[4,1024,512]{2,1,0:T(8,128)(2,1)}, u32[]{:S(2)}) copy-start(bf16[4,1024,512]{2,1,0:T(8,128)(2,1)} %get-tuple-element.61.refs_5_.solved_ref) | copy-start | bytes 12582916
  34.7 9.8 %copy-start.4 = (f32[4,200,128]{2,1,0:T(8,128)S(1)}, f32[4,200,128]{2,1,0:T(8,128)}, u32[]{:S(2)}) copy-start(f32[4,200,128]{2,1,0:T(8,128)} %get-tuple-element.70.c0) | copy-start | bytes 1228804
  39.9 16.1 %copy-start.9 = (f32[4,128,128]{2,1,0:T(8,128)S(1)}, f32[4,128,128]{2,1,0:T(8,128)}, u32[]{:S(2)}) copy-start(f32[4,128,128]{2,1,0:T(8,128)} %hess_ref.1) | copy-start | bytes 786436
  39.9 16.1 %copy-start.10 = (f32[4,128,128]{2,1,0:T(8,128)S(1)}, f32[4,128,128]{2,1,0:T(8,128)}, u32[]{:S(2)}) copy-start(f32[4,128,128]{2,1,0:T(8,128)} %grad_ref.1) | copy-start | bytes 786436
  45.2 10.8 %collective-permute-start.3 = (f32[4,200,128]{2,1,0:T(8,128)S(1)}, f32[4,200,128]{2,1,0:T(8,128)S(1)}, u32[]{:S(2)}, u32[]{:S(2)}) collective-permute-start(f32[4,200,128]{2,1,0:T(8,128)S(1)} %get-tuple-element.75), channel_id=1, source_target_pairs={{0,4},{1,5},{2,6},{3,7},{4,8},{5,9},{6,10},{7,11},{8,12},{9,13},{1... | collective-permute-start | bytes 1228808 | tf_op jit(solution)/shard_map/ppermute | solution.py:596
  45.3 18.7 %collective-permute-start.7 = (f32[2,128,384]{2,1,0:T(8,128)S(1)}, f32[2,128,384]{2,1,0:T(8,128)S(1)}, u32[]{:S(2)}, u32[]{:S(2)}) collective-permute-start(f32[2,128,384]{2,1,0:T(8,128)S(1)} %get-tuple-element.83), channel_id=1, source_target_pairs={{0,1},{1,2},{2,3},{3,0},{4,5},{5,6},{6,7},{7,4},{8,9},{9,10},{10,1... | collective-permute-start | bytes 1179656 | tf_op jit(solution)/shard_map/ppermute | solution.py:596
  46.6 20.2 %collective-permute-start.8 = (f32[2,128,384]{2,1,0:T(8,128)S(1)}, f32[2,128,384]{2,1,0:T(8,128)S(1)}, u32[]{:S(2)}, u32[]{:S(2)}) collective-permute-start(f32[2,128,384]{2,1,0:T(8,128)S(1)} %get-tuple-element.84), channel_id=1, source_target_pairs={{0,2},{1,3},{2,0},{3,1},{4,6},{5,7},{6,4},{7,5},{8,10},{9,11},{10,... | collective-permute-start | bytes 1179656 | tf_op jit(solution)/shard_map/ppermute | solution.py:596
  49.0 18.6 %collective-permute-start.9 = (f32[2,128,384]{2,1,0:T(8,128)S(1)}, f32[2,128,384]{2,1,0:T(8,128)S(1)}, u32[]{:S(2)}, u32[]{:S(2)}) collective-permute-start(f32[2,128,384]{2,1,0:T(8,128)S(1)} %get-tuple-element.85), channel_id=1, source_target_pairs={{0,3},{1,0},{2,1},{3,2},{4,7},{5,4},{6,5},{7,6},{8,11},{9,8},{10,9... | collective-permute-start | bytes 1179656 | tf_op jit(solution)/shard_map/ppermute | solution.py:596
  67.9 10.8 %collective-permute-start.13 = (f32[520,128]{1,0:T(8,128)S(1)}, f32[520,128]{1,0:T(8,128)S(1)}, u32[]{:S(2)}, u32[]{:S(2)}) collective-permute-start(f32[520,128]{1,0:T(8,128)S(1)} %begin.1.rest_5_.rest_0_.w0_ref), channel_id=1, source_target_pairs={{0,2},{1,3},{2,0},{3,1},{4,6},{5,7},{6,4},{7,5},{8,10},{9,11},{10,... | collective-permute-start | bytes 798728 | tf_op jit(solution)/shard_map/ppermute | solution.py:596
  70.2 13.6 %collective-permute-start.12 = (f32[520,128]{1,0:T(8,128)S(1)}, f32[520,128]{1,0:T(8,128)S(1)}, u32[]{:S(2)}, u32[]{:S(2)}) collective-permute-start(f32[520,128]{1,0:T(8,128)S(1)} %begin.1.rest_5_.rest_0_.w0_ref), channel_id=1, source_target_pairs={{0,3},{1,0},{2,1},{3,2},{4,7},{5,4},{6,5},{7,6},{8,11},{9,8},{10,9... | collective-permute-start | bytes 798728 | tf_op jit(solution)/shard_map/ppermute | solution.py:596
  72.5 11.3 %collective-permute-start.11 = (f32[520,128]{1,0:T(8,128)S(1)}, f32[520,128]{1,0:T(8,128)S(1)}, u32[]{:S(2)}, u32[]{:S(2)}) collective-permute-start(f32[520,128]{1,0:T(8,128)S(1)} %begin.1.rest_5_.rest_0_.w0_ref), channel_id=1, source_target_pairs={{0,1},{1,2},{2,3},{3,0},{4,5},{5,6},{6,7},{7,4},{8,9},{9,10},{10,1... | collective-permute-start | bytes 798728 | tf_op jit(solution)/shard_map/ppermute | solution.py:596
  72.6 45.9 %collective-permute-start.10 = (f32[8,128,384]{2,1,0:T(8,128)S(1)}, f32[8,128,384]{2,1,0:T(8,128)S(1)}, u32[]{:S(2)}, u32[]{:S(2)}) collective-permute-start(f32[8,128,384]{2,1,0:T(8,128)S(1)} %pad_maximum_fusion), channel_id=1, source_target_pairs={{0,4},{1,5},{2,6},{3,7},{4,8},{5,9},{6,10},{7,11},{8,12},{9,13},{1... | collective-permute-start | bytes 4718600 | tf_op jit(solution)/shard_map/ppermute | solution.py:596
  84.0 34.6 %collective-permute-start.17 = (f32[2080,128]{1,0:T(8,128)S(1)}, f32[2080,128]{1,0:T(8,128)S(1)}, u32[]{:S(2)}, u32[]{:S(2)}) collective-permute-start(f32[2080,128]{1,0:T(8,128)S(1)} %pad_maximum_fusion.1), channel_id=1, source_target_pairs={{0,4},{1,5},{2,6},{3,7},{4,0},{5,1},{6,2},{7,3},{8,12},{9,13},{10,... | collective-permute-start | bytes 3194888 | tf_op jit(solution)/shard_map/ppermute | solution.py:600
  84.0 12.7 %collective-permute-start.4 = (f32[2,128,384]{2,1,0:T(8,128)S(1)}, f32[2,128,384]{2,1,0:T(8,128)S(1)}, u32[]{:S(2)}, u32[]{:S(2)}) collective-permute-start(f32[2,128,384]{2,1,0:T(8,128)S(1)} %get-tuple-element.78), channel_id=1, source_target_pairs={{0,1},{1,2},{2,3},{3,0},{4,5},{5,6},{6,7},{7,4},{8,9},{9,10},{10,1... | collective-permute-start | bytes 1179656 | tf_op jit(solution)/shard_map/ppermute | solution.py:596
  85.7 20.4 %collective-permute-start.5 = (f32[2,128,384]{2,1,0:T(8,128)S(1)}, f32[2,128,384]{2,1,0:T(8,128)S(1)}, u32[]{:S(2)}, u32[]{:S(2)}) collective-permute-start(f32[2,128,384]{2,1,0:T(8,128)S(1)} %get-tuple-element.79), channel_id=1, source_target_pairs={{0,2},{1,3},{2,0},{3,1},{4,6},{5,7},{6,4},{7,5},{8,10},{9,11},{10,... | collective-permute-start | bytes 1179656 | tf_op jit(solution)/shard_map/ppermute | solution.py:596
  88.2 21.2 %collective-permute-start.6 = (f32[2,128,384]{2,1,0:T(8,128)S(1)}, f32[2,128,384]{2,1,0:T(8,128)S(1)}, u32[]{:S(2)}, u32[]{:S(2)}) collective-permute-start(f32[2,128,384]{2,1,0:T(8,128)S(1)} %get-tuple-element.80), channel_id=1, source_target_pairs={{0,3},{1,0},{2,1},{3,2},{4,7},{5,4},{6,5},{7,6},{8,11},{9,8},{10,9... | collective-permute-start | bytes 1179656 | tf_op jit(solution)/shard_map/ppermute | solution.py:596
  96.8 21.7 %collective-permute-start.15 = (f32[1040,128]{1,0:T(8,128)S(1)}, f32[1040,128]{1,0:T(8,128)S(1)}, u32[]{:S(2)}, u32[]{:S(2)}) collective-permute-start(f32[1040,128]{1,0:T(8,128)S(1)} %pad_maximum_fusion.4), channel_id=1, source_target_pairs={{0,124},{1,125},{2,126},{3,127},{4,8},{5,9},{6,10},{7,11},{8,4},{9... | collective-permute-start | bytes 1597448 | tf_op jit(solution)/shard_map/ppermute | solution.py:600
  106.1 9.2 %collective-permute-start.14 = (f32[520,128]{1,0:T(8,128)S(1)}, f32[520,128]{1,0:T(8,128)S(1)}, u32[]{:S(2)}, u32[]{:S(2)}) collective-permute-start(f32[520,128]{1,0:T(8,128)S(1)} %begin.1.rest_5_.rest_0_.w0_ref), channel_id=1, source_target_pairs={{0,124},{1,125},{2,126},{3,127},{4,8},{5,9},{6,10},{7,11},{8,4},{9... | collective-permute-start | bytes 798728 | tf_op jit(solution)/shard_map/ppermute | solution.py:600
  109.4 9.2 %collective-permute-start.16 = (f32[520,128]{1,0:T(8,128)S(1)}, f32[520,128]{1,0:T(8,128)S(1)}, u32[]{:S(2)}, u32[]{:S(2)}) collective-permute-start(f32[520,128]{1,0:T(8,128)S(1)} %collective-permute-done.13.rest_8_.rest_3_), channel_id=1, source_target_pairs={{0,124},{1,125},{2,126},{3,127},{4,8},{5,9},{6,10},{7,11},{8,4},{9... | collective-permute-start | bytes 798728 | tf_op jit(solution)/shard_map/ppermute | solution.py:600
  121.1 9.4 %collective-permute-start.20 = (f32[520,128]{1,0:T(8,128)S(1)}, f32[520,128]{1,0:T(8,128)S(1)}, u32[]{:S(2)}, u32[]{:S(2)}) collective-permute-start(f32[520,128]{1,0:T(8,128)S(1)} %get-tuple-element.91.rest_5_.rest_8_.w1_ref), channel_id=1, source_target_pairs={{0,2},{1,3},{2,0},{3,1},{4,6},{5,7},{6,4},{7,5},{8,10},{9,11},{10,... | collective-permute-start | bytes 798728 | tf_op jit(solution)/shard_map/ppermute | solution.py:596
  122.2 8.3 %collective-permute-start.19 = (f32[520,128]{1,0:T(8,128)S(1)}, f32[520,128]{1,0:T(8,128)S(1)}, u32[]{:S(2)}, u32[]{:S(2)}) collective-permute-start(f32[520,128]{1,0:T(8,128)S(1)} %get-tuple-element.91.rest_5_.rest_8_.w1_ref), channel_id=1, source_target_pairs={{0,3},{1,0},{2,1},{3,2},{4,7},{5,4},{6,5},{7,6},{8,11},{9,8},{10,9... | collective-permute-start | bytes 798728 | tf_op jit(solution)/shard_map/ppermute | solution.py:596
  122.2 11.0 %collective-permute-start.18 = (f32[520,128]{1,0:T(8,128)S(1)}, f32[520,128]{1,0:T(8,128)S(1)}, u32[]{:S(2)}, u32[]{:S(2)}) collective-permute-start(f32[520,128]{1,0:T(8,128)S(1)} %get-tuple-element.91.rest_5_.rest_8_.w1_ref), channel_id=1, source_target_pairs={{0,1},{1,2},{2,3},{3,0},{4,5},{5,6},{6,7},{7,4},{8,9},{9,10},{10,1... | collective-permute-start | bytes 798728 | tf_op jit(solution)/shard_map/ppermute | solution.py:596
  133.3 10.0 %collective-permute-start.21 = (f32[2080,128]{1,0:T(8,128)S(1)}, f32[2080,128]{1,0:T(8,128)S(1)}, u32[]{:S(2)}, u32[]{:S(2)}) collective-permute-start(f32[2080,128]{1,0:T(8,128)S(1)} %pad_maximum_fusion.2), channel_id=1, source_target_pairs={{0,4},{1,5},{2,6},{3,7},{4,0},{5,1},{6,2},{7,3},{8,12},{9,13},{10,... | collective-permute-start | bytes 3194888 | tf_op jit(solution)/shard_map/ppermute | solution.py:600
  133.4 17.8 %collective-permute-start.25 = (f32[1040,128]{1,0:T(8,128)S(1)}, f32[1040,128]{1,0:T(8,128)S(1)}, u32[]{:S(2)}, u32[]{:S(2)}) collective-permute-start(f32[1040,128]{1,0:T(8,128)S(1)} %pad_maximum_fusion.5), channel_id=1, source_target_pairs={{0,124},{1,125},{2,126},{3,127},{4,8},{5,9},{6,10},{7,11},{8,4},{9... | collective-permute-start | bytes 1597448 | tf_op jit(solution)/shard_map/ppermute | solution.py:600
  138.2 10.1 %collective-permute-start.24 = (f32[520,128]{1,0:T(8,128)S(1)}, f32[520,128]{1,0:T(8,128)S(1)}, u32[]{:S(2)}, u32[]{:S(2)}) collective-permute-start(f32[520,128]{1,0:T(8,128)S(1)} %get-tuple-element.91.rest_5_.rest_8_.w1_ref), channel_id=1, source_target_pairs={{0,124},{1,125},{2,126},{3,127},{4,8},{5,9},{6,10},{7,11},{8,4},{9... | collective-permute-start | bytes 798728 | tf_op jit(solution)/shard_map/ppermute | solution.py:600
  138.6 12.7 %collective-permute-start.26 = (f32[520,128]{1,0:T(8,128)S(1)}, f32[520,128]{1,0:T(8,128)S(1)}, u32[]{:S(2)}, u32[]{:S(2)}) collective-permute-start(f32[520,128]{1,0:T(8,128)S(1)} %collective-permute-done.20.rest_8_.rest_11_), channel_id=1, source_target_pairs={{0,124},{1,125},{2,126},{3,127},{4,8},{5,9},{6,10},{7,11},{8,4},{9... | collective-permute-start | bytes 798728 | tf_op jit(solution)/shard_map/ppermute | solution.py:600
  151.2 31.6 %copy-start.2 = (bf16[4,1024,512]{2,1,0:T(8,128)(2,1)S(1)}, bf16[4,1024,512]{2,1,0:T(8,128)(2,1)}, u32[]{:S(2)}) copy-start(bf16[4,1024,512]{2,1,0:T(8,128)(2,1)} %get-tuple-element.61.refs_5_.solved_ref) | copy-start | bytes 12582916
  154.2 10.2 %collective-permute-start.27 = (f32[520,128]{1,0:T(8,128)S(1)}, f32[520,128]{1,0:T(8,128)S(1)}, u32[]{:S(2)}, u32[]{:S(2)}) collective-permute-start(f32[520,128]{1,0:T(8,128)S(1)} %get-tuple-element.94.rest_5_), channel_id=1, source_target_pairs={{0,2},{1,3},{2,0},{3,1},{4,6},{5,7},{6,4},{7,5},{8,10},{9,11},{10,... | collective-permute-start | bytes 798728 | tf_op jit(solution)/shard_map/ppermute | solution.py:596
  155.2 10.0 %collective-permute-start.30 = (f32[520,128]{1,0:T(8,128)S(1)}, f32[520,128]{1,0:T(8,128)S(1)}, u32[]{:S(2)}, u32[]{:S(2)}) collective-permute-start(f32[520,128]{1,0:T(8,128)S(1)} %get-tuple-element.94.rest_5_), channel_id=1, source_target_pairs={{0,3},{1,0},{2,1},{3,2},{4,7},{5,4},{6,5},{7,6},{8,11},{9,8},{10,9... | collective-permute-start | bytes 798728 | tf_op jit(solution)/shard_map/ppermute | solution.py:596
  156.4 10.7 %collective-permute-start.29 = (f32[520,128]{1,0:T(8,128)S(1)}, f32[520,128]{1,0:T(8,128)S(1)}, u32[]{:S(2)}, u32[]{:S(2)}) collective-permute-start(f32[520,128]{1,0:T(8,128)S(1)} %get-tuple-element.94.rest_5_), channel_id=1, source_target_pairs={{0,1},{1,2},{2,3},{3,0},{4,5},{5,6},{6,7},{7,4},{8,9},{9,10},{10,1... | collective-permute-start | bytes 798728 | tf_op jit(solution)/shard_map/ppermute | solution.py:596
  157.2 1.2 collective-permute-start.22
  158.4 3.6 %collective-permute-start.23 = (f32[8,128]{1,0:T(8,128)S(1)}, f32[8,128]{1,0:T(8,128)S(1)}, u32[]{:S(2)}, u32[]{:S(2)}) collective-permute-start(f32[8,128]{1,0:T(8,128)S(1)} %add.49), channel_id=1, source_target_pairs={{0,8},{1,9},{2,10},{3,11},{4,12},{5,13},{6,14},{7,15},{8,0},{9,1},... | collective-permute-start | bytes 12296 | tf_op jit(solution)/shard_map/ppermute | solution.py:600
  167.2 8.0 %collective-permute-start.31 = (f32[2080,128]{1,0:T(8,128)S(1)}, f32[2080,128]{1,0:T(8,128)S(1)}, u32[]{:S(2)}, u32[]{:S(2)}) collective-permute-start(f32[2080,128]{1,0:T(8,128)S(1)} %pad_maximum_fusion.3), channel_id=1, source_target_pairs={{0,4},{1,5},{2,6},{3,7},{4,0},{5,1},{6,2},{7,3},{8,12},{9,13},{10,... | collective-permute-start | bytes 3194888 | tf_op jit(solution)/shard_map/ppermute | solution.py:600
  167.3 7.9 %collective-permute-start.28 = (f32[8,128]{1,0:T(8,128)S(1)}, f32[8,128]{1,0:T(8,128)S(1)}, u32[]{:S(2)}, u32[]{:S(2)}) collective-permute-start(f32[8,128]{1,0:T(8,128)S(1)} %add.50), channel_id=1, source_target_pairs={{0,16},{1,17},{2,18},{3,19},{4,20},{5,21},{6,22},{7,23},{8,24},{9,... | collective-permute-start | bytes 12296 | tf_op jit(solution)/shard_map/ppermute | solution.py:600
  170.1 16.2 %collective-permute-start.34 = (f32[520,128]{1,0:T(8,128)S(1)}, f32[520,128]{1,0:T(8,128)S(1)}, u32[]{:S(2)}, u32[]{:S(2)}) collective-permute-start(f32[520,128]{1,0:T(8,128)S(1)} %get-tuple-element.94.rest_5_), channel_id=1, source_target_pairs={{0,124},{1,125},{2,126},{3,127},{4,8},{5,9},{6,10},{7,11},{8,4},{9... | collective-permute-start | bytes 798728 | tf_op jit(solution)/shard_map/ppermute | solution.py:600
  173.2 13.1 %collective-permute-start.36 = (f32[520,128]{1,0:T(8,128)S(1)}, f32[520,128]{1,0:T(8,128)S(1)}, u32[]{:S(2)}, u32[]{:S(2)}) collective-permute-start(f32[520,128]{1,0:T(8,128)S(1)} %collective-permute-done.27.rest_8_), channel_id=1, source_target_pairs={{0,124},{1,125},{2,126},{3,127},{4,8},{5,9},{6,10},{7,11},{8,4},{9... | collective-permute-start | bytes 798728 | tf_op jit(solution)/shard_map/ppermute | solution.py:600
  175.2 4.9 %collective-permute-start.32 = (f32[8,128]{1,0:T(8,128)S(1)}, f32[8,128]{1,0:T(8,128)S(1)}, u32[]{:S(2)}, u32[]{:S(2)}) collective-permute-start(f32[8,128]{1,0:T(8,128)S(1)} %add.51), channel_id=1, source_target_pairs={{0,32},{1,33},{2,34},{3,35},{4,36},{5,37},{6,38},{7,39},{8,40},{9,... | collective-permute-start | bytes 12296 | tf_op jit(solution)/shard_map/ppermute | solution.py:600
  175.6 12.5 %collective-permute-start.35 = (f32[1040,128]{1,0:T(8,128)S(1)}, f32[1040,128]{1,0:T(8,128)S(1)}, u32[]{:S(2)}, u32[]{:S(2)}) collective-permute-start(f32[1040,128]{1,0:T(8,128)S(1)} %pad_maximum_fusion.6), channel_id=1, source_target_pairs={{0,124},{1,125},{2,126},{3,127},{4,8},{5,9},{6,10},{7,11},{8,4},{9... | collective-permute-start | bytes 1597448 | tf_op jit(solution)/shard_map/ppermute | solution.py:600
  180.1 6.2 %collective-permute-start.33 = (f32[8,128]{1,0:T(8,128)S(1)}, f32[8,128]{1,0:T(8,128)S(1)}, u32[]{:S(2)}, u32[]{:S(2)}) collective-permute-start(f32[8,128]{1,0:T(8,128)S(1)} %add.52), channel_id=1, source_target_pairs={{0,64},{1,65},{2,66},{3,67},{4,68},{5,69},{6,70},{7,71},{8,72},{9,... | collective-permute-start | bytes 12296 | tf_op jit(solution)/shard_map/ppermute | solution.py:600
  182.8 5.3 %copy-start.3 = (f32[4,512,128]{2,1,0:T(8,128)S(1)}, f32[4,512,128]{2,1,0:T(8,128)}, u32[]{:S(2)}) copy-start(f32[4,512,128]{2,1,0:T(8,128)} %get-tuple-element.98.reduced_ref) | copy-start | bytes 3145732

commit v3 on v2

--- a/solution.py
+++ b/solution.py
@@ -70,8 +70,8 @@
     return n.bit_length() - 1
 
 
-def send_slots(place_ref, list_ref, owner_ref, slot_ref, count_ref, n_region, n_sub):
-    region, sub = place_ref[0], place_ref[1]
+def send_slots(list_ref, owner_ref, slot_ref, count_ref, n_region, n_sub):
+    region, sub = lax.axis_index("region"), lax.axis_index("sub")
     begin = (n_sub + sub) * PER_DEV
     for c in range(2 * n_sub):
         count_ref[c] = 0
@@ -89,8 +89,8 @@
     lax.fori_loop(0, PER_DEV, step, 0)
 
 
-def plan_kernel(n_region, n_sub, place_ref, list_ref, owner_ref, target_ref, seen_ref, own_ref, next_ref):
-    region, sub = place_ref[0], place_ref[1]
+def plan_kernel(n_region, n_sub, list_ref, owner_ref, target_ref, seen_ref, own_ref, next_ref):
+    region, sub = lax.axis_index("region"), lax.axis_index("sub")
     me = region * n_sub + sub
     after = ((region + 1) & (n_region - 1)) * n_sub + sub
 
@@ -141,17 +141,17 @@
     lax.fori_loop(0, PER_DEV, mine, 0)
 
 
-def plan(place, near, owner, n_region, n_sub):
+def plan(near, owner, n_region, n_sub):
     shapes = (PER_DEV, PER_DEV * (SLOTS - 1), PER_DEV, 2 * n_sub)
     return pl.pallas_call(
         lambda *refs: plan_kernel(n_region, n_sub, *refs),
         out_shape=tuple(jax.ShapeDtypeStruct((n,), jnp.int32) for n in shapes),
-        in_specs=[SMEM] * 3,
+        in_specs=[SMEM] * 2,
         out_specs=(SMEM,) * 4,
         compiler_params=params(2),
         cost_estimate=pl.CostEstimate(flops=2 * 10**9, bytes_accessed=8192, transcendentals=0),
         name="plan",
-    )(place, near, owner)
+    )(near, owner)
 
 
 def pack_symmetric(t):
@@ -176,18 +176,18 @@
 
 
 def eliminate_kernel(
-    n_region, n_sub, place_ref, list_ref, owner_ref, live_ref, inverse_ref, coupling_ref, grad_ref,
+    n_region, n_sub, list_ref, owner_ref, live_ref, inverse_ref, coupling_ref, grad_ref,
     solved_ref, reduced_ref, *rest
 ):
-    chunks, (pay_ref, left_ref, right_ref, turned_ref, pair_ref, slot_ref, count_ref) = rest[:4], rest[4:]
+    chunks, (pay_ref, left_ref, right_ref, turned_ref, slot_ref, count_ref) = rest[:4], rest[4:]
     i = pl.program_id(0)
     span = SLOTS * TILE
 
     @pl.when(i == 0)
     def _():
-        send_slots(place_ref, list_ref, owner_ref, slot_ref, count_ref, n_region, n_sub)
-
-    live = live_ref[i]
+        send_slots(list_ref, owner_ref, slot_ref, count_ref, n_region, n_sub)
+
+    live = live_ref[(lax.axis_index("region") * n_sub + lax.axis_index("sub")) * SUB_DEV + i]
     ah, al = halves(inverse_ref[0])
     left_ref[:, :NI] = ah
     left_ref[:, NI : 2 * NI] = al
@@ -206,20 +206,17 @@
     both = product(left_ref[...], right_ref[...])
     reduced = both[:, span:]
     reduced_ref[0] = reduced
-    rh, rl = halves(reduced)
-    pair_ref[:, TILE : 2 * TILE] = rh
-    pair_ref[:, 3 * TILE :] = rl
+    pushed = product(turned_ref[...], pair_halves(reduced))
     for j in range(SLOTS):
         cols = slice(j * TILE, (j + 1) * TILE)
         sh, sl = halves(both[:, cols])
         solved_ref[0, :NI, cols] = sh
         solved_ref[0, NI:, cols] = sl
-        pair_ref[:, :TILE] = sh
-        pair_ref[:, 2 * TILE : 3 * TILE] = sl
-        result = dot4(turned_ref[2 * j * TILE : (2 * j + 2) * TILE], pair_ref[...])
         slot = slot_ref[i * SLOTS + j]
-        pay_ref[slot, :PACKED] = pack_symmetric(result[:, :TILE])
-        pay_ref[slot, PACKED:] = result[:, TILE:]
+        diagonal = dot4(turned_ref[2 * j * TILE : (2 * j + 2) * TILE], jnp.concatenate([sh, sl], axis=1))
+        pay_ref[slot, :PACKED] = pack_symmetric(diagonal)
+        part = pushed[2 * j * TILE : (2 * j + 2) * TILE]
+        pay_ref[slot, PACKED:] = (part[TILE:, NRHS:] + (part[TILE:, :NRHS] + part[:TILE, NRHS:])) + part[:TILE, :NRHS]
 
     @pl.when(i == SUB_DEV - 1)
     def _():
@@ -228,7 +225,7 @@
             chunks[c][2:] = pay_ref[8 + 2 * c : 10 + 2 * c]
 
 
-def eliminate(place, near, owner, live, interior_inverse, coupling, interior_grad, n_region, n_sub):
+def eliminate(near, owner, live, interior_inverse, coupling, interior_grad, n_region, n_sub):
     span = SLOTS * TILE
     tall = PACKED + TILE
     step = lambda i: (i, 0, 0)
@@ -240,7 +237,7 @@
             jax.ShapeDtypeStruct((SUB_DEV, NI, NRHS), F32),
         )
         + (jax.ShapeDtypeStruct((4, tall, TILE), F32),) * 4,
-        in_specs=[SMEM] * 4
+        in_specs=[SMEM] * 3
         + [
             pl.BlockSpec((1, NI, NI), step),
             pl.BlockSpec((1, SLOTS, NI, TILE), lambda i: (i, 0, 0, 0)),
@@ -253,26 +250,25 @@
             pltpu.VMEM((NI, 3 * NI), BF16),
             pltpu.VMEM((3 * NI, span + NRHS), BF16),
             pltpu.VMEM((2 * span, NI), BF16),
-            pltpu.VMEM((NI, 2 * (TILE + NRHS)), BF16),
             pltpu.SMEM((PER_DEV,), jnp.int32),
             pltpu.SMEM((2 * n_sub,), jnp.int32),
         ],
         compiler_params=params(56),
         name="eliminate",
-    )(place, near, owner, live, interior_inverse, coupling, interior_grad)
+    )(near, owner, live, interior_inverse, coupling, interior_grad)
 
 
 def couple_kernel(
-    n_region, n_sub, place_ref, list_ref, owner_ref, live_ref, coupling_ref, solved_ref, *rest
+    n_region, n_sub, list_ref, owner_ref, live_ref, coupling_ref, solved_ref, *rest
 ):
     chunks, (pay_ref, turned_ref, right_ref, slot_ref, count_ref) = rest[:8], rest[8:]
     i = pl.program_id(0)
 
     @pl.when(i == 0)
     def _():
-        send_slots(place_ref, list_ref, owner_ref, slot_ref, count_ref, n_region, n_sub)
-
-    live = live_ref[i]
+        send_slots(list_ref, owner_ref, slot_ref, count_ref, n_region, n_sub)
+
+    live = live_ref[(lax.axis_index("region") * n_sub + lax.axis_index("sub")) * SUB_DEV + i]
     for j in range(SLOTS):
         rows = slice(j * TILE, (j + 1) * TILE)
         th, tl = halves((coupling_ref[0, j] * (j < live).astype(F32)).T)
@@ -297,14 +293,14 @@
             chunks[c][...] = pay_ref[2 * c : 2 * c + 2]
 
 
-def couple(place, near, owner, live, coupling, solved, n_region, n_sub):
+def couple(near, owner, live, coupling, solved, n_region, n_sub):
     span = SLOTS * TILE
     wide = (SLOTS - 1) * TILE
     return pl.pallas_call(
         lambda *refs: couple_kernel(n_region, n_sub, *refs),
         grid=(SUB_DEV,),
         out_shape=(jax.ShapeDtypeStruct((2, TILE, wide), F32),) * 8,
-        in_specs=[SMEM] * 4
+        in_specs=[SMEM] * 3
         + [
             pl.BlockSpec((1, SLOTS, NI, TILE), lambda i: (i, 0, 0, 0)),
             pl.BlockSpec((1, 2 * NI, span), lambda i: (i, 0, 0)),
@@ -320,7 +316,7 @@
         compiler_params=params(32),
         cost_estimate=pl.CostEstimate(flops=8 * 10**9, bytes_accessed=12 * MIB, transcendentals=0),
         name="couple",
-    )(place, near, owner, live, coupling, solved)
+    )(near, owner, live, coupling, solved)
 
 
 def lane_group(shape, axis):
@@ -484,12 +480,12 @@
     for a in range(PER_DEV):
         t = target_ref[a]
         right = [v_ref[seen_ref[a * (SLOTS - 1) + k]] for k in range(SLOTS - 1)]
-        off = offs[a // 2][a % 2] if a < 8 else offs[4][a - 8]
+        off = offs[a // 2][a % 2] if a < 10 else offs[5][a - 10]
         u_ref[t] = u_ref[t] + dot4(stack_halves(off), jnp.concatenate(right, axis=0))
 
 
 def apply_kernel(target_ref, seen_ref, inv_ref, *rest):
-    offs, pieces, (u_ref, w_ref, v_ref) = rest[:5], rest[5:13], rest[13:]
+    offs, pieces, (u_ref, w_ref, v_ref) = rest[:6], rest[6:14], rest[14:]
     lay_out(pieces, v_ref, (0, 1, 2))
     scatter(target_ref, seen_ref, offs, v_ref, u_ref)
     precondition(inv_ref, u_ref, pieces[0][SEP_DEV * TILE : SEP_DEV * TILE + 1], w_ref)
@@ -500,7 +496,7 @@
     return pl.pallas_call(
         apply_kernel,
         out_shape=(tile, WIDE),
-        in_specs=[SMEM] * 2 + [VMEM] * 14,
+        in_specs=[SMEM] * 2 + [VMEM] * 15,
         out_specs=(VMEM,) * 2,
         scratch_shapes=[pltpu.VMEM((12 * SEP_DEV, TILE, 2 * NRHS), BF16)],
         compiler_params=params(16),
@@ -542,7 +538,7 @@
 def finish_kernel(
     target_ref, seen_ref, own_ref, norm_ref, solved_ref, reduced_ref, ya_ref, yb_ref, u1_ref, w0_ref, w1_ref, *rest
 ):
-    offs, pieces, (interior_ref, x_ref, resid_ref, v_ref, u_ref) = rest[:5], rest[5:13], rest[13:]
+    offs, pieces, (interior_ref, x_ref, resid_ref, v_ref, u_ref) = rest[:6], rest[6:14], rest[14:]
     whole = lambda x: jnp.sum(jnp.sum(x, axis=0, keepdims=True), axis=1, keepdims=True)
     q = whole(norm_ref[1:2]) / whole(norm_ref[:1])
     g1 = 1.0 / (2.0 - q)
@@ -567,7 +563,7 @@
     return pl.pallas_call(
         finish_kernel,
         out_shape=(jax.ShapeDtypeStruct((SUB_DEV, NI, NRHS), F32), tile, tile),
-        in_specs=[SMEM] * 3 + [VMEM] * 21,
+        in_specs=[SMEM] * 3 + [VMEM] * 22,
         out_specs=(VMEM,) * 3,
         scratch_shapes=[
             pltpu.VMEM((12 * SEP_DEV, TILE, 2 * NRHS), BF16),
@@ -584,7 +580,6 @@
     n_region = lax.axis_size("region")
     n_sub = lax.axis_size("sub")
     region = lax.axis_index("region")
-    sub = lax.axis_index("sub")
     both = ("region", "sub")
 
     def shift(x, ahead, turn):
@@ -633,24 +628,23 @@
     here = lax.dynamic_slice_in_dim(lists, region * per_region, per_region, 0)
     behind = lax.dynamic_slice_in_dim(lists, (region - 1) % n_region * per_region, per_region, 0)
     near = jnp.concatenate([behind, here], axis=0).reshape(-1)
-    live = lax.dynamic_slice_in_dim(counts, (region * n_sub + sub) * SUB_DEV, SUB_DEV, 0)
-    place = jnp.stack([region, sub]).astype(jnp.int32)
-    key = (place, near, owner)
-
-    solved, reduced, *pay = eliminate(*key, live, interior_inverse, coupling, interior_grad, n_region, n_sub)
+    key = (near, owner)
+
+    solved, reduced, *pay = eliminate(*key, counts, interior_inverse, coupling, interior_grad, n_region, n_sub)
     arrived = around(pay)
     target, seen, own, later = plan(*key, n_region, n_sub)
-    offs = couple(*key, live, coupling, solved, n_region, n_sub)
+    offs = couple(*key, counts, coupling, solved, n_region, n_sub)
     arrived, offs = lax.optimization_barrier((arrived, offs))
     far = around(offs[4:])
     here, following = gather(target, later, arrived)
     got = shift(following, 1, 0)
     inv, u0 = invert(separator_hessian_blocks, sep_grad, here, got)
-    u0, far = lax.optimization_barrier((u0, far))
-    forwarded = shift(jnp.concatenate(far, axis=0), 1, 0)
+    straight = shift(far[0], 1, 0)
+    u0, far[1], far[3], straight = lax.optimization_barrier((u0, far[1], far[3], straight))
+    forwarded = shift(jnp.concatenate(far[1:], axis=0), 1, 0)
     w0 = begin(inv, u0)
     w0s, _ = spread(w0, u0[0, :NORM_ROWS])
-    offs = around(offs[:4]) + [forwarded]
+    offs = around(offs[:4]) + [straight, forwarded]
     u1, w1 = apply(target, seen, inv, offs, w0s)
     w1s, norms = spread(w1, None, ((), (1, 2)))
     u2, w2 = apply(target, seen, inv, offs, w1s)

time: 193 us -> 190 us (0.984)
  starting transfers between devices: 59.9 us -> 57.8 us
    ppermute x17, starting transfers between devices: 32.4 us -> 30.2 us  [swap(): return lax.ppermute(x, both, pairs)]
    ppermute x20 -> x21, waiting for transfers between devices: 52.8 us -> 53.7 us  [shift(): return lax.ppermute(x, both, pairs)]
    ppermute x20 -> x21, starting transfers between devices: 27.6 us -> 27.7 us  [shift(): return lax.ppermute(x, both, pairs)]
  transfers between devices with their start and end apart: 37 -> 38, of which waited for: 21 -> 19; matrix products, arithmetic and copies ran while one was open for 0% -> 0% of each run, Pallas kernels for 11% -> 12%
where the time goes in v3:
time: 190 us
  waiting for transfers between devices  77.5 us (41%)
  starting transfers between devices  57.8 us (30%)
  Pallas kernels  49.4 us (26%)
  local copies, waits for them, and re-layouts  3.71 us (2%)
    ppermute x21, waiting for transfers between devices, shift(): return lax.ppermute(x, both, pairs)  53.7 us
    ppermute x17, starting transfers between devices, swap(): return lax.ppermute(x, both, pairs)  30.2 us
    ppermute x21, starting transfers between devices, shift(): return lax.ppermute(x, both, pairs)  27.7 us
    ppermute x17, waiting for transfers between devices, swap(): return lax.ppermute(x, both, pairs)  23.8 us
    pallas_call x1, Pallas kernels, eliminate(): pl.pallas_call(lambda *refs: eliminate_kernel(n_region, n_sub, *refs), gr...  16.2 us
    pallas_call x1, Pallas kernels, invert(): pl.pallas_call(invert_kernel, out_shape=(jax.ShapeDtypeStruct((SEP_DEV, 2...  8.03 us
    pallas_call x2, Pallas kernels, apply(): pl.pallas_call(apply_kernel, out_shape=(tile, WIDE), in_specs=[SMEM] * 2...  5.52 us
    pallas_call x1, Pallas kernels, couple(): pl.pallas_call(lambda *refs: couple_kernel(n_region, n_sub, *refs), grid=...  5.39 us
  transfers between devices with their start and end apart: 38, of which 19 were waited for; matrix products, arithmetic and copies ran while one was open for 0% of the time, Pallas kernels for 12%

profile of v3, /device:TPU:0, one launch (start us, length us, event | category | flops | bytes accessed | tf_op | source)
XLA Modules:
  0.0 189.8 jit_solution(4930857312279166351)
XLA Ops:
  0.7 0.8 constant_dynamic-slice_fusion.1
  1.5 0.1 copy.12
  1.6 0.6 reshape.9.refs_0_
  2.2 16.2 %eliminate.1 = (bf16[4,1024,512]{2,1,0:T(8,128)(2,1)}, f32[4,512,128]{2,1,0:T(8,128)}, f32[4,200,128]{2,1,0:T(8,128)}, f32[4,200,128]{2,1,0:T(8,128)}, f32[4,200,128]{2,1,0:T(8,128)}, /*index=5*/f32[4,200,128]{2,1,0:T(8,128)}) custom-call(s32[128]{0:T(128)} %reshape.9.refs_0_, s32[512]{0:T(512)} %refs_1_.5, s32[512]{0:T(512)} %refs_2_.3, ...), custom_call_target="tpu_custom_call" | custom-call | tf_op jit(solution)/shard_map/eliminate/pallas_call | solution.py:232
  18.5 2.1 %collective-permute-start = (f32[4,200,128]{2,1,0:T(8,128)}, f32[4,200,128]{2,1,0:T(8,128)S(1)}, u32[]{:S(2)}, u32[]{:S(2)}) collective-permute-start(f32[4,200,128]{2,1,0:T(8,128)} %get-tuple-element.57), channel_id=1, source_target_pairs={{0,1},{1,2},{2,3},{3,0},{4,5},{5,6},{6,7},{7,4},{8,9},{9,10},{10,1... | collective-permute-start | bytes 1228808 | tf_op jit(solution)/shard_map/ppermute | solution.py:591
  20.5 3.6 %collective-permute-start.1 = (f32[4,200,128]{2,1,0:T(8,128)}, f32[4,200,128]{2,1,0:T(8,128)S(1)}, u32[]{:S(2)}, u32[]{:S(2)}) collective-permute-start(f32[4,200,128]{2,1,0:T(8,128)} %get-tuple-element.58), channel_id=1, source_target_pairs={{0,2},{1,3},{2,0},{3,1},{4,6},{5,7},{6,4},{7,5},{8,10},{9,11},{10,... | collective-permute-start | bytes 1228808 | tf_op jit(solution)/shard_map/ppermute | solution.py:591
  24.1 1.0 collective-permute-start.2
  25.1 2.2 %copy-done.1 = bf16[4,1024,512]{2,1,0:T(8,128)(2,1)S(1)} copy-done((bf16[4,1024,512]{2,1,0:T(8,128)(2,1)S(1)}, bf16[4,1024,512]{2,1,0:T(8,128)(2,1)}, u32[]{:S(2)}) %copy-start.1) | copy-done | bytes 4194328
  27.3 5.4 %couple.1 = (f32[2,128,384]{2,1,0:T(8,128)S(1)}, f32[2,128,384]{2,1,0:T(8,128)S(1)}, f32[2,128,384]{2,1,0:T(8,128)S(1)}, f32[2,128,384]{2,1,0:T(8,128)S(1)}, f32...) custom-call(s32[128]{0:T(128)S(1)} %copy-done.7, ...), custom_call_target="tpu_custom_call" | custom-call | flops 8000000000 | bytes 12582912 | tf_op jit(solution)/shard_map/couple/pallas_call | solution.py:299
  32.7 5.2 %plan.1 = (s32[16]{0:T(128)S(1)}, s32[48]{0:T(128)S(1)}, s32[16]{0:T(128)S(1)}, s32[8]{0:T(128)S(1)}) custom-call(s32[128]{0:T(128)S(1)} %copy-done.7, s32[512]{0:T(512)S(1)} %copy-done.6), custom_call_target="tpu_custom_call" | custom-call | flops 2000000000 | bytes 8192 | tf_op jit(solution)/shard_map/plan/pallas_call | solution.py:146
  38.0 4.4 %collective-permute-done.1.c2 = f32[4,200,128]{2,1,0:T(8,128)S(1)} collective-permute-done((f32[4,200,128]{2,1,0:T(8,128)}, f32[4,200,128]{2,1,0:T(8,128)S(1)}, u32[]{:S(2)}, u32[]{:S(2)}) %collective-permute-start.1) | collective-permute-done | bytes 409632 | tf_op jit(solution)/shard_map/ppermute | solution.py:591
  42.3 0.8 gather.1
  43.2 1.3 collective-permute-start.7
  44.5 2.0 %collective-permute-start.8 = (f32[2,128,384]{2,1,0:T(8,128)S(1)}, f32[2,128,384]{2,1,0:T(8,128)S(1)}, u32[]{:S(2)}, u32[]{:S(2)}) collective-permute-start(f32[2,128,384]{2,1,0:T(8,128)S(1)} %get-tuple-element.82), channel_id=1, source_target_pairs={{0,3},{1,0},{2,1},{3,2},{4,7},{5,4},{6,5},{7,6},{8,11},{9,8},{10,9... | collective-permute-start | bytes 1179656 | tf_op jit(solution)/shard_map/ppermute | solution.py:591
  46.5 1.0 collective-permute-start.9
  47.6 1.0 collective-permute-start.10
  48.6 5.3 %collective-permute-done.3.got_ref = f32[4,200,128]{2,1,0:T(8,128)S(1)} collective-permute-done((f32[4,200,128]{2,1,0:T(8,128)S(1)}, f32[4,200,128]{2,1,0:T(8,128)S(1)}, u32[]{:S(2)}, u32[]{:S(2)}) %collective-permute-start.3) | collective-permute-done | bytes 409632 | tf_op jit(solution)/shard_map/ppermute | solution.py:591
  53.9 8.0 %invert.1 = (bf16[4,256,128]{2,1,0:T(8,128)(2,1)S(1)}, f32[4,128,128]{2,1,0:T(8,128)S(1)}) custom-call(f32[4,128,128]{2,1,0:T(8,128)S(1)} %copy-done.8, f32[4,128,128]{2,1,0:T(8,128)S(1)} %copy-done.9, f32[4,200,128]{2,1,0:T(8,128)S(1)} %get-tuple-element.73.here_ref, f32[4,200,128]{2,1,0:T(8,128)S(1)} %collective-permute-done.3.got_ref), custom_call_target="tpu_custom_call" | custom-call | flops 10000000000 | bytes 4194304 | tf_op jit(solution)/shard_map/invert/pallas_call | solution.py:427
  62.0 0.3 begin.1.rest_6_.rest_0_.w0_ref
  62.3 2.3 %collective-permute-start.14 = (f32[520,128]{1,0:T(8,128)S(1)}, f32[520,128]{1,0:T(8,128)S(1)}, u32[]{:S(2)}, u32[]{:S(2)}) collective-permute-start(f32[520,128]{1,0:T(8,128)S(1)} %begin.1.rest_6_.rest_0_.w0_ref), channel_id=1, source_target_pairs={{0,2},{1,3},{2,0},{3,1},{4,6},{5,7},{6,4},{7,5},{8,10},{9,11},{10,... | collective-permute-start | bytes 798728 | tf_op jit(solution)/shard_map/ppermute | solution.py:591
  64.6 3.8 %collective-permute-start.13 = (f32[520,128]{1,0:T(8,128)S(1)}, f32[520,128]{1,0:T(8,128)S(1)}, u32[]{:S(2)}, u32[]{:S(2)}) collective-permute-start(f32[520,128]{1,0:T(8,128)S(1)} %begin.1.rest_6_.rest_0_.w0_ref), channel_id=1, source_target_pairs={{0,3},{1,0},{2,1},{3,2},{4,7},{5,4},{6,5},{7,6},{8,11},{9,8},{10,9... | collective-permute-start | bytes 798728 | tf_op jit(solution)/shard_map/ppermute | solution.py:591
  68.4 0.8 collective-permute-start.12
  69.3 2.1 %collective-permute-done.14.rest_9_.rest_3_ = f32[520,128]{1,0:T(8,128)S(1)} collective-permute-done((f32[520,128]{1,0:T(8,128)S(1)}, f32[520,128]{1,0:T(8,128)S(1)}, u32[]{:S(2)}, u32[]{:S(2)}) %collective-permute-start.14) | collective-permute-done | bytes 266272 | tf_op jit(solution)/shard_map/ppermute | solution.py:591
  71.4 9.8 %collective-permute-done.13.rest_8_.rest_2_ = f32[520,128]{1,0:T(8,128)S(1)} collective-permute-done((f32[520,128]{1,0:T(8,128)S(1)}, f32[520,128]{1,0:T(8,128)S(1)}, u32[]{:S(2)}, u32[]{:S(2)}) %collective-permute-start.13) | collective-permute-done | bytes 266272 | tf_op jit(solution)/shard_map/ppermute | solution.py:591
  81.3 0.1 collective-permute-start.18
  81.4 0.5 collective-permute-start.4
  81.9 3.6 %collective-permute-start.5 = (f32[2,128,384]{2,1,0:T(8,128)S(1)}, f32[2,128,384]{2,1,0:T(8,128)S(1)}, u32[]{:S(2)}, u32[]{:S(2)}) collective-permute-start(f32[2,128,384]{2,1,0:T(8,128)S(1)} %get-tuple-element.78), channel_id=1, source_target_pairs={{0,2},{1,3},{2,0},{3,1},{4,6},{5,7},{6,4},{7,5},{8,10},{9,11},{10,... | collective-permute-start | bytes 1179656 | tf_op jit(solution)/shard_map/ppermute | solution.py:591
  85.6 8.6 %collective-permute-done.4.rest_1_ = f32[2,128,384]{2,1,0:T(8,128)S(1)} collective-permute-done((f32[2,128,384]{2,1,0:T(8,128)S(1)}, f32[2,128,384]{2,1,0:T(8,128)S(1)}, u32[]{:S(2)}, u32[]{:S(2)}) %collective-permute-start.4) | collective-permute-done | bytes 393248 | tf_op jit(solution)/shard_map/ppermute | solution.py:591
  94.2 1.8 collective-permute-start.16
  96.0 7.3 %collective-permute-done.5.rest_2_ = f32[2,128,384]{2,1,0:T(8,128)S(1)} collective-permute-done((f32[2,128,384]{2,1,0:T(8,128)S(1)}, f32[2,128,384]{2,1,0:T(8,128)S(1)}, u32[]{:S(2)}, u32[]{:S(2)}) %collective-permute-start.5) | collective-permute-done | bytes 393248 | tf_op jit(solution)/shard_map/ppermute | solution.py:591
  103.2 1.8 collective-permute-start.15
  105.0 3.3 %collective-permute-start.17 = (f32[520,128]{1,0:T(8,128)S(1)}, f32[520,128]{1,0:T(8,128)S(1)}, u32[]{:S(2)}, u32[]{:S(2)}) collective-permute-start(f32[520,128]{1,0:T(8,128)S(1)} %collective-permute-done.14.rest_9_.rest_3_), channel_id=1, source_target_pairs={{0,124},{1,125},{2,126},{3,127},{4,8},{5,9},{6,10},{7,11},{8,4},{9... | collective-permute-start | bytes 798728 | tf_op jit(solution)/shard_map/ppermute | solution.py:595
  108.3 4.1 %collective-permute-done.15.rest_10_.rest_4_ = f32[520,128]{1,0:T(8,128)S(1)} collective-permute-done((f32[520,128]{1,0:T(8,128)S(1)}, f32[520,128]{1,0:T(8,128)S(1)}, u32[]{:S(2)}, u32[]{:S(2)}) %collective-permute-start.15) | collective-permute-done | bytes 266272 | tf_op jit(solution)/shard_map/ppermute | solution.py:595
  112.4 2.9 %collective-permute-done.17.rest_12_.rest_6_ = f32[520,128]{1,0:T(8,128)S(1)} collective-permute-done((f32[520,128]{1,0:T(8,128)S(1)}, f32[520,128]{1,0:T(8,128)S(1)}, u32[]{:S(2)}, u32[]{:S(2)}) %collective-permute-start.17) | collective-permute-done | bytes 266272 | tf_op jit(solution)/shard_map/ppermute | solution.py:595
  115.3 2.6 %apply.2 = (f32[4,128,128]{2,1,0:T(8,128)S(1)}, f32[520,128]{1,0:T(8,128)S(1)}) custom-call(s32[16]{0:T(128)S(1)} %get-tuple-element.52.target_ref, s32[48]{0:T(128)S(1)} %get-tuple-element.53.seen_ref, bf16[4,256,128]{2,1,0:T(8,128)(2,1)S(1)} %get-tuple-element.75.inv_ref, f32[2,128,384]{2,1,0:T(8,128)S(1)} %get-tuple-element.76.rest_0_, ...), custom_call_target="tpu_custom_call" | custom-call | flops 2000000000 | bytes 7340032 | tf_op jit(solution)/shard_map/apply/pallas_call | solution.py:496
  117.8 0.1 collective-permute-start.21
  118.0 2.0 %collective-permute-start.19 = (f32[520,128]{1,0:T(8,128)S(1)}, f32[520,128]{1,0:T(8,128)S(1)}, u32[]{:S(2)}, u32[]{:S(2)}) collective-permute-start(f32[520,128]{1,0:T(8,128)S(1)} %get-tuple-element.89.rest_6_.rest_8_.w1_ref), channel_id=1, source_target_pairs={{0,1},{1,2},{2,3},{3,0},{4,5},{5,6},{6,7},{7,4},{8,9},{9,10},{10,1... | collective-permute-start | bytes 798728 | tf_op jit(solution)/shard_map/ppermute | solution.py:591
  120.0 7.6 %collective-permute-done.21.rest_9_.rest_11_ = f32[520,128]{1,0:T(8,128)S(1)} collective-permute-done((f32[520,128]{1,0:T(8,128)S(1)}, f32[520,128]{1,0:T(8,128)S(1)}, u32[]{:S(2)}, u32[]{:S(2)}) %collective-permute-start.21) | collective-permute-done | bytes 266272 | tf_op jit(solution)/shard_map/ppermute | solution.py:591
  127.6 2.7 %collective-permute-done.19.rest_7_.rest_9_ = f32[520,128]{1,0:T(8,128)S(1)} collective-permute-done((f32[520,128]{1,0:T(8,128)S(1)}, f32[520,128]{1,0:T(8,128)S(1)}, u32[]{:S(2)}, u32[]{:S(2)}) %collective-permute-start.19) | collective-permute-done | bytes 266272 | tf_op jit(solution)/shard_map/ppermute | solution.py:591
  130.4 0.1 collective-permute-start.22
  130.5 4.3 %collective-permute-start.26 = (f32[1040,128]{1,0:T(8,128)S(1)}, f32[1040,128]{1,0:T(8,128)S(1)}, u32[]{:S(2)}, u32[]{:S(2)}) collective-permute-start(f32[1040,128]{1,0:T(8,128)S(1)} %pad_maximum_fusion.5), channel_id=1, source_target_pairs={{0,124},{1,125},{2,126},{3,127},{4,8},{5,9},{6,10},{7,11},{8,4},{9... | collective-permute-start | bytes 1597448 | tf_op jit(solution)/shard_map/ppermute | solution.py:595
  134.8 0.9 collective-permute-start.25
  135.7 4.2 %collective-permute-start.27 = (f32[520,128]{1,0:T(8,128)S(1)}, f32[520,128]{1,0:T(8,128)S(1)}, u32[]{:S(2)}, u32[]{:S(2)}) collective-permute-start(f32[520,128]{1,0:T(8,128)S(1)} %collective-permute-done.21.rest_9_.rest_11_), channel_id=1, source_target_pairs={{0,124},{1,125},{2,126},{3,127},{4,8},{5,9},{6,10},{7,11},{8,4},{9... | collective-permute-start | bytes 798728 | tf_op jit(solution)/shard_map/ppermute | solution.py:595
  139.9 5.6 %collective-permute-done.25.rest_10_.rest_12_ = f32[520,128]{1,0:T(8,128)S(1)} collective-permute-done((f32[520,128]{1,0:T(8,128)S(1)}, f32[520,128]{1,0:T(8,128)S(1)}, u32[]{:S(2)}, u32[]{:S(2)}) %collective-permute-start.25) | collective-permute-done | bytes 266272 | tf_op jit(solution)/shard_map/ppermute | solution.py:595
  145.5 2.9 %collective-permute-done.27.rest_12_.rest_14_ = f32[520,128]{1,0:T(8,128)S(1)} collective-permute-done((f32[520,128]{1,0:T(8,128)S(1)}, f32[520,128]{1,0:T(8,128)S(1)}, u32[]{:S(2)}, u32[]{:S(2)}) %collective-permute-start.27) | collective-permute-done | bytes 266272 | tf_op jit(solution)/shard_map/ppermute | solution.py:595
  148.3 2.9 %apply.3 = (f32[4,128,128]{2,1,0:T(8,128)}, f32[520,128]{1,0:T(8,128)S(1)}) custom-call(s32[16]{0:T(128)S(1)} %get-tuple-element.52.target_ref, s32[48]{0:T(128)S(1)} %get-tuple-element.53.seen_ref, bf16[4,256,128]{2,1,0:T(8,128)(2,1)S(1)} %get-tuple-element.75.inv_ref, f32[2,128,384]{2,1,0:T(8,128)S(1)} %get-tuple-element.76.rest_0_, ...), custom_call_target="tpu_custom_call" | custom-call | flops 2000000000 | bytes 7340032 | tf_op jit(solution)/shard_map/apply/pallas_call | solution.py:496
  151.3 0.3 collective-permute-start.28
  151.6 1.2 collective-permute-start.31
  152.8 0.8 collective-permute-start.30
  153.6 1.2 collective-permute-done.23
  154.8 3.6 %collective-permute-done.24 = f32[8,128]{1,0:T(8,128)S(1)} collective-permute-done((f32[8,128]{1,0:T(8,128)S(1)}, f32[8,128]{1,0:T(8,128)S(1)}, u32[]{:S(2)}, u32[]{:S(2)}) %collective-permute-start.24) | collective-permute-done | bytes 4128 | tf_op jit(solution)/shard_map/ppermute | solution.py:595
  158.4 3.1 %collective-permute-done.28.rest_9_ = f32[520,128]{1,0:T(8,128)S(1)} collective-permute-done((f32[520,128]{1,0:T(8,128)S(1)}, f32[520,128]{1,0:T(8,128)S(1)}, u32[]{:S(2)}, u32[]{:S(2)}) %collective-permute-start.28) | collective-permute-done | bytes 266272 | tf_op jit(solution)/shard_map/ppermute | solution.py:591
  161.5 0.8 collective-permute-done.31.rest_8_
  162.3 2.0 %collective-permute-done.30.rest_7_ = f32[520,128]{1,0:T(8,128)S(1)} collective-permute-done((f32[520,128]{1,0:T(8,128)S(1)}, f32[520,128]{1,0:T(8,128)S(1)}, u32[]{:S(2)}, u32[]{:S(2)}) %collective-permute-start.30) | collective-permute-done | bytes 266272 | tf_op jit(solution)/shard_map/ppermute | solution.py:591
  164.4 3.1 %collective-permute-start.29 = (f32[8,128]{1,0:T(8,128)S(1)}, f32[8,128]{1,0:T(8,128)S(1)}, u32[]{:S(2)}, u32[]{:S(2)}) collective-permute-start(f32[8,128]{1,0:T(8,128)S(1)} %add.42), channel_id=1, source_target_pairs={{0,16},{1,17},{2,18},{3,19},{4,20},{5,21},{6,22},{7,23},{8,24},{9,... | collective-permute-start | bytes 12296 | tf_op jit(solution)/shard_map/ppermute | solution.py:595
  167.5 2.8 %collective-permute-start.35 = (f32[520,128]{1,0:T(8,128)S(1)}, f32[520,128]{1,0:T(8,128)S(1)}, u32[]{:S(2)}, u32[]{:S(2)}) collective-permute-start(f32[520,128]{1,0:T(8,128)S(1)} %get-tuple-element.92.rest_6_), channel_id=1, source_target_pairs={{0,124},{1,125},{2,126},{3,127},{4,8},{5,9},{6,10},{7,11},{8,4},{9... | collective-permute-start | bytes 798728 | tf_op jit(solution)/shard_map/ppermute | solution.py:595
  170.3 2.3 %collective-permute-start.37 = (f32[520,128]{1,0:T(8,128)S(1)}, f32[520,128]{1,0:T(8,128)S(1)}, u32[]{:S(2)}, u32[]{:S(2)}) collective-permute-start(f32[520,128]{1,0:T(8,128)S(1)} %collective-permute-done.28.rest_9_), channel_id=1, source_target_pairs={{0,124},{1,125},{2,126},{3,127},{4,8},{5,9},{6,10},{7,11},{8,4},{9... | collective-permute-start | bytes 798728 | tf_op jit(solution)/shard_map/ppermute | solution.py:595
  172.6 0.3 collective-permute-start.33
  173.0 2.6 %collective-permute-start.36 = (f32[1040,128]{1,0:T(8,128)S(1)}, f32[1040,128]{1,0:T(8,128)S(1)}, u32[]{:S(2)}, u32[]{:S(2)}) collective-permute-start(f32[1040,128]{1,0:T(8,128)S(1)} %pad_maximum_fusion.6), channel_id=1, source_target_pairs={{0,124},{1,125},{2,126},{3,127},{4,8},{5,9},{6,10},{7,11},{8,4},{9... | collective-permute-start | bytes 1597448 | tf_op jit(solution)/shard_map/ppermute | solution.py:595
  175.6 1.8 collective-permute-done.33
  177.4 2.6 %collective-permute-start.34 = (f32[8,128]{1,0:T(8,128)S(1)}, f32[8,128]{1,0:T(8,128)S(1)}, u32[]{:S(2)}, u32[]{:S(2)}) collective-permute-start(f32[8,128]{1,0:T(8,128)S(1)} %add.44), channel_id=1, source_target_pairs={{0,64},{1,65},{2,66},{3,67},{4,68},{5,69},{6,70},{7,71},{8,72},{9,... | collective-permute-start | bytes 12296 | tf_op jit(solution)/shard_map/ppermute | solution.py:595
  180.0 3.4 %ahead.1 = (f32[4,512,128]{2,1,0:T(8,128)S(1)}, f32[4,512,128]{2,1,0:T(8,128)S(1)}) custom-call(s32[16]{0:T(128)S(1)} %get-tuple-element.54.own_ref, bf16[4,1024,512]{2,1,0:T(8,128)(2,1)S(1)} %copy-done.2, f32[520,128]{1,0:T(8,128)S(1)} %begin.1.rest_6_.rest_0_.w0_ref, f32[520,128]{1,0:T(8,128)S(1)} %collective-permute-done.12.rest_7_.rest_1_, ...), custom_call_target="tpu_custom_call" | custom-call | flops 8000000000 | bytes 14680064 | tf_op jit(solution)/shard_map/ahead/pallas_call | solution.py:526
  183.5 1.8 collective-permute-done.36.rest_11_
  185.3 4.5 %finish.1 = (f32[4,512,128]{2,1,0:T(8,128)}, f32[4,128,128]{2,1,0:T(8,128)}, f32[4,128,128]{2,1,0:T(8,128)}) custom-call(s32[16]{0:T(128)S(1)} %get-tuple-element.52.target_ref, s32[48]{0:T(128)S(1)} %get-tuple-element.53.seen_ref, s32[16]{0:T(128)S(1)} %get-tuple-element.54.own_ref, f32[8,128]{1,0:T(8,128)S(1)} %add.45.norm_ref, ...), custom_call_target="tpu_custom_call" | custom-call | tf_op jit(solution)/shard_map/finish/pallas_call | solution.py:563
  (59 shorter events, 0.9 us)
Async XLA Ops:
  2.2 22.9 %copy-start = (f32[4,4,512,128]{3,2,1,0:T(8,128)S(1)}, f32[4,4,512,128]{3,2,1,0:T(8,128)}, u32[]{:S(2)}) copy-start(f32[4,4,512,128]{3,2,1,0:T(8,128)} %refs_3_.3) | copy-start | bytes 12582916
  2.2 22.9 %copy-start.5 = (s32[512]{0:T(512)S(1)}, s32[512]{0:T(512)}, u32[]{:S(2)}) copy-start(s32[512]{0:T(512)} %refs_2_.3) | copy-start | bytes 6148
  2.2 22.9 %copy-start.6 = (s32[512]{0:T(512)S(1)}, s32[512]{0:T(512)}, u32[]{:S(2)}) copy-start(s32[512]{0:T(512)} %refs_1_.5) | copy-start | bytes 6148
  2.2 22.9 %copy-start.7 = (s32[128]{0:T(128)S(1)}, s32[128]{0:T(128)}, u32[]{:S(2)}) copy-start(s32[128]{0:T(128)} %reshape.9.refs_0_) | copy-start | bytes 1540
  18.5 19.5 %collective-permute-start = (f32[4,200,128]{2,1,0:T(8,128)}, f32[4,200,128]{2,1,0:T(8,128)S(1)}, u32[]{:S(2)}, u32[]{:S(2)}) collective-permute-start(f32[4,200,128]{2,1,0:T(8,128)} %get-tuple-element.57), channel_id=1, source_target_pairs={{0,1},{1,2},{2,3},{3,0},{4,5},{5,6},{6,7},{7,4},{8,9},{9,10},{10,1... | collective-permute-start | bytes 1228808 | tf_op jit(solution)/shard_map/ppermute | solution.py:591
  20.5 21.8 %collective-permute-start.1 = (f32[4,200,128]{2,1,0:T(8,128)}, f32[4,200,128]{2,1,0:T(8,128)S(1)}, u32[]{:S(2)}, u32[]{:S(2)}) collective-permute-start(f32[4,200,128]{2,1,0:T(8,128)} %get-tuple-element.58), channel_id=1, source_target_pairs={{0,2},{1,3},{2,0},{3,1},{4,6},{5,7},{6,4},{7,5},{8,10},{9,11},{10,... | collective-permute-start | bytes 1228808 | tf_op jit(solution)/shard_map/ppermute | solution.py:591
  24.1 18.2 %collective-permute-start.2 = (f32[4,200,128]{2,1,0:T(8,128)}, f32[4,200,128]{2,1,0:T(8,128)S(1)}, u32[]{:S(2)}, u32[]{:S(2)}) collective-permute-start(f32[4,200,128]{2,1,0:T(8,128)} %get-tuple-element.59), channel_id=1, source_target_pairs={{0,3},{1,0},{2,1},{3,2},{4,7},{5,4},{6,5},{7,6},{8,11},{9,8},{10,9... | collective-permute-start | bytes 1228808 | tf_op jit(solution)/shard_map/ppermute | solution.py:591
  25.1 2.2 %copy-start.1 = (bf16[4,1024,512]{2,1,0:T(8,128)(2,1)S(1)}, bf16[4,1024,512]{2,1,0:T(8,128)(2,1)}, u32[]{:S(2)}) copy-start(bf16[4,1024,512]{2,1,0:T(8,128)(2,1)} %get-tuple-element.60.refs_4_.solved_ref) | copy-start | bytes 12582916
  32.7 9.6 %copy-start.4 = (f32[4,200,128]{2,1,0:T(8,128)S(1)}, f32[4,200,128]{2,1,0:T(8,128)}, u32[]{:S(2)}) copy-start(f32[4,200,128]{2,1,0:T(8,128)} %get-tuple-element.69.c0) | copy-start | bytes 1228804
  37.9 16.0 %copy-start.8 = (f32[4,128,128]{2,1,0:T(8,128)S(1)}, f32[4,128,128]{2,1,0:T(8,128)}, u32[]{:S(2)}) copy-start(f32[4,128,128]{2,1,0:T(8,128)} %hess_ref.1) | copy-start | bytes 786436
  37.9 16.0 %copy-start.9 = (f32[4,128,128]{2,1,0:T(8,128)S(1)}, f32[4,128,128]{2,1,0:T(8,128)}, u32[]{:S(2)}) copy-start(f32[4,128,128]{2,1,0:T(8,128)} %grad_ref.1) | copy-start | bytes 786436
  43.1 10.8 %collective-permute-start.3 = (f32[4,200,128]{2,1,0:T(8,128)S(1)}, f32[4,200,128]{2,1,0:T(8,128)S(1)}, u32[]{:S(2)}, u32[]{:S(2)}) collective-permute-start(f32[4,200,128]{2,1,0:T(8,128)S(1)} %get-tuple-element.74), channel_id=1, source_target_pairs={{0,4},{1,5},{2,6},{3,7},{4,8},{5,9},{6,10},{7,11},{8,12},{9,13},{1... | collective-permute-start | bytes 1228808 | tf_op jit(solution)/shard_map/ppermute | solution.py:591
  43.2 18.7 %collective-permute-start.7 = (f32[2,128,384]{2,1,0:T(8,128)S(1)}, f32[2,128,384]{2,1,0:T(8,128)S(1)}, u32[]{:S(2)}, u32[]{:S(2)}) collective-permute-start(f32[2,128,384]{2,1,0:T(8,128)S(1)} %get-tuple-element.81), channel_id=1, source_target_pairs={{0,1},{1,2},{2,3},{3,0},{4,5},{5,6},{6,7},{7,4},{8,9},{9,10},{10,1... | collective-permute-start | bytes 1179656 | tf_op jit(solution)/shard_map/ppermute | solution.py:591
  44.5 17.5 %collective-permute-start.8 = (f32[2,128,384]{2,1,0:T(8,128)S(1)}, f32[2,128,384]{2,1,0:T(8,128)S(1)}, u32[]{:S(2)}, u32[]{:S(2)}) collective-permute-start(f32[2,128,384]{2,1,0:T(8,128)S(1)} %get-tuple-element.82), channel_id=1, source_target_pairs={{0,3},{1,0},{2,1},{3,2},{4,7},{5,4},{6,5},{7,6},{8,11},{9,8},{10,9... | collective-permute-start | bytes 1179656 | tf_op jit(solution)/shard_map/ppermute | solution.py:591
  46.5 15.4 %collective-permute-start.9 = (f32[2,128,384]{2,1,0:T(8,128)S(1)}, f32[2,128,384]{2,1,0:T(8,128)S(1)}, u32[]{:S(2)}, u32[]{:S(2)}) collective-permute-start(f32[2,128,384]{2,1,0:T(8,128)S(1)} %get-tuple-element.83), channel_id=1, source_target_pairs={{0,4},{1,5},{2,6},{3,7},{4,8},{5,9},{6,10},{7,11},{8,12},{9,13},{1... | collective-permute-start | bytes 1179656 | tf_op jit(solution)/shard_map/ppermute | solution.py:591
  47.6 21.6 %collective-permute-start.10 = (f32[2,128,384]{2,1,0:T(8,128)S(1)}, f32[2,128,384]{2,1,0:T(8,128)S(1)}, u32[]{:S(2)}, u32[]{:S(2)}) collective-permute-start(f32[2,128,384]{2,1,0:T(8,128)S(1)} %get-tuple-element.86), channel_id=1, source_target_pairs={{0,2},{1,3},{2,0},{3,1},{4,6},{5,7},{6,4},{7,5},{8,10},{9,11},{10,... | collective-permute-start | bytes 1179656 | tf_op jit(solution)/shard_map/ppermute | solution.py:591
  62.3 9.2 %collective-permute-start.14 = (f32[520,128]{1,0:T(8,128)S(1)}, f32[520,128]{1,0:T(8,128)S(1)}, u32[]{:S(2)}, u32[]{:S(2)}) collective-permute-start(f32[520,128]{1,0:T(8,128)S(1)} %begin.1.rest_6_.rest_0_.w0_ref), channel_id=1, source_target_pairs={{0,2},{1,3},{2,0},{3,1},{4,6},{5,7},{6,4},{7,5},{8,10},{9,11},{10,... | collective-permute-start | bytes 798728 | tf_op jit(solution)/shard_map/ppermute | solution.py:591
  64.6 16.7 %collective-permute-start.13 = (f32[520,128]{1,0:T(8,128)S(1)}, f32[520,128]{1,0:T(8,128)S(1)}, u32[]{:S(2)}, u32[]{:S(2)}) collective-permute-start(f32[520,128]{1,0:T(8,128)S(1)} %begin.1.rest_6_.rest_0_.w0_ref), channel_id=1, source_target_pairs={{0,3},{1,0},{2,1},{3,2},{4,7},{5,4},{6,5},{7,6},{8,11},{9,8},{10,9... | collective-permute-start | bytes 798728 | tf_op jit(solution)/shard_map/ppermute | solution.py:591
  68.4 12.9 %collective-permute-start.12 = (f32[520,128]{1,0:T(8,128)S(1)}, f32[520,128]{1,0:T(8,128)S(1)}, u32[]{:S(2)}, u32[]{:S(2)}) collective-permute-start(f32[520,128]{1,0:T(8,128)S(1)} %begin.1.rest_6_.rest_0_.w0_ref), channel_id=1, source_target_pairs={{0,1},{1,2},{2,3},{3,0},{4,5},{5,6},{6,7},{7,4},{8,9},{9,10},{10,1... | collective-permute-start | bytes 798728 | tf_op jit(solution)/shard_map/ppermute | solution.py:591
  69.2 46.0 %collective-permute-start.11 = (f32[6,128,384]{2,1,0:T(8,128)S(1)}, f32[6,128,384]{2,1,0:T(8,128)S(1)}, u32[]{:S(2)}, u32[]{:S(2)}) collective-permute-start(f32[6,128,384]{2,1,0:T(8,128)S(1)} %pad_maximum_fusion), channel_id=1, source_target_pairs={{0,4},{1,5},{2,6},{3,7},{4,8},{5,9},{6,10},{7,11},{8,12},{9,13},{1... | collective-permute-start | bytes 3538952 | tf_op jit(solution)/shard_map/ppermute | solution.py:591
  81.3 33.9 %collective-permute-start.18 = (f32[2080,128]{1,0:T(8,128)S(1)}, f32[2080,128]{1,0:T(8,128)S(1)}, u32[]{:S(2)}, u32[]{:S(2)}) collective-permute-start(f32[2080,128]{1,0:T(8,128)S(1)} %pad_maximum_fusion.1), channel_id=1, source_target_pairs={{0,4},{1,5},{2,6},{3,7},{4,0},{5,1},{6,2},{7,3},{8,12},{9,13},{10,... | collective-permute-start | bytes 3194888 | tf_op jit(solution)/shard_map/ppermute | solution.py:595
  81.4 12.8 %collective-permute-start.4 = (f32[2,128,384]{2,1,0:T(8,128)S(1)}, f32[2,128,384]{2,1,0:T(8,128)S(1)}, u32[]{:S(2)}, u32[]{:S(2)}) collective-permute-start(f32[2,128,384]{2,1,0:T(8,128)S(1)} %get-tuple-element.77), channel_id=1, source_target_pairs={{0,1},{1,2},{2,3},{3,0},{4,5},{5,6},{6,7},{7,4},{8,9},{9,10},{10,1... | collective-permute-start | bytes 1179656 | tf_op jit(solution)/shard_map/ppermute | solution.py:591
  81.9 21.3 %collective-permute-start.5 = (f32[2,128,384]{2,1,0:T(8,128)S(1)}, f32[2,128,384]{2,1,0:T(8,128)S(1)}, u32[]{:S(2)}, u32[]{:S(2)}) collective-permute-start(f32[2,128,384]{2,1,0:T(8,128)S(1)} %get-tuple-element.78), channel_id=1, source_target_pairs={{0,2},{1,3},{2,0},{3,1},{4,6},{5,7},{6,4},{7,5},{8,10},{9,11},{10,... | collective-permute-start | bytes 1179656 | tf_op jit(solution)/shard_map/ppermute | solution.py:591
  85.6 19.5 %collective-permute-start.6 = (f32[2,128,384]{2,1,0:T(8,128)S(1)}, f32[2,128,384]{2,1,0:T(8,128)S(1)}, u32[]{:S(2)}, u32[]{:S(2)}) collective-permute-start(f32[2,128,384]{2,1,0:T(8,128)S(1)} %get-tuple-element.79), channel_id=1, source_target_pairs={{0,3},{1,0},{2,1},{3,2},{4,7},{5,4},{6,5},{7,6},{8,11},{9,8},{10,9... | collective-permute-start | bytes 1179656 | tf_op jit(solution)/shard_map/ppermute | solution.py:591
  94.2 21.1 %collective-permute-start.16 = (f32[1040,128]{1,0:T(8,128)S(1)}, f32[1040,128]{1,0:T(8,128)S(1)}, u32[]{:S(2)}, u32[]{:S(2)}) collective-permute-start(f32[1040,128]{1,0:T(8,128)S(1)} %pad_maximum_fusion.4), channel_id=1, source_target_pairs={{0,124},{1,125},{2,126},{3,127},{4,8},{5,9},{6,10},{7,11},{8,4},{9... | collective-permute-start | bytes 1597448 | tf_op jit(solution)/shard_map/ppermute | solution.py:595
  103.2 9.2 %collective-permute-start.15 = (f32[520,128]{1,0:T(8,128)S(1)}, f32[520,128]{1,0:T(8,128)S(1)}, u32[]{:S(2)}, u32[]{:S(2)}) collective-permute-start(f32[520,128]{1,0:T(8,128)S(1)} %begin.1.rest_6_.rest_0_.w0_ref), channel_id=1, source_target_pairs={{0,124},{1,125},{2,126},{3,127},{4,8},{5,9},{6,10},{7,11},{8,4},{9... | collective-permute-start | bytes 798728 | tf_op jit(solution)/shard_map/ppermute | solution.py:595
  105.0 10.2 %collective-permute-start.17 = (f32[520,128]{1,0:T(8,128)S(1)}, f32[520,128]{1,0:T(8,128)S(1)}, u32[]{:S(2)}, u32[]{:S(2)}) collective-permute-start(f32[520,128]{1,0:T(8,128)S(1)} %collective-permute-done.14.rest_9_.rest_3_), channel_id=1, source_target_pairs={{0,124},{1,125},{2,126},{3,127},{4,8},{5,9},{6,10},{7,11},{8,4},{9... | collective-permute-start | bytes 798728 | tf_op jit(solution)/shard_map/ppermute | solution.py:595
  117.8 9.8 %collective-permute-start.21 = (f32[520,128]{1,0:T(8,128)S(1)}, f32[520,128]{1,0:T(8,128)S(1)}, u32[]{:S(2)}, u32[]{:S(2)}) collective-permute-start(f32[520,128]{1,0:T(8,128)S(1)} %get-tuple-element.89.rest_6_.rest_8_.w1_ref), channel_id=1, source_target_pairs={{0,2},{1,3},{2,0},{3,1},{4,6},{5,7},{6,4},{7,5},{8,10},{9,11},{10,... | collective-permute-start | bytes 798728 | tf_op jit(solution)/shard_map/ppermute | solution.py:591
  117.9 9.7 %collective-permute-start.20 = (f32[520,128]{1,0:T(8,128)S(1)}, f32[520,128]{1,0:T(8,128)S(1)}, u32[]{:S(2)}, u32[]{:S(2)}) collective-permute-start(f32[520,128]{1,0:T(8,128)S(1)} %get-tuple-element.89.rest_6_.rest_8_.w1_ref), channel_id=1, source_target_pairs={{0,3},{1,0},{2,1},{3,2},{4,7},{5,4},{6,5},{7,6},{8,11},{9,8},{10,9... | collective-permute-start | bytes 798728 | tf_op jit(solution)/shard_map/ppermute | solution.py:591
  118.0 12.3 %collective-permute-start.19 = (f32[520,128]{1,0:T(8,128)S(1)}, f32[520,128]{1,0:T(8,128)S(1)}, u32[]{:S(2)}, u32[]{:S(2)}) collective-permute-start(f32[520,128]{1,0:T(8,128)S(1)} %get-tuple-element.89.rest_6_.rest_8_.w1_ref), channel_id=1, source_target_pairs={{0,1},{1,2},{2,3},{3,0},{4,5},{5,6},{6,7},{7,4},{8,9},{9,10},{10,1... | collective-permute-start | bytes 798728 | tf_op jit(solution)/shard_map/ppermute | solution.py:591
  130.4 9.5 %collective-permute-start.22 = (f32[2080,128]{1,0:T(8,128)S(1)}, f32[2080,128]{1,0:T(8,128)S(1)}, u32[]{:S(2)}, u32[]{:S(2)}) collective-permute-start(f32[2080,128]{1,0:T(8,128)S(1)} %pad_maximum_fusion.2), channel_id=1, source_target_pairs={{0,4},{1,5},{2,6},{3,7},{4,0},{5,1},{6,2},{7,3},{8,12},{9,13},{10,... | collective-permute-start | bytes 3194888 | tf_op jit(solution)/shard_map/ppermute | solution.py:595
  130.5 17.8 %collective-permute-start.26 = (f32[1040,128]{1,0:T(8,128)S(1)}, f32[1040,128]{1,0:T(8,128)S(1)}, u32[]{:S(2)}, u32[]{:S(2)}) collective-permute-start(f32[1040,128]{1,0:T(8,128)S(1)} %pad_maximum_fusion.5), channel_id=1, source_target_pairs={{0,124},{1,125},{2,126},{3,127},{4,8},{5,9},{6,10},{7,11},{8,4},{9... | collective-permute-start | bytes 1597448 | tf_op jit(solution)/shard_map/ppermute | solution.py:595
  134.8 10.7 %collective-permute-start.25 = (f32[520,128]{1,0:T(8,128)S(1)}, f32[520,128]{1,0:T(8,128)S(1)}, u32[]{:S(2)}, u32[]{:S(2)}) collective-permute-start(f32[520,128]{1,0:T(8,128)S(1)} %get-tuple-element.89.rest_6_.rest_8_.w1_ref), channel_id=1, source_target_pairs={{0,124},{1,125},{2,126},{3,127},{4,8},{5,9},{6,10},{7,11},{8,4},{9... | collective-permute-start | bytes 798728 | tf_op jit(solution)/shard_map/ppermute | solution.py:595
  135.7 12.7 %collective-permute-start.27 = (f32[520,128]{1,0:T(8,128)S(1)}, f32[520,128]{1,0:T(8,128)S(1)}, u32[]{:S(2)}, u32[]{:S(2)}) collective-permute-start(f32[520,128]{1,0:T(8,128)S(1)} %collective-permute-done.21.rest_9_.rest_11_), channel_id=1, source_target_pairs={{0,124},{1,125},{2,126},{3,127},{4,8},{5,9},{6,10},{7,11},{8,4},{9... | collective-permute-start | bytes 798728 | tf_op jit(solution)/shard_map/ppermute | solution.py:595
  148.3 31.7 %copy-start.2 = (bf16[4,1024,512]{2,1,0:T(8,128)(2,1)S(1)}, bf16[4,1024,512]{2,1,0:T(8,128)(2,1)}, u32[]{:S(2)}) copy-start(bf16[4,1024,512]{2,1,0:T(8,128)(2,1)} %get-tuple-element.60.refs_4_.solved_ref) | copy-start | bytes 12582916
  151.3 10.2 %collective-permute-start.28 = (f32[520,128]{1,0:T(8,128)S(1)}, f32[520,128]{1,0:T(8,128)S(1)}, u32[]{:S(2)}, u32[]{:S(2)}) collective-permute-start(f32[520,128]{1,0:T(8,128)S(1)} %get-tuple-element.92.rest_6_), channel_id=1, source_target_pairs={{0,2},{1,3},{2,0},{3,1},{4,6},{5,7},{6,4},{7,5},{8,10},{9,11},{10,... | collective-permute-start | bytes 798728 | tf_op jit(solution)/shard_map/ppermute | solution.py:591
  151.6 10.7 %collective-permute-start.31 = (f32[520,128]{1,0:T(8,128)S(1)}, f32[520,128]{1,0:T(8,128)S(1)}, u32[]{:S(2)}, u32[]{:S(2)}) collective-permute-start(f32[520,128]{1,0:T(8,128)S(1)} %get-tuple-element.92.rest_6_), channel_id=1, source_target_pairs={{0,3},{1,0},{2,1},{3,2},{4,7},{5,4},{6,5},{7,6},{8,11},{9,8},{10,9... | collective-permute-start | bytes 798728 | tf_op jit(solution)/shard_map/ppermute | solution.py:591
  152.8 11.5 %collective-permute-start.30 = (f32[520,128]{1,0:T(8,128)S(1)}, f32[520,128]{1,0:T(8,128)S(1)}, u32[]{:S(2)}, u32[]{:S(2)}) collective-permute-start(f32[520,128]{1,0:T(8,128)S(1)} %get-tuple-element.92.rest_6_), channel_id=1, source_target_pairs={{0,1},{1,2},{2,3},{3,0},{4,5},{5,6},{6,7},{7,4},{8,9},{9,10},{10,1... | collective-permute-start | bytes 798728 | tf_op jit(solution)/shard_map/ppermute | solution.py:591
  153.6 1.2 collective-permute-start.23
  154.8 3.6 %collective-permute-start.24 = (f32[8,128]{1,0:T(8,128)S(1)}, f32[8,128]{1,0:T(8,128)S(1)}, u32[]{:S(2)}, u32[]{:S(2)}) collective-permute-start(f32[8,128]{1,0:T(8,128)S(1)} %add.41), channel_id=1, source_target_pairs={{0,8},{1,9},{2,10},{3,11},{4,12},{5,13},{6,14},{7,15},{8,0},{9,1},... | collective-permute-start | bytes 12296 | tf_op jit(solution)/shard_map/ppermute | solution.py:595
  164.3 8.3 %collective-permute-start.32 = (f32[2080,128]{1,0:T(8,128)S(1)}, f32[2080,128]{1,0:T(8,128)S(1)}, u32[]{:S(2)}, u32[]{:S(2)}) collective-permute-start(f32[2080,128]{1,0:T(8,128)S(1)} %pad_maximum_fusion.3), channel_id=1, source_target_pairs={{0,4},{1,5},{2,6},{3,7},{4,0},{5,1},{6,2},{7,3},{8,12},{9,13},{10,... | collective-permute-start | bytes 3194888 | tf_op jit(solution)/shard_map/ppermute | solution.py:595
  164.4 8.2 %collective-permute-start.29 = (f32[8,128]{1,0:T(8,128)S(1)}, f32[8,128]{1,0:T(8,128)S(1)}, u32[]{:S(2)}, u32[]{:S(2)}) collective-permute-start(f32[8,128]{1,0:T(8,128)S(1)} %add.42), channel_id=1, source_target_pairs={{0,16},{1,17},{2,18},{3,19},{4,20},{5,21},{6,22},{7,23},{8,24},{9,... | collective-permute-start | bytes 12296 | tf_op jit(solution)/shard_map/ppermute | solution.py:595
  167.5 15.9 %collective-permute-start.35 = (f32[520,128]{1,0:T(8,128)S(1)}, f32[520,128]{1,0:T(8,128)S(1)}, u32[]{:S(2)}, u32[]{:S(2)}) collective-permute-start(f32[520,128]{1,0:T(8,128)S(1)} %get-tuple-element.92.rest_6_), channel_id=1, source_target_pairs={{0,124},{1,125},{2,126},{3,127},{4,8},{5,9},{6,10},{7,11},{8,4},{9... | collective-permute-start | bytes 798728 | tf_op jit(solution)/shard_map/ppermute | solution.py:595
  170.3 13.1 %collective-permute-start.37 = (f32[520,128]{1,0:T(8,128)S(1)}, f32[520,128]{1,0:T(8,128)S(1)}, u32[]{:S(2)}, u32[]{:S(2)}) collective-permute-start(f32[520,128]{1,0:T(8,128)S(1)} %collective-permute-done.28.rest_9_), channel_id=1, source_target_pairs={{0,124},{1,125},{2,126},{3,127},{4,8},{5,9},{6,10},{7,11},{8,4},{9... | collective-permute-start | bytes 798728 | tf_op jit(solution)/shard_map/ppermute | solution.py:595
  172.6 4.8 %collective-permute-start.33 = (f32[8,128]{1,0:T(8,128)S(1)}, f32[8,128]{1,0:T(8,128)S(1)}, u32[]{:S(2)}, u32[]{:S(2)}) collective-permute-start(f32[8,128]{1,0:T(8,128)S(1)} %add.43), channel_id=1, source_target_pairs={{0,32},{1,33},{2,34},{3,35},{4,36},{5,37},{6,38},{7,39},{8,40},{9,... | collective-permute-start | bytes 12296 | tf_op jit(solution)/shard_map/ppermute | solution.py:595
  173.0 12.3 %collective-permute-start.36 = (f32[1040,128]{1,0:T(8,128)S(1)}, f32[1040,128]{1,0:T(8,128)S(1)}, u32[]{:S(2)}, u32[]{:S(2)}) collective-permute-start(f32[1040,128]{1,0:T(8,128)S(1)} %pad_maximum_fusion.6), channel_id=1, source_target_pairs={{0,124},{1,125},{2,126},{3,127},{4,8},{5,9},{6,10},{7,11},{8,4},{9... | collective-permute-start | bytes 1597448 | tf_op jit(solution)/shard_map/ppermute | solution.py:595
  177.4 6.0 %collective-permute-start.34 = (f32[8,128]{1,0:T(8,128)S(1)}, f32[8,128]{1,0:T(8,128)S(1)}, u32[]{:S(2)}, u32[]{:S(2)}) collective-permute-start(f32[8,128]{1,0:T(8,128)S(1)} %add.44), channel_id=1, source_target_pairs={{0,64},{1,65},{2,66},{3,67},{4,68},{5,69},{6,70},{7,71},{8,72},{9,... | collective-permute-start | bytes 12296 | tf_op jit(solution)/shard_map/ppermute | solution.py:595
  180.0 5.3 %copy-start.3 = (f32[4,512,128]{2,1,0:T(8,128)S(1)}, f32[4,512,128]{2,1,0:T(8,128)}, u32[]{:S(2)}) copy-start(f32[4,512,128]{2,1,0:T(8,128)} %get-tuple-element.96.reduced_ref) | copy-start | bytes 3145732

commit v4 on v3

--- a/solution.py
+++ b/solution.py
@@ -189,22 +189,25 @@
 
     live = live_ref[(lax.axis_index("region") * n_sub + lax.axis_index("sub")) * SUB_DEV + i]
     ah, al = halves(inverse_ref[0])
-    left_ref[:, :NI] = ah
-    left_ref[:, NI : 2 * NI] = al
-    left_ref[:, 2 * NI :] = ah
+    left_ref[:NI] = ah
+    left_ref[NI:] = al
     for j in range(SLOTS + 1):
         x = grad_ref[0] if j == SLOTS else coupling_ref[0, j] * (j < live).astype(F32)
         cols = slice(j * TILE, (j + 1) * TILE)
         high, low = halves(x)
-        right_ref[:NI, cols] = low
-        right_ref[NI : 2 * NI, cols] = high
-        right_ref[2 * NI :, cols] = high
+        right_ref[:, cols] = high
+        right_ref[:, j * TILE + span + NRHS : (j + 1) * TILE + span + NRHS] = low
         if j < SLOTS:
             th, tl = halves(x.T)
             turned_ref[2 * j * TILE : (2 * j + 1) * TILE] = th
             turned_ref[(2 * j + 1) * TILE : (2 * j + 2) * TILE] = tl
-    both = product(left_ref[...], right_ref[...])
-    reduced = both[:, span:]
+    low_cols = span + NRHS
+    both = (
+        product(left_ref[NI:], right_ref[:, :span])
+        + product(left_ref[:NI], right_ref[:, low_cols : low_cols + span])
+    ) + product(left_ref[:NI], right_ref[:, :span])
+    grad = jnp.concatenate([right_ref[:, span:low_cols], right_ref[:, low_cols + span :]], axis=1)
+    reduced = dot4(left_ref[...], grad)
     reduced_ref[0] = reduced
     pushed = product(turned_ref[...], pair_halves(reduced))
     for j in range(SLOTS):
@@ -247,8 +250,8 @@
         + (pl.BlockSpec((4, tall, TILE), lambda i: (0, 0, 0)),) * 4,
         scratch_shapes=[
             pltpu.VMEM((PER_DEV, tall, TILE), F32),
-            pltpu.VMEM((NI, 3 * NI), BF16),
-            pltpu.VMEM((3 * NI, span + NRHS), BF16),
+            pltpu.VMEM((2 * NI, NI), BF16),
+            pltpu.VMEM((NI, 2 * (span + NRHS)), BF16),
             pltpu.VMEM((2 * span, NI), BF16),
             pltpu.SMEM((PER_DEV,), jnp.int32),
             pltpu.SMEM((2 * n_sub,), jnp.int32),

time: 190 us -> 189 us (level)
  no operation moved by 1% of the time
where the time goes in v4:
time: 189 us
  waiting for transfers between devices  77.5 us (41%)
  starting transfers between devices  57.8 us (31%)
  Pallas kernels  48.1 us (25%)
  local copies, waits for them, and re-layouts  3.71 us (2%)
    ppermute x21, waiting for transfers between devices, shift(): return lax.ppermute(x, both, pairs)  53.7 us
    ppermute x17, starting transfers between devices, swap(): return lax.ppermute(x, both, pairs)  30.2 us
    ppermute x21, starting transfers between devices, shift(): return lax.ppermute(x, both, pairs)  27.7 us
    ppermute x17, waiting for transfers between devices, swap(): return lax.ppermute(x, both, pairs)  23.8 us
    pallas_call x1, Pallas kernels, eliminate(): pl.pallas_call(lambda *refs: eliminate_kernel(n_region, n_sub, *refs), gr...  14.9 us
    pallas_call x1, Pallas kernels, invert(): pl.pallas_call(invert_kernel, out_shape=(jax.ShapeDtypeStruct((SEP_DEV, 2...  8.03 us
    pallas_call x2, Pallas kernels, apply(): pl.pallas_call(apply_kernel, out_shape=(tile, WIDE), in_specs=[SMEM] * 2...  5.52 us
    pallas_call x1, Pallas kernels, couple(): pl.pallas_call(lambda *refs: couple_kernel(n_region, n_sub, *refs), grid=...  5.39 us
  transfers between devices with their start and end apart: 38, of which 19 were waited for; matrix products, arithmetic and copies ran while one was open for 0% of the time, Pallas kernels for 12%

profile of v4, /device:TPU:0, one launch (start us, length us, event | category | flops | bytes accessed | tf_op | source)
XLA Modules:
  0.0 188.5 jit_solution(5103136469761764413)
XLA Ops:
  0.7 0.8 constant_dynamic-slice_fusion.1
  1.5 0.1 copy.12
  1.6 0.6 reshape.9.refs_0_
  2.2 14.9 %eliminate.1 = (bf16[4,1024,512]{2,1,0:T(8,128)(2,1)}, f32[4,512,128]{2,1,0:T(8,128)}, f32[4,200,128]{2,1,0:T(8,128)}, f32[4,200,128]{2,1,0:T(8,128)}, f32[4,200,128]{2,1,0:T(8,128)}, /*index=5*/f32[4,200,128]{2,1,0:T(8,128)}) custom-call(s32[128]{0:T(128)} %reshape.9.refs_0_, s32[512]{0:T(512)} %refs_1_.5, s32[512]{0:T(512)} %refs_2_.3, ...), custom_call_target="tpu_custom_call" | custom-call | tf_op jit(solution)/shard_map/eliminate/pallas_call | solution.py:235
  17.1 2.1 %collective-permute-start = (f32[4,200,128]{2,1,0:T(8,128)}, f32[4,200,128]{2,1,0:T(8,128)S(1)}, u32[]{:S(2)}, u32[]{:S(2)}) collective-permute-start(f32[4,200,128]{2,1,0:T(8,128)} %get-tuple-element.57), channel_id=1, source_target_pairs={{0,1},{1,2},{2,3},{3,0},{4,5},{5,6},{6,7},{7,4},{8,9},{9,10},{10,1... | collective-permute-start | bytes 1228808 | tf_op jit(solution)/shard_map/ppermute | solution.py:594
  19.2 3.6 %collective-permute-start.1 = (f32[4,200,128]{2,1,0:T(8,128)}, f32[4,200,128]{2,1,0:T(8,128)S(1)}, u32[]{:S(2)}, u32[]{:S(2)}) collective-permute-start(f32[4,200,128]{2,1,0:T(8,128)} %get-tuple-element.58), channel_id=1, source_target_pairs={{0,2},{1,3},{2,0},{3,1},{4,6},{5,7},{6,4},{7,5},{8,10},{9,11},{10,... | collective-permute-start | bytes 1228808 | tf_op jit(solution)/shard_map/ppermute | solution.py:594
  22.8 1.0 collective-permute-start.2
  23.8 2.2 %copy-done.1 = bf16[4,1024,512]{2,1,0:T(8,128)(2,1)S(1)} copy-done((bf16[4,1024,512]{2,1,0:T(8,128)(2,1)S(1)}, bf16[4,1024,512]{2,1,0:T(8,128)(2,1)}, u32[]{:S(2)}) %copy-start.1) | copy-done | bytes 4194328
  26.0 5.4 %couple.1 = (f32[2,128,384]{2,1,0:T(8,128)S(1)}, f32[2,128,384]{2,1,0:T(8,128)S(1)}, f32[2,128,384]{2,1,0:T(8,128)S(1)}, f32[2,128,384]{2,1,0:T(8,128)S(1)}, f32...) custom-call(s32[128]{0:T(128)S(1)} %copy-done.7, ...), custom_call_target="tpu_custom_call" | custom-call | flops 8000000000 | bytes 12582912 | tf_op jit(solution)/shard_map/couple/pallas_call | solution.py:302
  31.4 5.2 %plan.1 = (s32[16]{0:T(128)S(1)}, s32[48]{0:T(128)S(1)}, s32[16]{0:T(128)S(1)}, s32[8]{0:T(128)S(1)}) custom-call(s32[128]{0:T(128)S(1)} %copy-done.7, s32[512]{0:T(512)S(1)} %copy-done.6), custom_call_target="tpu_custom_call" | custom-call | flops 2000000000 | bytes 8192 | tf_op jit(solution)/shard_map/plan/pallas_call | solution.py:146
  36.7 4.4 %collective-permute-done.1.c2 = f32[4,200,128]{2,1,0:T(8,128)S(1)} collective-permute-done((f32[4,200,128]{2,1,0:T(8,128)}, f32[4,200,128]{2,1,0:T(8,128)S(1)}, u32[]{:S(2)}, u32[]{:S(2)}) %collective-permute-start.1) | collective-permute-done | bytes 409632 | tf_op jit(solution)/shard_map/ppermute | solution.py:594
  41.0 0.8 gather.1
  41.9 1.3 collective-permute-start.7
  43.2 2.0 %collective-permute-start.8 = (f32[2,128,384]{2,1,0:T(8,128)S(1)}, f32[2,128,384]{2,1,0:T(8,128)S(1)}, u32[]{:S(2)}, u32[]{:S(2)}) collective-permute-start(f32[2,128,384]{2,1,0:T(8,128)S(1)} %get-tuple-element.82), channel_id=1, source_target_pairs={{0,3},{1,0},{2,1},{3,2},{4,7},{5,4},{6,5},{7,6},{8,11},{9,8},{10,9... | collective-permute-start | bytes 1179656 | tf_op jit(solution)/shard_map/ppermute | solution.py:594
  45.2 1.0 collective-permute-start.9
  46.2 1.0 collective-permute-start.10
  47.3 5.3 %collective-permute-done.3.got_ref = f32[4,200,128]{2,1,0:T(8,128)S(1)} collective-permute-done((f32[4,200,128]{2,1,0:T(8,128)S(1)}, f32[4,200,128]{2,1,0:T(8,128)S(1)}, u32[]{:S(2)}, u32[]{:S(2)}) %collective-permute-start.3) | collective-permute-done | bytes 409632 | tf_op jit(solution)/shard_map/ppermute | solution.py:594
  52.6 8.0 %invert.1 = (bf16[4,256,128]{2,1,0:T(8,128)(2,1)S(1)}, f32[4,128,128]{2,1,0:T(8,128)S(1)}) custom-call(f32[4,128,128]{2,1,0:T(8,128)S(1)} %copy-done.8, f32[4,128,128]{2,1,0:T(8,128)S(1)} %copy-done.9, f32[4,200,128]{2,1,0:T(8,128)S(1)} %get-tuple-element.73.here_ref, f32[4,200,128]{2,1,0:T(8,128)S(1)} %collective-permute-done.3.got_ref), custom_call_target="tpu_custom_call" | custom-call | flops 10000000000 | bytes 4194304 | tf_op jit(solution)/shard_map/invert/pallas_call | solution.py:430
  60.7 0.3 begin.1.rest_6_.rest_0_.w0_ref
  61.0 2.3 %collective-permute-start.14 = (f32[520,128]{1,0:T(8,128)S(1)}, f32[520,128]{1,0:T(8,128)S(1)}, u32[]{:S(2)}, u32[]{:S(2)}) collective-permute-start(f32[520,128]{1,0:T(8,128)S(1)} %begin.1.rest_6_.rest_0_.w0_ref), channel_id=1, source_target_pairs={{0,2},{1,3},{2,0},{3,1},{4,6},{5,7},{6,4},{7,5},{8,10},{9,11},{10,... | collective-permute-start | bytes 798728 | tf_op jit(solution)/shard_map/ppermute | solution.py:594
  63.3 3.8 %collective-permute-start.13 = (f32[520,128]{1,0:T(8,128)S(1)}, f32[520,128]{1,0:T(8,128)S(1)}, u32[]{:S(2)}, u32[]{:S(2)}) collective-permute-start(f32[520,128]{1,0:T(8,128)S(1)} %begin.1.rest_6_.rest_0_.w0_ref), channel_id=1, source_target_pairs={{0,3},{1,0},{2,1},{3,2},{4,7},{5,4},{6,5},{7,6},{8,11},{9,8},{10,9... | collective-permute-start | bytes 798728 | tf_op jit(solution)/shard_map/ppermute | solution.py:594
  67.0 0.8 collective-permute-start.12
  68.0 2.1 %collective-permute-done.14.rest_9_.rest_3_ = f32[520,128]{1,0:T(8,128)S(1)} collective-permute-done((f32[520,128]{1,0:T(8,128)S(1)}, f32[520,128]{1,0:T(8,128)S(1)}, u32[]{:S(2)}, u32[]{:S(2)}) %collective-permute-start.14) | collective-permute-done | bytes 266272 | tf_op jit(solution)/shard_map/ppermute | solution.py:594
  70.1 9.8 %collective-permute-done.13.rest_8_.rest_2_ = f32[520,128]{1,0:T(8,128)S(1)} collective-permute-done((f32[520,128]{1,0:T(8,128)S(1)}, f32[520,128]{1,0:T(8,128)S(1)}, u32[]{:S(2)}, u32[]{:S(2)}) %collective-permute-start.13) | collective-permute-done | bytes 266272 | tf_op jit(solution)/shard_map/ppermute | solution.py:594
  80.0 0.1 collective-permute-start.18
  80.1 0.5 collective-permute-start.4
  80.6 3.6 %collective-permute-start.5 = (f32[2,128,384]{2,1,0:T(8,128)S(1)}, f32[2,128,384]{2,1,0:T(8,128)S(1)}, u32[]{:S(2)}, u32[]{:S(2)}) collective-permute-start(f32[2,128,384]{2,1,0:T(8,128)S(1)} %get-tuple-element.78), channel_id=1, source_target_pairs={{0,2},{1,3},{2,0},{3,1},{4,6},{5,7},{6,4},{7,5},{8,10},{9,11},{10,... | collective-permute-start | bytes 1179656 | tf_op jit(solution)/shard_map/ppermute | solution.py:594
  84.3 8.6 %collective-permute-done.4.rest_1_ = f32[2,128,384]{2,1,0:T(8,128)S(1)} collective-permute-done((f32[2,128,384]{2,1,0:T(8,128)S(1)}, f32[2,128,384]{2,1,0:T(8,128)S(1)}, u32[]{:S(2)}, u32[]{:S(2)}) %collective-permute-start.4) | collective-permute-done | bytes 393248 | tf_op jit(solution)/shard_map/ppermute | solution.py:594
  92.9 1.8 collective-permute-start.16
  94.7 7.3 %collective-permute-done.5.rest_2_ = f32[2,128,384]{2,1,0:T(8,128)S(1)} collective-permute-done((f32[2,128,384]{2,1,0:T(8,128)S(1)}, f32[2,128,384]{2,1,0:T(8,128)S(1)}, u32[]{:S(2)}, u32[]{:S(2)}) %collective-permute-start.5) | collective-permute-done | bytes 393248 | tf_op jit(solution)/shard_map/ppermute | solution.py:594
  101.9 1.8 collective-permute-start.15
  103.7 3.3 %collective-permute-start.17 = (f32[520,128]{1,0:T(8,128)S(1)}, f32[520,128]{1,0:T(8,128)S(1)}, u32[]{:S(2)}, u32[]{:S(2)}) collective-permute-start(f32[520,128]{1,0:T(8,128)S(1)} %collective-permute-done.14.rest_9_.rest_3_), channel_id=1, source_target_pairs={{0,124},{1,125},{2,126},{3,127},{4,8},{5,9},{6,10},{7,11},{8,4},{9... | collective-permute-start | bytes 798728 | tf_op jit(solution)/shard_map/ppermute | solution.py:598
  107.0 4.1 %collective-permute-done.15.rest_10_.rest_4_ = f32[520,128]{1,0:T(8,128)S(1)} collective-permute-done((f32[520,128]{1,0:T(8,128)S(1)}, f32[520,128]{1,0:T(8,128)S(1)}, u32[]{:S(2)}, u32[]{:S(2)}) %collective-permute-start.15) | collective-permute-done | bytes 266272 | tf_op jit(solution)/shard_map/ppermute | solution.py:598
  111.1 2.9 %collective-permute-done.17.rest_12_.rest_6_ = f32[520,128]{1,0:T(8,128)S(1)} collective-permute-done((f32[520,128]{1,0:T(8,128)S(1)}, f32[520,128]{1,0:T(8,128)S(1)}, u32[]{:S(2)}, u32[]{:S(2)}) %collective-permute-start.17) | collective-permute-done | bytes 266272 | tf_op jit(solution)/shard_map/ppermute | solution.py:598
  114.0 2.6 %apply.2 = (f32[4,128,128]{2,1,0:T(8,128)S(1)}, f32[520,128]{1,0:T(8,128)S(1)}) custom-call(s32[16]{0:T(128)S(1)} %get-tuple-element.52.target_ref, s32[48]{0:T(128)S(1)} %get-tuple-element.53.seen_ref, bf16[4,256,128]{2,1,0:T(8,128)(2,1)S(1)} %get-tuple-element.75.inv_ref, f32[2,128,384]{2,1,0:T(8,128)S(1)} %get-tuple-element.76.rest_0_, ...), custom_call_target="tpu_custom_call" | custom-call | flops 2000000000 | bytes 7340032 | tf_op jit(solution)/shard_map/apply/pallas_call | solution.py:499
  116.5 0.1 collective-permute-start.21
  116.7 2.0 %collective-permute-start.19 = (f32[520,128]{1,0:T(8,128)S(1)}, f32[520,128]{1,0:T(8,128)S(1)}, u32[]{:S(2)}, u32[]{:S(2)}) collective-permute-start(f32[520,128]{1,0:T(8,128)S(1)} %get-tuple-element.89.rest_6_.rest_8_.w1_ref), channel_id=1, source_target_pairs={{0,1},{1,2},{2,3},{3,0},{4,5},{5,6},{6,7},{7,4},{8,9},{9,10},{10,1... | collective-permute-start | bytes 798728 | tf_op jit(solution)/shard_map/ppermute | solution.py:594
  118.7 7.6 %collective-permute-done.21.rest_9_.rest_11_ = f32[520,128]{1,0:T(8,128)S(1)} collective-permute-done((f32[520,128]{1,0:T(8,128)S(1)}, f32[520,128]{1,0:T(8,128)S(1)}, u32[]{:S(2)}, u32[]{:S(2)}) %collective-permute-start.21) | collective-permute-done | bytes 266272 | tf_op jit(solution)/shard_map/ppermute | solution.py:594
  126.3 2.7 %collective-permute-done.19.rest_7_.rest_9_ = f32[520,128]{1,0:T(8,128)S(1)} collective-permute-done((f32[520,128]{1,0:T(8,128)S(1)}, f32[520,128]{1,0:T(8,128)S(1)}, u32[]{:S(2)}, u32[]{:S(2)}) %collective-permute-start.19) | collective-permute-done | bytes 266272 | tf_op jit(solution)/shard_map/ppermute | solution.py:594
  129.2 4.3 %collective-permute-start.26 = (f32[1040,128]{1,0:T(8,128)S(1)}, f32[1040,128]{1,0:T(8,128)S(1)}, u32[]{:S(2)}, u32[]{:S(2)}) collective-permute-start(f32[1040,128]{1,0:T(8,128)S(1)} %pad_maximum_fusion.5), channel_id=1, source_target_pairs={{0,124},{1,125},{2,126},{3,127},{4,8},{5,9},{6,10},{7,11},{8,4},{9... | collective-permute-start | bytes 1597448 | tf_op jit(solution)/shard_map/ppermute | solution.py:598
  133.5 0.9 collective-permute-start.25
  134.4 4.2 %collective-permute-start.27 = (f32[520,128]{1,0:T(8,128)S(1)}, f32[520,128]{1,0:T(8,128)S(1)}, u32[]{:S(2)}, u32[]{:S(2)}) collective-permute-start(f32[520,128]{1,0:T(8,128)S(1)} %collective-permute-done.21.rest_9_.rest_11_), channel_id=1, source_target_pairs={{0,124},{1,125},{2,126},{3,127},{4,8},{5,9},{6,10},{7,11},{8,4},{9... | collective-permute-start | bytes 798728 | tf_op jit(solution)/shard_map/ppermute | solution.py:598
  138.6 5.6 %collective-permute-done.25.rest_10_.rest_12_ = f32[520,128]{1,0:T(8,128)S(1)} collective-permute-done((f32[520,128]{1,0:T(8,128)S(1)}, f32[520,128]{1,0:T(8,128)S(1)}, u32[]{:S(2)}, u32[]{:S(2)}) %collective-permute-start.25) | collective-permute-done | bytes 266272 | tf_op jit(solution)/shard_map/ppermute | solution.py:598
  144.2 2.9 %collective-permute-done.27.rest_12_.rest_14_ = f32[520,128]{1,0:T(8,128)S(1)} collective-permute-done((f32[520,128]{1,0:T(8,128)S(1)}, f32[520,128]{1,0:T(8,128)S(1)}, u32[]{:S(2)}, u32[]{:S(2)}) %collective-permute-start.27) | collective-permute-done | bytes 266272 | tf_op jit(solution)/shard_map/ppermute | solution.py:598
  147.0 2.9 %apply.3 = (f32[4,128,128]{2,1,0:T(8,128)}, f32[520,128]{1,0:T(8,128)S(1)}) custom-call(s32[16]{0:T(128)S(1)} %get-tuple-element.52.target_ref, s32[48]{0:T(128)S(1)} %get-tuple-element.53.seen_ref, bf16[4,256,128]{2,1,0:T(8,128)(2,1)S(1)} %get-tuple-element.75.inv_ref, f32[2,128,384]{2,1,0:T(8,128)S(1)} %get-tuple-element.76.rest_0_, ...), custom_call_target="tpu_custom_call" | custom-call | flops 2000000000 | bytes 7340032 | tf_op jit(solution)/shard_map/apply/pallas_call | solution.py:499
  150.0 0.3 collective-permute-start.28
  150.3 1.2 collective-permute-start.31
  151.5 0.8 collective-permute-start.30
  152.3 1.2 collective-permute-done.23
  153.5 3.6 %collective-permute-done.24 = f32[8,128]{1,0:T(8,128)S(1)} collective-permute-done((f32[8,128]{1,0:T(8,128)S(1)}, f32[8,128]{1,0:T(8,128)S(1)}, u32[]{:S(2)}, u32[]{:S(2)}) %collective-permute-start.24) | collective-permute-done | bytes 4128 | tf_op jit(solution)/shard_map/ppermute | solution.py:598
  157.1 3.1 %collective-permute-done.28.rest_9_ = f32[520,128]{1,0:T(8,128)S(1)} collective-permute-done((f32[520,128]{1,0:T(8,128)S(1)}, f32[520,128]{1,0:T(8,128)S(1)}, u32[]{:S(2)}, u32[]{:S(2)}) %collective-permute-start.28) | collective-permute-done | bytes 266272 | tf_op jit(solution)/shard_map/ppermute | solution.py:594
  160.2 0.8 collective-permute-done.31.rest_8_
  161.0 2.0 %collective-permute-done.30.rest_7_ = f32[520,128]{1,0:T(8,128)S(1)} collective-permute-done((f32[520,128]{1,0:T(8,128)S(1)}, f32[520,128]{1,0:T(8,128)S(1)}, u32[]{:S(2)}, u32[]{:S(2)}) %collective-permute-start.30) | collective-permute-done | bytes 266272 | tf_op jit(solution)/shard_map/ppermute | solution.py:594
  163.0 0.1 collective-permute-start.32
  163.1 3.1 %collective-permute-start.29 = (f32[8,128]{1,0:T(8,128)S(1)}, f32[8,128]{1,0:T(8,128)S(1)}, u32[]{:S(2)}, u32[]{:S(2)}) collective-permute-start(f32[8,128]{1,0:T(8,128)S(1)} %add.42), channel_id=1, source_target_pairs={{0,16},{1,17},{2,18},{3,19},{4,20},{5,21},{6,22},{7,23},{8,24},{9,... | collective-permute-start | bytes 12296 | tf_op jit(solution)/shard_map/ppermute | solution.py:598
  166.2 2.8 %collective-permute-start.35 = (f32[520,128]{1,0:T(8,128)S(1)}, f32[520,128]{1,0:T(8,128)S(1)}, u32[]{:S(2)}, u32[]{:S(2)}) collective-permute-start(f32[520,128]{1,0:T(8,128)S(1)} %get-tuple-element.92.rest_6_), channel_id=1, source_target_pairs={{0,124},{1,125},{2,126},{3,127},{4,8},{5,9},{6,10},{7,11},{8,4},{9... | collective-permute-start | bytes 798728 | tf_op jit(solution)/shard_map/ppermute | solution.py:598
  169.0 2.3 %collective-permute-start.37 = (f32[520,128]{1,0:T(8,128)S(1)}, f32[520,128]{1,0:T(8,128)S(1)}, u32[]{:S(2)}, u32[]{:S(2)}) collective-permute-start(f32[520,128]{1,0:T(8,128)S(1)} %collective-permute-done.28.rest_9_), channel_id=1, source_target_pairs={{0,124},{1,125},{2,126},{3,127},{4,8},{5,9},{6,10},{7,11},{8,4},{9... | collective-permute-start | bytes 798728 | tf_op jit(solution)/shard_map/ppermute | solution.py:598
  171.3 0.4 collective-permute-start.33
  171.7 2.6 %collective-permute-start.36 = (f32[1040,128]{1,0:T(8,128)S(1)}, f32[1040,128]{1,0:T(8,128)S(1)}, u32[]{:S(2)}, u32[]{:S(2)}) collective-permute-start(f32[1040,128]{1,0:T(8,128)S(1)} %pad_maximum_fusion.6), channel_id=1, source_target_pairs={{0,124},{1,125},{2,126},{3,127},{4,8},{5,9},{6,10},{7,11},{8,4},{9... | collective-permute-start | bytes 1597448 | tf_op jit(solution)/shard_map/ppermute | solution.py:598
  174.3 1.8 collective-permute-done.33
  176.1 2.6 %collective-permute-start.34 = (f32[8,128]{1,0:T(8,128)S(1)}, f32[8,128]{1,0:T(8,128)S(1)}, u32[]{:S(2)}, u32[]{:S(2)}) collective-permute-start(f32[8,128]{1,0:T(8,128)S(1)} %add.44), channel_id=1, source_target_pairs={{0,64},{1,65},{2,66},{3,67},{4,68},{5,69},{6,70},{7,71},{8,72},{9,... | collective-permute-start | bytes 12296 | tf_op jit(solution)/shard_map/ppermute | solution.py:598
  178.7 3.4 %ahead.1 = (f32[4,512,128]{2,1,0:T(8,128)S(1)}, f32[4,512,128]{2,1,0:T(8,128)S(1)}) custom-call(s32[16]{0:T(128)S(1)} %get-tuple-element.54.own_ref, bf16[4,1024,512]{2,1,0:T(8,128)(2,1)S(1)} %copy-done.2, f32[520,128]{1,0:T(8,128)S(1)} %begin.1.rest_6_.rest_0_.w0_ref, f32[520,128]{1,0:T(8,128)S(1)} %collective-permute-done.12.rest_7_.rest_1_, ...), custom_call_target="tpu_custom_call" | custom-call | flops 8000000000 | bytes 14680064 | tf_op jit(solution)/shard_map/ahead/pallas_call | solution.py:529
  182.2 1.8 collective-permute-done.36.rest_11_
  184.0 4.5 %finish.1 = (f32[4,512,128]{2,1,0:T(8,128)}, f32[4,128,128]{2,1,0:T(8,128)}, f32[4,128,128]{2,1,0:T(8,128)}) custom-call(s32[16]{0:T(128)S(1)} %get-tuple-element.52.target_ref, s32[48]{0:T(128)S(1)} %get-tuple-element.53.seen_ref, s32[16]{0:T(128)S(1)} %get-tuple-element.54.own_ref, f32[8,128]{1,0:T(8,128)S(1)} %add.45.norm_ref, ...), custom_call_target="tpu_custom_call" | custom-call | tf_op jit(solution)/shard_map/finish/pallas_call | solution.py:566
  (59 shorter events, 0.9 us)
Async XLA Ops:
  2.2 21.6 %copy-start = (f32[4,4,512,128]{3,2,1,0:T(8,128)S(1)}, f32[4,4,512,128]{3,2,1,0:T(8,128)}, u32[]{:S(2)}) copy-start(f32[4,4,512,128]{3,2,1,0:T(8,128)} %refs_3_.3) | copy-start | bytes 12582916
  2.2 21.6 %copy-start.5 = (s32[512]{0:T(512)S(1)}, s32[512]{0:T(512)}, u32[]{:S(2)}) copy-start(s32[512]{0:T(512)} %refs_2_.3) | copy-start | bytes 6148
  2.2 21.6 %copy-start.6 = (s32[512]{0:T(512)S(1)}, s32[512]{0:T(512)}, u32[]{:S(2)}) copy-start(s32[512]{0:T(512)} %refs_1_.5) | copy-start | bytes 6148
  2.2 21.6 %copy-start.7 = (s32[128]{0:T(128)S(1)}, s32[128]{0:T(128)}, u32[]{:S(2)}) copy-start(s32[128]{0:T(128)} %reshape.9.refs_0_) | copy-start | bytes 1540
  17.1 19.5 %collective-permute-start = (f32[4,200,128]{2,1,0:T(8,128)}, f32[4,200,128]{2,1,0:T(8,128)S(1)}, u32[]{:S(2)}, u32[]{:S(2)}) collective-permute-start(f32[4,200,128]{2,1,0:T(8,128)} %get-tuple-element.57), channel_id=1, source_target_pairs={{0,1},{1,2},{2,3},{3,0},{4,5},{5,6},{6,7},{7,4},{8,9},{9,10},{10,1... | collective-permute-start | bytes 1228808 | tf_op jit(solution)/shard_map/ppermute | solution.py:594
  19.2 21.8 %collective-permute-start.1 = (f32[4,200,128]{2,1,0:T(8,128)}, f32[4,200,128]{2,1,0:T(8,128)S(1)}, u32[]{:S(2)}, u32[]{:S(2)}) collective-permute-start(f32[4,200,128]{2,1,0:T(8,128)} %get-tuple-element.58), channel_id=1, source_target_pairs={{0,2},{1,3},{2,0},{3,1},{4,6},{5,7},{6,4},{7,5},{8,10},{9,11},{10,... | collective-permute-start | bytes 1228808 | tf_op jit(solution)/shard_map/ppermute | solution.py:594
  22.8 18.2 %collective-permute-start.2 = (f32[4,200,128]{2,1,0:T(8,128)}, f32[4,200,128]{2,1,0:T(8,128)S(1)}, u32[]{:S(2)}, u32[]{:S(2)}) collective-permute-start(f32[4,200,128]{2,1,0:T(8,128)} %get-tuple-element.59), channel_id=1, source_target_pairs={{0,3},{1,0},{2,1},{3,2},{4,7},{5,4},{6,5},{7,6},{8,11},{9,8},{10,9... | collective-permute-start | bytes 1228808 | tf_op jit(solution)/shard_map/ppermute | solution.py:594
  23.8 2.2 %copy-start.1 = (bf16[4,1024,512]{2,1,0:T(8,128)(2,1)S(1)}, bf16[4,1024,512]{2,1,0:T(8,128)(2,1)}, u32[]{:S(2)}) copy-start(bf16[4,1024,512]{2,1,0:T(8,128)(2,1)} %get-tuple-element.60.refs_4_.solved_ref) | copy-start | bytes 12582916
  31.4 9.6 %copy-start.4 = (f32[4,200,128]{2,1,0:T(8,128)S(1)}, f32[4,200,128]{2,1,0:T(8,128)}, u32[]{:S(2)}) copy-start(f32[4,200,128]{2,1,0:T(8,128)} %get-tuple-element.69.c0) | copy-start | bytes 1228804
  36.6 16.0 %copy-start.8 = (f32[4,128,128]{2,1,0:T(8,128)S(1)}, f32[4,128,128]{2,1,0:T(8,128)}, u32[]{:S(2)}) copy-start(f32[4,128,128]{2,1,0:T(8,128)} %hess_ref.1) | copy-start | bytes 786436
  36.6 16.0 %copy-start.9 = (f32[4,128,128]{2,1,0:T(8,128)S(1)}, f32[4,128,128]{2,1,0:T(8,128)}, u32[]{:S(2)}) copy-start(f32[4,128,128]{2,1,0:T(8,128)} %grad_ref.1) | copy-start | bytes 786436
  41.8 10.8 %collective-permute-start.3 = (f32[4,200,128]{2,1,0:T(8,128)S(1)}, f32[4,200,128]{2,1,0:T(8,128)S(1)}, u32[]{:S(2)}, u32[]{:S(2)}) collective-permute-start(f32[4,200,128]{2,1,0:T(8,128)S(1)} %get-tuple-element.74), channel_id=1, source_target_pairs={{0,4},{1,5},{2,6},{3,7},{4,8},{5,9},{6,10},{7,11},{8,12},{9,13},{1... | collective-permute-start | bytes 1228808 | tf_op jit(solution)/shard_map/ppermute | solution.py:594
  41.9 18.7 %collective-permute-start.7 = (f32[2,128,384]{2,1,0:T(8,128)S(1)}, f32[2,128,384]{2,1,0:T(8,128)S(1)}, u32[]{:S(2)}, u32[]{:S(2)}) collective-permute-start(f32[2,128,384]{2,1,0:T(8,128)S(1)} %get-tuple-element.81), channel_id=1, source_target_pairs={{0,1},{1,2},{2,3},{3,0},{4,5},{5,6},{6,7},{7,4},{8,9},{9,10},{10,1... | collective-permute-start | bytes 1179656 | tf_op jit(solution)/shard_map/ppermute | solution.py:594
  43.2 17.4 %collective-permute-start.8 = (f32[2,128,384]{2,1,0:T(8,128)S(1)}, f32[2,128,384]{2,1,0:T(8,128)S(1)}, u32[]{:S(2)}, u32[]{:S(2)}) collective-permute-start(f32[2,128,384]{2,1,0:T(8,128)S(1)} %get-tuple-element.82), channel_id=1, source_target_pairs={{0,3},{1,0},{2,1},{3,2},{4,7},{5,4},{6,5},{7,6},{8,11},{9,8},{10,9... | collective-permute-start | bytes 1179656 | tf_op jit(solution)/shard_map/ppermute | solution.py:594
  45.2 15.4 %collective-permute-start.9 = (f32[2,128,384]{2,1,0:T(8,128)S(1)}, f32[2,128,384]{2,1,0:T(8,128)S(1)}, u32[]{:S(2)}, u32[]{:S(2)}) collective-permute-start(f32[2,128,384]{2,1,0:T(8,128)S(1)} %get-tuple-element.83), channel_id=1, source_target_pairs={{0,4},{1,5},{2,6},{3,7},{4,8},{5,9},{6,10},{7,11},{8,12},{9,13},{1... | collective-permute-start | bytes 1179656 | tf_op jit(solution)/shard_map/ppermute | solution.py:594
  46.2 21.6 %collective-permute-start.10 = (f32[2,128,384]{2,1,0:T(8,128)S(1)}, f32[2,128,384]{2,1,0:T(8,128)S(1)}, u32[]{:S(2)}, u32[]{:S(2)}) collective-permute-start(f32[2,128,384]{2,1,0:T(8,128)S(1)} %get-tuple-element.86), channel_id=1, source_target_pairs={{0,2},{1,3},{2,0},{3,1},{4,6},{5,7},{6,4},{7,5},{8,10},{9,11},{10,... | collective-permute-start | bytes 1179656 | tf_op jit(solution)/shard_map/ppermute | solution.py:594
  61.0 9.2 %collective-permute-start.14 = (f32[520,128]{1,0:T(8,128)S(1)}, f32[520,128]{1,0:T(8,128)S(1)}, u32[]{:S(2)}, u32[]{:S(2)}) collective-permute-start(f32[520,128]{1,0:T(8,128)S(1)} %begin.1.rest_6_.rest_0_.w0_ref), channel_id=1, source_target_pairs={{0,2},{1,3},{2,0},{3,1},{4,6},{5,7},{6,4},{7,5},{8,10},{9,11},{10,... | collective-permute-start | bytes 798728 | tf_op jit(solution)/shard_map/ppermute | solution.py:594
  63.3 16.7 %collective-permute-start.13 = (f32[520,128]{1,0:T(8,128)S(1)}, f32[520,128]{1,0:T(8,128)S(1)}, u32[]{:S(2)}, u32[]{:S(2)}) collective-permute-start(f32[520,128]{1,0:T(8,128)S(1)} %begin.1.rest_6_.rest_0_.w0_ref), channel_id=1, source_target_pairs={{0,3},{1,0},{2,1},{3,2},{4,7},{5,4},{6,5},{7,6},{8,11},{9,8},{10,9... | collective-permute-start | bytes 798728 | tf_op jit(solution)/shard_map/ppermute | solution.py:594
  67.0 12.9 %collective-permute-start.12 = (f32[520,128]{1,0:T(8,128)S(1)}, f32[520,128]{1,0:T(8,128)S(1)}, u32[]{:S(2)}, u32[]{:S(2)}) collective-permute-start(f32[520,128]{1,0:T(8,128)S(1)} %begin.1.rest_6_.rest_0_.w0_ref), channel_id=1, source_target_pairs={{0,1},{1,2},{2,3},{3,0},{4,5},{5,6},{6,7},{7,4},{8,9},{9,10},{10,1... | collective-permute-start | bytes 798728 | tf_op jit(solution)/shard_map/ppermute | solution.py:594
  67.9 46.0 %collective-permute-start.11 = (f32[6,128,384]{2,1,0:T(8,128)S(1)}, f32[6,128,384]{2,1,0:T(8,128)S(1)}, u32[]{:S(2)}, u32[]{:S(2)}) collective-permute-start(f32[6,128,384]{2,1,0:T(8,128)S(1)} %pad_maximum_fusion), channel_id=1, source_target_pairs={{0,4},{1,5},{2,6},{3,7},{4,8},{5,9},{6,10},{7,11},{8,12},{9,13},{1... | collective-permute-start | bytes 3538952 | tf_op jit(solution)/shard_map/ppermute | solution.py:594
  80.0 33.9 %collective-permute-start.18 = (f32[2080,128]{1,0:T(8,128)S(1)}, f32[2080,128]{1,0:T(8,128)S(1)}, u32[]{:S(2)}, u32[]{:S(2)}) collective-permute-start(f32[2080,128]{1,0:T(8,128)S(1)} %pad_maximum_fusion.1), channel_id=1, source_target_pairs={{0,4},{1,5},{2,6},{3,7},{4,0},{5,1},{6,2},{7,3},{8,12},{9,13},{10,... | collective-permute-start | bytes 3194888 | tf_op jit(solution)/shard_map/ppermute | solution.py:598
  80.1 12.8 %collective-permute-start.4 = (f32[2,128,384]{2,1,0:T(8,128)S(1)}, f32[2,128,384]{2,1,0:T(8,128)S(1)}, u32[]{:S(2)}, u32[]{:S(2)}) collective-permute-start(f32[2,128,384]{2,1,0:T(8,128)S(1)} %get-tuple-element.77), channel_id=1, source_target_pairs={{0,1},{1,2},{2,3},{3,0},{4,5},{5,6},{6,7},{7,4},{8,9},{9,10},{10,1... | collective-permute-start | bytes 1179656 | tf_op jit(solution)/shard_map/ppermute | solution.py:594
  80.6 21.3 %collective-permute-start.5 = (f32[2,128,384]{2,1,0:T(8,128)S(1)}, f32[2,128,384]{2,1,0:T(8,128)S(1)}, u32[]{:S(2)}, u32[]{:S(2)}) collective-permute-start(f32[2,128,384]{2,1,0:T(8,128)S(1)} %get-tuple-element.78), channel_id=1, source_target_pairs={{0,2},{1,3},{2,0},{3,1},{4,6},{5,7},{6,4},{7,5},{8,10},{9,11},{10,... | collective-permute-start | bytes 1179656 | tf_op jit(solution)/shard_map/ppermute | solution.py:594
  84.3 19.5 %collective-permute-start.6 = (f32[2,128,384]{2,1,0:T(8,128)S(1)}, f32[2,128,384]{2,1,0:T(8,128)S(1)}, u32[]{:S(2)}, u32[]{:S(2)}) collective-permute-start(f32[2,128,384]{2,1,0:T(8,128)S(1)} %get-tuple-element.79), channel_id=1, source_target_pairs={{0,3},{1,0},{2,1},{3,2},{4,7},{5,4},{6,5},{7,6},{8,11},{9,8},{10,9... | collective-permute-start | bytes 1179656 | tf_op jit(solution)/shard_map/ppermute | solution.py:594
  92.9 21.1 %collective-permute-start.16 = (f32[1040,128]{1,0:T(8,128)S(1)}, f32[1040,128]{1,0:T(8,128)S(1)}, u32[]{:S(2)}, u32[]{:S(2)}) collective-permute-start(f32[1040,128]{1,0:T(8,128)S(1)} %pad_maximum_fusion.4), channel_id=1, source_target_pairs={{0,124},{1,125},{2,126},{3,127},{4,8},{5,9},{6,10},{7,11},{8,4},{9... | collective-permute-start | bytes 1597448 | tf_op jit(solution)/shard_map/ppermute | solution.py:598
  101.9 9.2 %collective-permute-start.15 = (f32[520,128]{1,0:T(8,128)S(1)}, f32[520,128]{1,0:T(8,128)S(1)}, u32[]{:S(2)}, u32[]{:S(2)}) collective-permute-start(f32[520,128]{1,0:T(8,128)S(1)} %begin.1.rest_6_.rest_0_.w0_ref), channel_id=1, source_target_pairs={{0,124},{1,125},{2,126},{3,127},{4,8},{5,9},{6,10},{7,11},{8,4},{9... | collective-permute-start | bytes 798728 | tf_op jit(solution)/shard_map/ppermute | solution.py:598
  103.7 10.2 %collective-permute-start.17 = (f32[520,128]{1,0:T(8,128)S(1)}, f32[520,128]{1,0:T(8,128)S(1)}, u32[]{:S(2)}, u32[]{:S(2)}) collective-permute-start(f32[520,128]{1,0:T(8,128)S(1)} %collective-permute-done.14.rest_9_.rest_3_), channel_id=1, source_target_pairs={{0,124},{1,125},{2,126},{3,127},{4,8},{5,9},{6,10},{7,11},{8,4},{9... | collective-permute-start | bytes 798728 | tf_op jit(solution)/shard_map/ppermute | solution.py:598
  116.5 9.8 %collective-permute-start.21 = (f32[520,128]{1,0:T(8,128)S(1)}, f32[520,128]{1,0:T(8,128)S(1)}, u32[]{:S(2)}, u32[]{:S(2)}) collective-permute-start(f32[520,128]{1,0:T(8,128)S(1)} %get-tuple-element.89.rest_6_.rest_8_.w1_ref), channel_id=1, source_target_pairs={{0,2},{1,3},{2,0},{3,1},{4,6},{5,7},{6,4},{7,5},{8,10},{9,11},{10,... | collective-permute-start | bytes 798728 | tf_op jit(solution)/shard_map/ppermute | solution.py:594
  116.6 9.7 %collective-permute-start.20 = (f32[520,128]{1,0:T(8,128)S(1)}, f32[520,128]{1,0:T(8,128)S(1)}, u32[]{:S(2)}, u32[]{:S(2)}) collective-permute-start(f32[520,128]{1,0:T(8,128)S(1)} %get-tuple-element.89.rest_6_.rest_8_.w1_ref), channel_id=1, source_target_pairs={{0,3},{1,0},{2,1},{3,2},{4,7},{5,4},{6,5},{7,6},{8,11},{9,8},{10,9... | collective-permute-start | bytes 798728 | tf_op jit(solution)/shard_map/ppermute | solution.py:594
  116.7 12.3 %collective-permute-start.19 = (f32[520,128]{1,0:T(8,128)S(1)}, f32[520,128]{1,0:T(8,128)S(1)}, u32[]{:S(2)}, u32[]{:S(2)}) collective-permute-start(f32[520,128]{1,0:T(8,128)S(1)} %get-tuple-element.89.rest_6_.rest_8_.w1_ref), channel_id=1, source_target_pairs={{0,1},{1,2},{2,3},{3,0},{4,5},{5,6},{6,7},{7,4},{8,9},{9,10},{10,1... | collective-permute-start | bytes 798728 | tf_op jit(solution)/shard_map/ppermute | solution.py:594
  129.1 9.5 %collective-permute-start.22 = (f32[2080,128]{1,0:T(8,128)S(1)}, f32[2080,128]{1,0:T(8,128)S(1)}, u32[]{:S(2)}, u32[]{:S(2)}) collective-permute-start(f32[2080,128]{1,0:T(8,128)S(1)} %pad_maximum_fusion.2), channel_id=1, source_target_pairs={{0,4},{1,5},{2,6},{3,7},{4,0},{5,1},{6,2},{7,3},{8,12},{9,13},{10,... | collective-permute-start | bytes 3194888 | tf_op jit(solution)/shard_map/ppermute | solution.py:598
  129.2 17.8 %collective-permute-start.26 = (f32[1040,128]{1,0:T(8,128)S(1)}, f32[1040,128]{1,0:T(8,128)S(1)}, u32[]{:S(2)}, u32[]{:S(2)}) collective-permute-start(f32[1040,128]{1,0:T(8,128)S(1)} %pad_maximum_fusion.5), channel_id=1, source_target_pairs={{0,124},{1,125},{2,126},{3,127},{4,8},{5,9},{6,10},{7,11},{8,4},{9... | collective-permute-start | bytes 1597448 | tf_op jit(solution)/shard_map/ppermute | solution.py:598
  133.5 10.7 %collective-permute-start.25 = (f32[520,128]{1,0:T(8,128)S(1)}, f32[520,128]{1,0:T(8,128)S(1)}, u32[]{:S(2)}, u32[]{:S(2)}) collective-permute-start(f32[520,128]{1,0:T(8,128)S(1)} %get-tuple-element.89.rest_6_.rest_8_.w1_ref), channel_id=1, source_target_pairs={{0,124},{1,125},{2,126},{3,127},{4,8},{5,9},{6,10},{7,11},{8,4},{9... | collective-permute-start | bytes 798728 | tf_op jit(solution)/shard_map/ppermute | solution.py:598
  134.4 12.7 %collective-permute-start.27 = (f32[520,128]{1,0:T(8,128)S(1)}, f32[520,128]{1,0:T(8,128)S(1)}, u32[]{:S(2)}, u32[]{:S(2)}) collective-permute-start(f32[520,128]{1,0:T(8,128)S(1)} %collective-permute-done.21.rest_9_.rest_11_), channel_id=1, source_target_pairs={{0,124},{1,125},{2,126},{3,127},{4,8},{5,9},{6,10},{7,11},{8,4},{9... | collective-permute-start | bytes 798728 | tf_op jit(solution)/shard_map/ppermute | solution.py:598
  147.0 31.7 %copy-start.2 = (bf16[4,1024,512]{2,1,0:T(8,128)(2,1)S(1)}, bf16[4,1024,512]{2,1,0:T(8,128)(2,1)}, u32[]{:S(2)}) copy-start(bf16[4,1024,512]{2,1,0:T(8,128)(2,1)} %get-tuple-element.60.refs_4_.solved_ref) | copy-start | bytes 12582916
  150.0 10.2 %collective-permute-start.28 = (f32[520,128]{1,0:T(8,128)S(1)}, f32[520,128]{1,0:T(8,128)S(1)}, u32[]{:S(2)}, u32[]{:S(2)}) collective-permute-start(f32[520,128]{1,0:T(8,128)S(1)} %get-tuple-element.92.rest_6_), channel_id=1, source_target_pairs={{0,2},{1,3},{2,0},{3,1},{4,6},{5,7},{6,4},{7,5},{8,10},{9,11},{10,... | collective-permute-start | bytes 798728 | tf_op jit(solution)/shard_map/ppermute | solution.py:594
  150.3 10.7 %collective-permute-start.31 = (f32[520,128]{1,0:T(8,128)S(1)}, f32[520,128]{1,0:T(8,128)S(1)}, u32[]{:S(2)}, u32[]{:S(2)}) collective-permute-start(f32[520,128]{1,0:T(8,128)S(1)} %get-tuple-element.92.rest_6_), channel_id=1, source_target_pairs={{0,3},{1,0},{2,1},{3,2},{4,7},{5,4},{6,5},{7,6},{8,11},{9,8},{10,9... | collective-permute-start | bytes 798728 | tf_op jit(solution)/shard_map/ppermute | solution.py:594
  151.5 11.5 %collective-permute-start.30 = (f32[520,128]{1,0:T(8,128)S(1)}, f32[520,128]{1,0:T(8,128)S(1)}, u32[]{:S(2)}, u32[]{:S(2)}) collective-permute-start(f32[520,128]{1,0:T(8,128)S(1)} %get-tuple-element.92.rest_6_), channel_id=1, source_target_pairs={{0,1},{1,2},{2,3},{3,0},{4,5},{5,6},{6,7},{7,4},{8,9},{9,10},{10,1... | collective-permute-start | bytes 798728 | tf_op jit(solution)/shard_map/ppermute | solution.py:594
  152.3 1.2 collective-permute-start.23
  153.5 3.6 %collective-permute-start.24 = (f32[8,128]{1,0:T(8,128)S(1)}, f32[8,128]{1,0:T(8,128)S(1)}, u32[]{:S(2)}, u32[]{:S(2)}) collective-permute-start(f32[8,128]{1,0:T(8,128)S(1)} %add.41), channel_id=1, source_target_pairs={{0,8},{1,9},{2,10},{3,11},{4,12},{5,13},{6,14},{7,15},{8,0},{9,1},... | collective-permute-start | bytes 12296 | tf_op jit(solution)/shard_map/ppermute | solution.py:598
  163.0 8.3 %collective-permute-start.32 = (f32[2080,128]{1,0:T(8,128)S(1)}, f32[2080,128]{1,0:T(8,128)S(1)}, u32[]{:S(2)}, u32[]{:S(2)}) collective-permute-start(f32[2080,128]{1,0:T(8,128)S(1)} %pad_maximum_fusion.3), channel_id=1, source_target_pairs={{0,4},{1,5},{2,6},{3,7},{4,0},{5,1},{6,2},{7,3},{8,12},{9,13},{10,... | collective-permute-start | bytes 3194888 | tf_op jit(solution)/shard_map/ppermute | solution.py:598
  163.1 8.2 %collective-permute-start.29 = (f32[8,128]{1,0:T(8,128)S(1)}, f32[8,128]{1,0:T(8,128)S(1)}, u32[]{:S(2)}, u32[]{:S(2)}) collective-permute-start(f32[8,128]{1,0:T(8,128)S(1)} %add.42), channel_id=1, source_target_pairs={{0,16},{1,17},{2,18},{3,19},{4,20},{5,21},{6,22},{7,23},{8,24},{9,... | collective-permute-start | bytes 12296 | tf_op jit(solution)/shard_map/ppermute | solution.py:598
  166.2 15.9 %collective-permute-start.35 = (f32[520,128]{1,0:T(8,128)S(1)}, f32[520,128]{1,0:T(8,128)S(1)}, u32[]{:S(2)}, u32[]{:S(2)}) collective-permute-start(f32[520,128]{1,0:T(8,128)S(1)} %get-tuple-element.92.rest_6_), channel_id=1, source_target_pairs={{0,124},{1,125},{2,126},{3,127},{4,8},{5,9},{6,10},{7,11},{8,4},{9... | collective-permute-start | bytes 798728 | tf_op jit(solution)/shard_map/ppermute | solution.py:598
  169.0 13.1 %collective-permute-start.37 = (f32[520,128]{1,0:T(8,128)S(1)}, f32[520,128]{1,0:T(8,128)S(1)}, u32[]{:S(2)}, u32[]{:S(2)}) collective-permute-start(f32[520,128]{1,0:T(8,128)S(1)} %collective-permute-done.28.rest_9_), channel_id=1, source_target_pairs={{0,124},{1,125},{2,126},{3,127},{4,8},{5,9},{6,10},{7,11},{8,4},{9... | collective-permute-start | bytes 798728 | tf_op jit(solution)/shard_map/ppermute | solution.py:598
  171.3 4.8 %collective-permute-start.33 = (f32[8,128]{1,0:T(8,128)S(1)}, f32[8,128]{1,0:T(8,128)S(1)}, u32[]{:S(2)}, u32[]{:S(2)}) collective-permute-start(f32[8,128]{1,0:T(8,128)S(1)} %add.43), channel_id=1, source_target_pairs={{0,32},{1,33},{2,34},{3,35},{4,36},{5,37},{6,38},{7,39},{8,40},{9,... | collective-permute-start | bytes 12296 | tf_op jit(solution)/shard_map/ppermute | solution.py:598
  171.7 12.3 %collective-permute-start.36 = (f32[1040,128]{1,0:T(8,128)S(1)}, f32[1040,128]{1,0:T(8,128)S(1)}, u32[]{:S(2)}, u32[]{:S(2)}) collective-permute-start(f32[1040,128]{1,0:T(8,128)S(1)} %pad_maximum_fusion.6), channel_id=1, source_target_pairs={{0,124},{1,125},{2,126},{3,127},{4,8},{5,9},{6,10},{7,11},{8,4},{9... | collective-permute-start | bytes 1597448 | tf_op jit(solution)/shard_map/ppermute | solution.py:598
  176.1 6.0 %collective-permute-start.34 = (f32[8,128]{1,0:T(8,128)S(1)}, f32[8,128]{1,0:T(8,128)S(1)}, u32[]{:S(2)}, u32[]{:S(2)}) collective-permute-start(f32[8,128]{1,0:T(8,128)S(1)} %add.44), channel_id=1, source_target_pairs={{0,64},{1,65},{2,66},{3,67},{4,68},{5,69},{6,70},{7,71},{8,72},{9,... | collective-permute-start | bytes 12296 | tf_op jit(solution)/shard_map/ppermute | solution.py:598
  178.7 5.3 %copy-start.3 = (f32[4,512,128]{2,1,0:T(8,128)S(1)}, f32[4,512,128]{2,1,0:T(8,128)}, u32[]{:S(2)}) copy-start(f32[4,512,128]{2,1,0:T(8,128)} %get-tuple-element.96.reduced_ref) | copy-start | bytes 3145732

commit v5 on v4

--- a/solution.py
+++ b/solution.py
@@ -611,20 +611,18 @@
     def around(chunks):
         return [chunks[0]] + [shift(chunks[turn], 0, turn) for turn in range(1, n_sub)]
 
-    def spread(v, small=None, steps=((), ())):
+    def spread(v, small=None, steps=()):
         z1, z3, z2 = (shift(v, 0, turn) for turn in (1, 3, 2))
         if small is None:
             small = sum(x[SEP_DEV * TILE :] for x in (v, z1, z3, z2))
         pair = jnp.concatenate([z1, z3], axis=0)
         pair_across = across(pair)
-        if steps[0]:
-            small, z2 = lax.optimization_barrier((small, z2))
-            small = add_over(small, steps[0])
         z2_across = across(z2)
         all_mate = mate(jnp.concatenate([v, z1, z3, z2], axis=0))
-        if steps[1]:
+        if steps:
+            small, _ = lax.optimization_barrier((small, z2))
+            small = add_over(small, steps)
             small, all_mate = lax.optimization_barrier((small, all_mate))
-            small = add_over(small, steps[1])
         return [v, z1, z3, z2, across(v), pair_across, z2_across, all_mate], small
 
     per_region = n_sub * SUB_DEV
@@ -649,9 +647,9 @@
     w0s, _ = spread(w0, u0[0, :NORM_ROWS])
     offs = around(offs[:4]) + [straight, forwarded]
     u1, w1 = apply(target, seen, inv, offs, w0s)
-    w1s, norms = spread(w1, None, ((), (1, 2)))
+    w1s, norms = spread(w1, None, (1, 2))
     u2, w2 = apply(target, seen, inv, offs, w1s)
-    w2s, norms = spread(w2, norms, ((4,), (8, 16)))
+    w2s, norms = spread(w2, norms, (4, 8, 16))
     ya, yb = ahead(own, solved, w0s, w1s)
     return finish(target, seen, own, norms, solved, reduced, ya, yb, u1, w0, w1, offs, w2s)
 

time: 189 us -> 190 us (level)
    ppermute x21, waiting for transfers between devices: 53.7 us -> 58.6 us  [shift(): return lax.ppermute(x, both, pairs)]
    ppermute x17, waiting for transfers between devices: 23.8 us -> 20.3 us  [swap(): return lax.ppermute(x, both, pairs)]
  transfers between devices with their start and end apart: 38 -> 38, of which waited for: 19 -> 17; matrix products, arithmetic and copies ran while one was open for 0% -> 0% of each run, Pallas kernels for 12% -> 12%
where the time goes in v5:
time: 190 us; the launch traced here: 189 us
  waiting for transfers between devices  78.9 us (42%)
  starting transfers between devices  57.4 us (30%)
  Pallas kernels  48.1 us (25%)
  local copies, waits for them, and re-layouts  3.71 us (2%)
    ppermute x21, waiting for transfers between devices, shift(): return lax.ppermute(x, both, pairs)  58.6 us
    ppermute x17, starting transfers between devices, swap(): return lax.ppermute(x, both, pairs)  29.7 us
    ppermute x21, starting transfers between devices, shift(): return lax.ppermute(x, both, pairs)  27.7 us
    ppermute x17, waiting for transfers between devices, swap(): return lax.ppermute(x, both, pairs)  20.3 us
    pallas_call x1, Pallas kernels, eliminate(): pl.pallas_call(lambda *refs: eliminate_kernel(n_region, n_sub, *refs), gr...  14.9 us
    pallas_call x1, Pallas kernels, invert(): pl.pallas_call(invert_kernel, out_shape=(jax.ShapeDtypeStruct((SEP_DEV, 2...  8.04 us
    pallas_call x2, Pallas kernels, apply(): pl.pallas_call(apply_kernel, out_shape=(tile, WIDE), in_specs=[SMEM] * 2...  5.53 us
    pallas_call x1, Pallas kernels, couple(): pl.pallas_call(lambda *refs: couple_kernel(n_region, n_sub, *refs), grid=...  5.39 us
  transfers between devices with their start and end apart: 38, of which 17 were waited for; matrix products, arithmetic and copies ran while one was open for 0% of the time, Pallas kernels for 12%

profile of v5, /device:TPU:0, one launch (start us, length us, event | category | flops | bytes accessed | tf_op | source)
XLA Modules:
  0.0 189.5 jit_solution(5747435629448233587)
XLA Ops:
  0.7 0.8 constant_dynamic-slice_fusion.1
  1.5 0.1 copy.12
  1.6 0.6 reshape.9.refs_0_
  2.2 14.9 %eliminate.1 = (bf16[4,1024,512]{2,1,0:T(8,128)(2,1)}, f32[4,512,128]{2,1,0:T(8,128)}, f32[4,200,128]{2,1,0:T(8,128)}, f32[4,200,128]{2,1,0:T(8,128)}, f32[4,200,128]{2,1,0:T(8,128)}, /*index=5*/f32[4,200,128]{2,1,0:T(8,128)}) custom-call(s32[128]{0:T(128)} %reshape.9.refs_0_, s32[512]{0:T(512)} %refs_1_.5, s32[512]{0:T(512)} %refs_2_.3, ...), custom_call_target="tpu_custom_call" | custom-call | tf_op jit(solution)/shard_map/eliminate/pallas_call | solution.py:235
  17.1 2.1 %collective-permute-start = (f32[4,200,128]{2,1,0:T(8,128)}, f32[4,200,128]{2,1,0:T(8,128)S(1)}, u32[]{:S(2)}, u32[]{:S(2)}) collective-permute-start(f32[4,200,128]{2,1,0:T(8,128)} %get-tuple-element.57), channel_id=1, source_target_pairs={{0,1},{1,2},{2,3},{3,0},{4,5},{5,6},{6,7},{7,4},{8,9},{9,10},{10,1... | collective-permute-start | bytes 1228808 | tf_op jit(solution)/shard_map/ppermute | solution.py:594
  19.2 3.6 %collective-permute-start.1 = (f32[4,200,128]{2,1,0:T(8,128)}, f32[4,200,128]{2,1,0:T(8,128)S(1)}, u32[]{:S(2)}, u32[]{:S(2)}) collective-permute-start(f32[4,200,128]{2,1,0:T(8,128)} %get-tuple-element.58), channel_id=1, source_target_pairs={{0,2},{1,3},{2,0},{3,1},{4,6},{5,7},{6,4},{7,5},{8,10},{9,11},{10,... | collective-permute-start | bytes 1228808 | tf_op jit(solution)/shard_map/ppermute | solution.py:594
  22.8 1.0 collective-permute-start.2
  23.8 2.2 %copy-done.1 = bf16[4,1024,512]{2,1,0:T(8,128)(2,1)S(1)} copy-done((bf16[4,1024,512]{2,1,0:T(8,128)(2,1)S(1)}, bf16[4,1024,512]{2,1,0:T(8,128)(2,1)}, u32[]{:S(2)}) %copy-start.1) | copy-done | bytes 4194328
  26.0 5.4 %couple.1 = (f32[2,128,384]{2,1,0:T(8,128)S(1)}, f32[2,128,384]{2,1,0:T(8,128)S(1)}, f32[2,128,384]{2,1,0:T(8,128)S(1)}, f32[2,128,384]{2,1,0:T(8,128)S(1)}, f32...) custom-call(s32[128]{0:T(128)S(1)} %copy-done.7, ...), custom_call_target="tpu_custom_call" | custom-call | flops 8000000000 | bytes 12582912 | tf_op jit(solution)/shard_map/couple/pallas_call | solution.py:302
  31.4 5.2 %plan.1 = (s32[16]{0:T(128)S(1)}, s32[48]{0:T(128)S(1)}, s32[16]{0:T(128)S(1)}, s32[8]{0:T(128)S(1)}) custom-call(s32[128]{0:T(128)S(1)} %copy-done.7, s32[512]{0:T(512)S(1)} %copy-done.6), custom_call_target="tpu_custom_call" | custom-call | flops 2000000000 | bytes 8192 | tf_op jit(solution)/shard_map/plan/pallas_call | solution.py:146
  36.7 4.4 %collective-permute-done.1.c2 = f32[4,200,128]{2,1,0:T(8,128)S(1)} collective-permute-done((f32[4,200,128]{2,1,0:T(8,128)}, f32[4,200,128]{2,1,0:T(8,128)S(1)}, u32[]{:S(2)}, u32[]{:S(2)}) %collective-permute-start.1) | collective-permute-done | bytes 409632 | tf_op jit(solution)/shard_map/ppermute | solution.py:594
  41.0 0.8 gather.1
  41.9 1.3 collective-permute-start.7
  43.2 2.0 %collective-permute-start.8 = (f32[2,128,384]{2,1,0:T(8,128)S(1)}, f32[2,128,384]{2,1,0:T(8,128)S(1)}, u32[]{:S(2)}, u32[]{:S(2)}) collective-permute-start(f32[2,128,384]{2,1,0:T(8,128)S(1)} %get-tuple-element.82), channel_id=1, source_target_pairs={{0,3},{1,0},{2,1},{3,2},{4,7},{5,4},{6,5},{7,6},{8,11},{9,8},{10,9... | collective-permute-start | bytes 1179656 | tf_op jit(solution)/shard_map/ppermute | solution.py:594
  45.2 1.1 collective-permute-start.9
  46.3 1.0 collective-permute-start.10
  47.3 5.3 %collective-permute-done.3.got_ref = f32[4,200,128]{2,1,0:T(8,128)S(1)} collective-permute-done((f32[4,200,128]{2,1,0:T(8,128)S(1)}, f32[4,200,128]{2,1,0:T(8,128)S(1)}, u32[]{:S(2)}, u32[]{:S(2)}) %collective-permute-start.3) | collective-permute-done | bytes 409632 | tf_op jit(solution)/shard_map/ppermute | solution.py:594
  52.6 8.0 %invert.1 = (bf16[4,256,128]{2,1,0:T(8,128)(2,1)S(1)}, f32[4,128,128]{2,1,0:T(8,128)S(1)}) custom-call(f32[4,128,128]{2,1,0:T(8,128)S(1)} %copy-done.8, f32[4,128,128]{2,1,0:T(8,128)S(1)} %copy-done.9, f32[4,200,128]{2,1,0:T(8,128)S(1)} %get-tuple-element.73.here_ref, f32[4,200,128]{2,1,0:T(8,128)S(1)} %collective-permute-done.3.got_ref), custom_call_target="tpu_custom_call" | custom-call | flops 10000000000 | bytes 4194304 | tf_op jit(solution)/shard_map/invert/pallas_call | solution.py:430
  60.7 0.3 begin.1.rest_6_.rest_0_.w0_ref
  61.0 2.3 %collective-permute-start.14 = (f32[520,128]{1,0:T(8,128)S(1)}, f32[520,128]{1,0:T(8,128)S(1)}, u32[]{:S(2)}, u32[]{:S(2)}) collective-permute-start(f32[520,128]{1,0:T(8,128)S(1)} %begin.1.rest_6_.rest_0_.w0_ref), channel_id=1, source_target_pairs={{0,2},{1,3},{2,0},{3,1},{4,6},{5,7},{6,4},{7,5},{8,10},{9,11},{10,... | collective-permute-start | bytes 798728 | tf_op jit(solution)/shard_map/ppermute | solution.py:594
  63.3 3.7 %collective-permute-start.13 = (f32[520,128]{1,0:T(8,128)S(1)}, f32[520,128]{1,0:T(8,128)S(1)}, u32[]{:S(2)}, u32[]{:S(2)}) collective-permute-start(f32[520,128]{1,0:T(8,128)S(1)} %begin.1.rest_6_.rest_0_.w0_ref), channel_id=1, source_target_pairs={{0,3},{1,0},{2,1},{3,2},{4,7},{5,4},{6,5},{7,6},{8,11},{9,8},{10,9... | collective-permute-start | bytes 798728 | tf_op jit(solution)/shard_map/ppermute | solution.py:594
  67.0 0.8 collective-permute-start.12
  67.8 0.1 pad_maximum_fusion
  68.0 2.2 %collective-permute-done.14.rest_9_.rest_3_ = f32[520,128]{1,0:T(8,128)S(1)} collective-permute-done((f32[520,128]{1,0:T(8,128)S(1)}, f32[520,128]{1,0:T(8,128)S(1)}, u32[]{:S(2)}, u32[]{:S(2)}) %collective-permute-start.14) | collective-permute-done | bytes 266272 | tf_op jit(solution)/shard_map/ppermute | solution.py:594
  70.1 9.8 %collective-permute-done.13.rest_8_.rest_2_ = f32[520,128]{1,0:T(8,128)S(1)} collective-permute-done((f32[520,128]{1,0:T(8,128)S(1)}, f32[520,128]{1,0:T(8,128)S(1)}, u32[]{:S(2)}, u32[]{:S(2)}) %collective-permute-start.13) | collective-permute-done | bytes 266272 | tf_op jit(solution)/shard_map/ppermute | solution.py:594
  80.0 0.1 collective-permute-start.18
  80.1 0.5 collective-permute-start.4
  80.6 3.6 %collective-permute-start.5 = (f32[2,128,384]{2,1,0:T(8,128)S(1)}, f32[2,128,384]{2,1,0:T(8,128)S(1)}, u32[]{:S(2)}, u32[]{:S(2)}) collective-permute-start(f32[2,128,384]{2,1,0:T(8,128)S(1)} %get-tuple-element.78), channel_id=1, source_target_pairs={{0,2},{1,3},{2,0},{3,1},{4,6},{5,7},{6,4},{7,5},{8,10},{9,11},{10,... | collective-permute-start | bytes 1179656 | tf_op jit(solution)/shard_map/ppermute | solution.py:594
  84.3 8.6 %collective-permute-done.4.rest_1_ = f32[2,128,384]{2,1,0:T(8,128)S(1)} collective-permute-done((f32[2,128,384]{2,1,0:T(8,128)S(1)}, f32[2,128,384]{2,1,0:T(8,128)S(1)}, u32[]{:S(2)}, u32[]{:S(2)}) %collective-permute-start.4) | collective-permute-done | bytes 393248 | tf_op jit(solution)/shard_map/ppermute | solution.py:594
  92.9 1.8 collective-permute-start.16
  94.7 7.2 %collective-permute-done.5.rest_2_ = f32[2,128,384]{2,1,0:T(8,128)S(1)} collective-permute-done((f32[2,128,384]{2,1,0:T(8,128)S(1)}, f32[2,128,384]{2,1,0:T(8,128)S(1)}, u32[]{:S(2)}, u32[]{:S(2)}) %collective-permute-start.5) | collective-permute-done | bytes 393248 | tf_op jit(solution)/shard_map/ppermute | solution.py:594
  101.9 1.8 collective-permute-start.15
  103.7 3.2 %collective-permute-start.17 = (f32[520,128]{1,0:T(8,128)S(1)}, f32[520,128]{1,0:T(8,128)S(1)}, u32[]{:S(2)}, u32[]{:S(2)}) collective-permute-start(f32[520,128]{1,0:T(8,128)S(1)} %collective-permute-done.14.rest_9_.rest_3_), channel_id=1, source_target_pairs={{0,124},{1,125},{2,126},{3,127},{4,8},{5,9},{6,10},{7,11},{8,4},{9... | collective-permute-start | bytes 798728 | tf_op jit(solution)/shard_map/ppermute | solution.py:598
  107.0 4.1 %collective-permute-done.15.rest_10_.rest_4_ = f32[520,128]{1,0:T(8,128)S(1)} collective-permute-done((f32[520,128]{1,0:T(8,128)S(1)}, f32[520,128]{1,0:T(8,128)S(1)}, u32[]{:S(2)}, u32[]{:S(2)}) %collective-permute-start.15) | collective-permute-done | bytes 266272 | tf_op jit(solution)/shard_map/ppermute | solution.py:598
  111.1 2.9 %collective-permute-done.17.rest_12_.rest_6_ = f32[520,128]{1,0:T(8,128)S(1)} collective-permute-done((f32[520,128]{1,0:T(8,128)S(1)}, f32[520,128]{1,0:T(8,128)S(1)}, u32[]{:S(2)}, u32[]{:S(2)}) %collective-permute-start.17) | collective-permute-done | bytes 266272 | tf_op jit(solution)/shard_map/ppermute | solution.py:598
  113.9 2.6 %apply.2 = (f32[4,128,128]{2,1,0:T(8,128)S(1)}, f32[520,128]{1,0:T(8,128)S(1)}) custom-call(s32[16]{0:T(128)S(1)} %get-tuple-element.52.target_ref, s32[48]{0:T(128)S(1)} %get-tuple-element.53.seen_ref, bf16[4,256,128]{2,1,0:T(8,128)(2,1)S(1)} %get-tuple-element.75.inv_ref, f32[2,128,384]{2,1,0:T(8,128)S(1)} %get-tuple-element.76.rest_0_, ...), custom_call_target="tpu_custom_call" | custom-call | flops 2000000000 | bytes 7340032 | tf_op jit(solution)/shard_map/apply/pallas_call | solution.py:499
  116.5 0.1 collective-permute-start.21
  116.7 2.0 %collective-permute-start.19 = (f32[520,128]{1,0:T(8,128)S(1)}, f32[520,128]{1,0:T(8,128)S(1)}, u32[]{:S(2)}, u32[]{:S(2)}) collective-permute-start(f32[520,128]{1,0:T(8,128)S(1)} %get-tuple-element.89.rest_6_.rest_8_.w1_ref), channel_id=1, source_target_pairs={{0,1},{1,2},{2,3},{3,0},{4,5},{5,6},{6,7},{7,4},{8,9},{9,10},{10,1... | collective-permute-start | bytes 798728 | tf_op jit(solution)/shard_map/ppermute | solution.py:594
  118.7 7.6 %collective-permute-done.21.rest_9_.rest_11_ = f32[520,128]{1,0:T(8,128)S(1)} collective-permute-done((f32[520,128]{1,0:T(8,128)S(1)}, f32[520,128]{1,0:T(8,128)S(1)}, u32[]{:S(2)}, u32[]{:S(2)}) %collective-permute-start.21) | collective-permute-done | bytes 266272 | tf_op jit(solution)/shard_map/ppermute | solution.py:594
  126.3 2.7 %collective-permute-done.19.rest_7_.rest_9_ = f32[520,128]{1,0:T(8,128)S(1)} collective-permute-done((f32[520,128]{1,0:T(8,128)S(1)}, f32[520,128]{1,0:T(8,128)S(1)}, u32[]{:S(2)}, u32[]{:S(2)}) %collective-permute-start.19) | collective-permute-done | bytes 266272 | tf_op jit(solution)/shard_map/ppermute | solution.py:594
  129.1 0.1 collective-permute-start.24
  129.2 4.2 %collective-permute-start.26 = (f32[1040,128]{1,0:T(8,128)S(1)}, f32[1040,128]{1,0:T(8,128)S(1)}, u32[]{:S(2)}, u32[]{:S(2)}) collective-permute-start(f32[1040,128]{1,0:T(8,128)S(1)} %pad_maximum_fusion.5), channel_id=1, source_target_pairs={{0,124},{1,125},{2,126},{3,127},{4,8},{5,9},{6,10},{7,11},{8,4},{9... | collective-permute-start | bytes 1597448 | tf_op jit(solution)/shard_map/ppermute | solution.py:598
  133.5 0.9 collective-permute-start.25
  134.4 4.2 %collective-permute-start.27 = (f32[520,128]{1,0:T(8,128)S(1)}, f32[520,128]{1,0:T(8,128)S(1)}, u32[]{:S(2)}, u32[]{:S(2)}) collective-permute-start(f32[520,128]{1,0:T(8,128)S(1)} %collective-permute-done.21.rest_9_.rest_11_), channel_id=1, source_target_pairs={{0,124},{1,125},{2,126},{3,127},{4,8},{5,9},{6,10},{7,11},{8,4},{9... | collective-permute-start | bytes 798728 | tf_op jit(solution)/shard_map/ppermute | solution.py:598
  138.6 1.2 collective-permute-done.22
  139.7 4.7 %collective-permute-done.23 = f32[8,128]{1,0:T(8,128)S(1)} collective-permute-done((f32[8,128]{1,0:T(8,128)S(1)}, f32[8,128]{1,0:T(8,128)S(1)}, u32[]{:S(2)}, u32[]{:S(2)}) %collective-permute-start.23) | collective-permute-done | bytes 4128 | tf_op jit(solution)/shard_map/ppermute | solution.py:598
  144.5 2.5 %collective-permute-done.27.rest_12_.rest_14_ = f32[520,128]{1,0:T(8,128)S(1)} collective-permute-done((f32[520,128]{1,0:T(8,128)S(1)}, f32[520,128]{1,0:T(8,128)S(1)}, u32[]{:S(2)}, u32[]{:S(2)}) %collective-permute-start.27) | collective-permute-done | bytes 266272 | tf_op jit(solution)/shard_map/ppermute | solution.py:598
  147.1 3.0 %apply.3 = (f32[4,128,128]{2,1,0:T(8,128)}, f32[520,128]{1,0:T(8,128)S(1)}) custom-call(s32[16]{0:T(128)S(1)} %get-tuple-element.52.target_ref, s32[48]{0:T(128)S(1)} %get-tuple-element.53.seen_ref, bf16[4,256,128]{2,1,0:T(8,128)(2,1)S(1)} %get-tuple-element.75.inv_ref, f32[2,128,384]{2,1,0:T(8,128)S(1)} %get-tuple-element.76.rest_0_, ...), custom_call_target="tpu_custom_call" | custom-call | flops 2000000000 | bytes 7340032 | tf_op jit(solution)/shard_map/apply/pallas_call | solution.py:499
  150.0 0.6 collective-permute-start.33
  150.7 1.4 collective-permute-start.32
  152.0 0.3 collective-permute-start.28
  152.3 6.3 %collective-permute-done.33.rest_8_ = f32[520,128]{1,0:T(8,128)S(1)} collective-permute-done((f32[520,128]{1,0:T(8,128)S(1)}, f32[520,128]{1,0:T(8,128)S(1)}, u32[]{:S(2)}, u32[]{:S(2)}) %collective-permute-start.33) | collective-permute-done | bytes 266272 | tf_op jit(solution)/shard_map/ppermute | solution.py:594
  158.7 4.4 %collective-permute-done.32.rest_7_ = f32[520,128]{1,0:T(8,128)S(1)} collective-permute-done((f32[520,128]{1,0:T(8,128)S(1)}, f32[520,128]{1,0:T(8,128)S(1)}, u32[]{:S(2)}, u32[]{:S(2)}) %collective-permute-start.32) | collective-permute-done | bytes 266272 | tf_op jit(solution)/shard_map/ppermute | solution.py:594
  163.2 0.1 collective-permute-start.34
  163.3 2.8 %collective-permute-start.29 = (f32[8,128]{1,0:T(8,128)S(1)}, f32[8,128]{1,0:T(8,128)S(1)}, u32[]{:S(2)}, u32[]{:S(2)}) collective-permute-start(f32[8,128]{1,0:T(8,128)S(1)} %add.42), channel_id=1, source_target_pairs={{0,16},{1,17},{2,18},{3,19},{4,20},{5,21},{6,22},{7,23},{8,24},{9,... | collective-permute-start | bytes 12296 | tf_op jit(solution)/shard_map/ppermute | solution.py:598
  166.0 3.0 %collective-permute-start.35 = (f32[520,128]{1,0:T(8,128)S(1)}, f32[520,128]{1,0:T(8,128)S(1)}, u32[]{:S(2)}, u32[]{:S(2)}) collective-permute-start(f32[520,128]{1,0:T(8,128)S(1)} %get-tuple-element.93.rest_6_), channel_id=1, source_target_pairs={{0,124},{1,125},{2,126},{3,127},{4,8},{5,9},{6,10},{7,11},{8,4},{9... | collective-permute-start | bytes 798728 | tf_op jit(solution)/shard_map/ppermute | solution.py:598
  169.1 0.8 collective-permute-start.30
  169.9 3.3 %collective-permute-start.36 = (f32[1040,128]{1,0:T(8,128)S(1)}, f32[1040,128]{1,0:T(8,128)S(1)}, u32[]{:S(2)}, u32[]{:S(2)}) collective-permute-start(f32[1040,128]{1,0:T(8,128)S(1)} %pad_maximum_fusion.6), channel_id=1, source_target_pairs={{0,124},{1,125},{2,126},{3,127},{4,8},{5,9},{6,10},{7,11},{8,4},{9... | collective-permute-start | bytes 1597448 | tf_op jit(solution)/shard_map/ppermute | solution.py:598
  173.2 1.9 collective-permute-start.37
  175.1 1.6 collective-permute-start.31
  176.6 3.4 %ahead.1 = (f32[4,512,128]{2,1,0:T(8,128)S(1)}, f32[4,512,128]{2,1,0:T(8,128)S(1)}) custom-call(s32[16]{0:T(128)S(1)} %get-tuple-element.54.own_ref, bf16[4,1024,512]{2,1,0:T(8,128)(2,1)S(1)} %copy-done.2, f32[520,128]{1,0:T(8,128)S(1)} %begin.1.rest_6_.rest_0_.w0_ref, f32[520,128]{1,0:T(8,128)S(1)} %collective-permute-done.12.rest_7_.rest_1_, ...), custom_call_target="tpu_custom_call" | custom-call | flops 8000000000 | bytes 14680064 | tf_op jit(solution)/shard_map/ahead/pallas_call | solution.py:529
  180.1 0.1 collective-permute-done.31
  180.2 4.7 %collective-permute-done.37.rest_12_ = f32[520,128]{1,0:T(8,128)S(1)} collective-permute-done((f32[520,128]{1,0:T(8,128)S(1)}, f32[520,128]{1,0:T(8,128)S(1)}, u32[]{:S(2)}, u32[]{:S(2)}) %collective-permute-start.37) | collective-permute-done | bytes 266272 | tf_op jit(solution)/shard_map/ppermute | solution.py:598
  184.9 4.5 %finish.1 = (f32[4,512,128]{2,1,0:T(8,128)}, f32[4,128,128]{2,1,0:T(8,128)}, f32[4,128,128]{2,1,0:T(8,128)}) custom-call(s32[16]{0:T(128)S(1)} %get-tuple-element.52.target_ref, s32[48]{0:T(128)S(1)} %get-tuple-element.53.seen_ref, s32[16]{0:T(128)S(1)} %get-tuple-element.54.own_ref, f32[8,128]{1,0:T(8,128)S(1)} %add.45.norm_ref, ...), custom_call_target="tpu_custom_call" | custom-call | tf_op jit(solution)/shard_map/finish/pallas_call | solution.py:566
  (59 shorter events, 0.7 us)
Async XLA Ops:
  2.2 21.6 %copy-start = (f32[4,4,512,128]{3,2,1,0:T(8,128)S(1)}, f32[4,4,512,128]{3,2,1,0:T(8,128)}, u32[]{:S(2)}) copy-start(f32[4,4,512,128]{3,2,1,0:T(8,128)} %refs_3_.3) | copy-start | bytes 12582916
  2.2 21.6 %copy-start.5 = (s32[512]{0:T(512)S(1)}, s32[512]{0:T(512)}, u32[]{:S(2)}) copy-start(s32[512]{0:T(512)} %refs_2_.3) | copy-start | bytes 6148
  2.2 21.6 %copy-start.6 = (s32[512]{0:T(512)S(1)}, s32[512]{0:T(512)}, u32[]{:S(2)}) copy-start(s32[512]{0:T(512)} %refs_1_.5) | copy-start | bytes 6148
  2.2 21.6 %copy-start.7 = (s32[128]{0:T(128)S(1)}, s32[128]{0:T(128)}, u32[]{:S(2)}) copy-start(s32[128]{0:T(128)} %reshape.9.refs_0_) | copy-start | bytes 1540
  17.1 19.5 %collective-permute-start = (f32[4,200,128]{2,1,0:T(8,128)}, f32[4,200,128]{2,1,0:T(8,128)S(1)}, u32[]{:S(2)}, u32[]{:S(2)}) collective-permute-start(f32[4,200,128]{2,1,0:T(8,128)} %get-tuple-element.57), channel_id=1, source_target_pairs={{0,1},{1,2},{2,3},{3,0},{4,5},{5,6},{6,7},{7,4},{8,9},{9,10},{10,1... | collective-permute-start | bytes 1228808 | tf_op jit(solution)/shard_map/ppermute | solution.py:594
  19.2 21.8 %collective-permute-start.1 = (f32[4,200,128]{2,1,0:T(8,128)}, f32[4,200,128]{2,1,0:T(8,128)S(1)}, u32[]{:S(2)}, u32[]{:S(2)}) collective-permute-start(f32[4,200,128]{2,1,0:T(8,128)} %get-tuple-element.58), channel_id=1, source_target_pairs={{0,2},{1,3},{2,0},{3,1},{4,6},{5,7},{6,4},{7,5},{8,10},{9,11},{10,... | collective-permute-start | bytes 1228808 | tf_op jit(solution)/shard_map/ppermute | solution.py:594
  22.8 18.2 %collective-permute-start.2 = (f32[4,200,128]{2,1,0:T(8,128)}, f32[4,200,128]{2,1,0:T(8,128)S(1)}, u32[]{:S(2)}, u32[]{:S(2)}) collective-permute-start(f32[4,200,128]{2,1,0:T(8,128)} %get-tuple-element.59), channel_id=1, source_target_pairs={{0,3},{1,0},{2,1},{3,2},{4,7},{5,4},{6,5},{7,6},{8,11},{9,8},{10,9... | collective-permute-start | bytes 1228808 | tf_op jit(solution)/shard_map/ppermute | solution.py:594
  23.8 2.2 %copy-start.1 = (bf16[4,1024,512]{2,1,0:T(8,128)(2,1)S(1)}, bf16[4,1024,512]{2,1,0:T(8,128)(2,1)}, u32[]{:S(2)}) copy-start(bf16[4,1024,512]{2,1,0:T(8,128)(2,1)} %get-tuple-element.60.refs_4_.solved_ref) | copy-start | bytes 12582916
  31.4 9.6 %copy-start.4 = (f32[4,200,128]{2,1,0:T(8,128)S(1)}, f32[4,200,128]{2,1,0:T(8,128)}, u32[]{:S(2)}) copy-start(f32[4,200,128]{2,1,0:T(8,128)} %get-tuple-element.69.c0) | copy-start | bytes 1228804
  36.6 16.0 %copy-start.8 = (f32[4,128,128]{2,1,0:T(8,128)S(1)}, f32[4,128,128]{2,1,0:T(8,128)}, u32[]{:S(2)}) copy-start(f32[4,128,128]{2,1,0:T(8,128)} %hess_ref.1) | copy-start | bytes 786436
  36.6 16.0 %copy-start.9 = (f32[4,128,128]{2,1,0:T(8,128)S(1)}, f32[4,128,128]{2,1,0:T(8,128)}, u32[]{:S(2)}) copy-start(f32[4,128,128]{2,1,0:T(8,128)} %grad_ref.1) | copy-start | bytes 786436
  41.8 10.8 %collective-permute-start.3 = (f32[4,200,128]{2,1,0:T(8,128)S(1)}, f32[4,200,128]{2,1,0:T(8,128)S(1)}, u32[]{:S(2)}, u32[]{:S(2)}) collective-permute-start(f32[4,200,128]{2,1,0:T(8,128)S(1)} %get-tuple-element.74), channel_id=1, source_target_pairs={{0,4},{1,5},{2,6},{3,7},{4,8},{5,9},{6,10},{7,11},{8,12},{9,13},{1... | collective-permute-start | bytes 1228808 | tf_op jit(solution)/shard_map/ppermute | solution.py:594
  41.9 18.7 %collective-permute-start.7 = (f32[2,128,384]{2,1,0:T(8,128)S(1)}, f32[2,128,384]{2,1,0:T(8,128)S(1)}, u32[]{:S(2)}, u32[]{:S(2)}) collective-permute-start(f32[2,128,384]{2,1,0:T(8,128)S(1)} %get-tuple-element.81), channel_id=1, source_target_pairs={{0,1},{1,2},{2,3},{3,0},{4,5},{5,6},{6,7},{7,4},{8,9},{9,10},{10,1... | collective-permute-start | bytes 1179656 | tf_op jit(solution)/shard_map/ppermute | solution.py:594
  43.2 17.4 %collective-permute-start.8 = (f32[2,128,384]{2,1,0:T(8,128)S(1)}, f32[2,128,384]{2,1,0:T(8,128)S(1)}, u32[]{:S(2)}, u32[]{:S(2)}) collective-permute-start(f32[2,128,384]{2,1,0:T(8,128)S(1)} %get-tuple-element.82), channel_id=1, source_target_pairs={{0,3},{1,0},{2,1},{3,2},{4,7},{5,4},{6,5},{7,6},{8,11},{9,8},{10,9... | collective-permute-start | bytes 1179656 | tf_op jit(solution)/shard_map/ppermute | solution.py:594
  45.2 15.4 %collective-permute-start.9 = (f32[2,128,384]{2,1,0:T(8,128)S(1)}, f32[2,128,384]{2,1,0:T(8,128)S(1)}, u32[]{:S(2)}, u32[]{:S(2)}) collective-permute-start(f32[2,128,384]{2,1,0:T(8,128)S(1)} %get-tuple-element.83), channel_id=1, source_target_pairs={{0,4},{1,5},{2,6},{3,7},{4,8},{5,9},{6,10},{7,11},{8,12},{9,13},{1... | collective-permute-start | bytes 1179656 | tf_op jit(solution)/shard_map/ppermute | solution.py:594
  46.3 21.5 %collective-permute-start.10 = (f32[2,128,384]{2,1,0:T(8,128)S(1)}, f32[2,128,384]{2,1,0:T(8,128)S(1)}, u32[]{:S(2)}, u32[]{:S(2)}) collective-permute-start(f32[2,128,384]{2,1,0:T(8,128)S(1)} %get-tuple-element.86), channel_id=1, source_target_pairs={{0,2},{1,3},{2,0},{3,1},{4,6},{5,7},{6,4},{7,5},{8,10},{9,11},{10,... | collective-permute-start | bytes 1179656 | tf_op jit(solution)/shard_map/ppermute | solution.py:594
  61.0 9.2 %collective-permute-start.14 = (f32[520,128]{1,0:T(8,128)S(1)}, f32[520,128]{1,0:T(8,128)S(1)}, u32[]{:S(2)}, u32[]{:S(2)}) collective-permute-start(f32[520,128]{1,0:T(8,128)S(1)} %begin.1.rest_6_.rest_0_.w0_ref), channel_id=1, source_target_pairs={{0,2},{1,3},{2,0},{3,1},{4,6},{5,7},{6,4},{7,5},{8,10},{9,11},{10,... | collective-permute-start | bytes 798728 | tf_op jit(solution)/shard_map/ppermute | solution.py:594
  63.3 16.7 %collective-permute-start.13 = (f32[520,128]{1,0:T(8,128)S(1)}, f32[520,128]{1,0:T(8,128)S(1)}, u32[]{:S(2)}, u32[]{:S(2)}) collective-permute-start(f32[520,128]{1,0:T(8,128)S(1)} %begin.1.rest_6_.rest_0_.w0_ref), channel_id=1, source_target_pairs={{0,3},{1,0},{2,1},{3,2},{4,7},{5,4},{6,5},{7,6},{8,11},{9,8},{10,9... | collective-permute-start | bytes 798728 | tf_op jit(solution)/shard_map/ppermute | solution.py:594
  67.0 12.9 %collective-permute-start.12 = (f32[520,128]{1,0:T(8,128)S(1)}, f32[520,128]{1,0:T(8,128)S(1)}, u32[]{:S(2)}, u32[]{:S(2)}) collective-permute-start(f32[520,128]{1,0:T(8,128)S(1)} %begin.1.rest_6_.rest_0_.w0_ref), channel_id=1, source_target_pairs={{0,1},{1,2},{2,3},{3,0},{4,5},{5,6},{6,7},{7,4},{8,9},{9,10},{10,1... | collective-permute-start | bytes 798728 | tf_op jit(solution)/shard_map/ppermute | solution.py:594
  67.9 46.0 %collective-permute-start.11 = (f32[6,128,384]{2,1,0:T(8,128)S(1)}, f32[6,128,384]{2,1,0:T(8,128)S(1)}, u32[]{:S(2)}, u32[]{:S(2)}) collective-permute-start(f32[6,128,384]{2,1,0:T(8,128)S(1)} %pad_maximum_fusion), channel_id=1, source_target_pairs={{0,4},{1,5},{2,6},{3,7},{4,8},{5,9},{6,10},{7,11},{8,12},{9,13},{1... | collective-permute-start | bytes 3538952 | tf_op jit(solution)/shard_map/ppermute | solution.py:594
  80.0 33.9 %collective-permute-start.18 = (f32[2080,128]{1,0:T(8,128)S(1)}, f32[2080,128]{1,0:T(8,128)S(1)}, u32[]{:S(2)}, u32[]{:S(2)}) collective-permute-start(f32[2080,128]{1,0:T(8,128)S(1)} %pad_maximum_fusion.1), channel_id=1, source_target_pairs={{0,4},{1,5},{2,6},{3,7},{4,0},{5,1},{6,2},{7,3},{8,12},{9,13},{10,... | collective-permute-start | bytes 3194888 | tf_op jit(solution)/shard_map/ppermute | solution.py:598
  80.1 12.8 %collective-permute-start.4 = (f32[2,128,384]{2,1,0:T(8,128)S(1)}, f32[2,128,384]{2,1,0:T(8,128)S(1)}, u32[]{:S(2)}, u32[]{:S(2)}) collective-permute-start(f32[2,128,384]{2,1,0:T(8,128)S(1)} %get-tuple-element.77), channel_id=1, source_target_pairs={{0,1},{1,2},{2,3},{3,0},{4,5},{5,6},{6,7},{7,4},{8,9},{9,10},{10,1... | collective-permute-start | bytes 1179656 | tf_op jit(solution)/shard_map/ppermute | solution.py:594
  80.6 21.3 %collective-permute-start.5 = (f32[2,128,384]{2,1,0:T(8,128)S(1)}, f32[2,128,384]{2,1,0:T(8,128)S(1)}, u32[]{:S(2)}, u32[]{:S(2)}) collective-permute-start(f32[2,128,384]{2,1,0:T(8,128)S(1)} %get-tuple-element.78), channel_id=1, source_target_pairs={{0,2},{1,3},{2,0},{3,1},{4,6},{5,7},{6,4},{7,5},{8,10},{9,11},{10,... | collective-permute-start | bytes 1179656 | tf_op jit(solution)/shard_map/ppermute | solution.py:594
  84.2 19.5 %collective-permute-start.6 = (f32[2,128,384]{2,1,0:T(8,128)S(1)}, f32[2,128,384]{2,1,0:T(8,128)S(1)}, u32[]{:S(2)}, u32[]{:S(2)}) collective-permute-start(f32[2,128,384]{2,1,0:T(8,128)S(1)} %get-tuple-element.79), channel_id=1, source_target_pairs={{0,3},{1,0},{2,1},{3,2},{4,7},{5,4},{6,5},{7,6},{8,11},{9,8},{10,9... | collective-permute-start | bytes 1179656 | tf_op jit(solution)/shard_map/ppermute | solution.py:594
  92.9 21.1 %collective-permute-start.16 = (f32[1040,128]{1,0:T(8,128)S(1)}, f32[1040,128]{1,0:T(8,128)S(1)}, u32[]{:S(2)}, u32[]{:S(2)}) collective-permute-start(f32[1040,128]{1,0:T(8,128)S(1)} %pad_maximum_fusion.4), channel_id=1, source_target_pairs={{0,124},{1,125},{2,126},{3,127},{4,8},{5,9},{6,10},{7,11},{8,4},{9... | collective-permute-start | bytes 1597448 | tf_op jit(solution)/shard_map/ppermute | solution.py:598
  101.9 9.2 %collective-permute-start.15 = (f32[520,128]{1,0:T(8,128)S(1)}, f32[520,128]{1,0:T(8,128)S(1)}, u32[]{:S(2)}, u32[]{:S(2)}) collective-permute-start(f32[520,128]{1,0:T(8,128)S(1)} %begin.1.rest_6_.rest_0_.w0_ref), channel_id=1, source_target_pairs={{0,124},{1,125},{2,126},{3,127},{4,8},{5,9},{6,10},{7,11},{8,4},{9... | collective-permute-start | bytes 798728 | tf_op jit(solution)/shard_map/ppermute | solution.py:598
  103.7 10.2 %collective-permute-start.17 = (f32[520,128]{1,0:T(8,128)S(1)}, f32[520,128]{1,0:T(8,128)S(1)}, u32[]{:S(2)}, u32[]{:S(2)}) collective-permute-start(f32[520,128]{1,0:T(8,128)S(1)} %collective-permute-done.14.rest_9_.rest_3_), channel_id=1, source_target_pairs={{0,124},{1,125},{2,126},{3,127},{4,8},{5,9},{6,10},{7,11},{8,4},{9... | collective-permute-start | bytes 798728 | tf_op jit(solution)/shard_map/ppermute | solution.py:598
  116.5 9.8 %collective-permute-start.21 = (f32[520,128]{1,0:T(8,128)S(1)}, f32[520,128]{1,0:T(8,128)S(1)}, u32[]{:S(2)}, u32[]{:S(2)}) collective-permute-start(f32[520,128]{1,0:T(8,128)S(1)} %get-tuple-element.89.rest_6_.rest_8_.w1_ref), channel_id=1, source_target_pairs={{0,2},{1,3},{2,0},{3,1},{4,6},{5,7},{6,4},{7,5},{8,10},{9,11},{10,... | collective-permute-start | bytes 798728 | tf_op jit(solution)/shard_map/ppermute | solution.py:594
  116.6 9.7 %collective-permute-start.20 = (f32[520,128]{1,0:T(8,128)S(1)}, f32[520,128]{1,0:T(8,128)S(1)}, u32[]{:S(2)}, u32[]{:S(2)}) collective-permute-start(f32[520,128]{1,0:T(8,128)S(1)} %get-tuple-element.89.rest_6_.rest_8_.w1_ref), channel_id=1, source_target_pairs={{0,3},{1,0},{2,1},{3,2},{4,7},{5,4},{6,5},{7,6},{8,11},{9,8},{10,9... | collective-permute-start | bytes 798728 | tf_op jit(solution)/shard_map/ppermute | solution.py:594
  116.7 12.3 %collective-permute-start.19 = (f32[520,128]{1,0:T(8,128)S(1)}, f32[520,128]{1,0:T(8,128)S(1)}, u32[]{:S(2)}, u32[]{:S(2)}) collective-permute-start(f32[520,128]{1,0:T(8,128)S(1)} %get-tuple-element.89.rest_6_.rest_8_.w1_ref), channel_id=1, source_target_pairs={{0,1},{1,2},{2,3},{3,0},{4,5},{5,6},{6,7},{7,4},{8,9},{9,10},{10,1... | collective-permute-start | bytes 798728 | tf_op jit(solution)/shard_map/ppermute | solution.py:594
  129.1 15.4 %collective-permute-start.24 = (f32[2080,128]{1,0:T(8,128)S(1)}, f32[2080,128]{1,0:T(8,128)S(1)}, u32[]{:S(2)}, u32[]{:S(2)}) collective-permute-start(f32[2080,128]{1,0:T(8,128)S(1)} %pad_maximum_fusion.2), channel_id=1, source_target_pairs={{0,4},{1,5},{2,6},{3,7},{4,0},{5,1},{6,2},{7,3},{8,12},{9,13},{10,... | collective-permute-start | bytes 3194888 | tf_op jit(solution)/shard_map/ppermute | solution.py:598
  129.2 17.8 %collective-permute-start.26 = (f32[1040,128]{1,0:T(8,128)S(1)}, f32[1040,128]{1,0:T(8,128)S(1)}, u32[]{:S(2)}, u32[]{:S(2)}) collective-permute-start(f32[1040,128]{1,0:T(8,128)S(1)} %pad_maximum_fusion.5), channel_id=1, source_target_pairs={{0,124},{1,125},{2,126},{3,127},{4,8},{5,9},{6,10},{7,11},{8,4},{9... | collective-permute-start | bytes 1597448 | tf_op jit(solution)/shard_map/ppermute | solution.py:598
  133.5 11.0 %collective-permute-start.25 = (f32[520,128]{1,0:T(8,128)S(1)}, f32[520,128]{1,0:T(8,128)S(1)}, u32[]{:S(2)}, u32[]{:S(2)}) collective-permute-start(f32[520,128]{1,0:T(8,128)S(1)} %get-tuple-element.89.rest_6_.rest_8_.w1_ref), channel_id=1, source_target_pairs={{0,124},{1,125},{2,126},{3,127},{4,8},{5,9},{6,10},{7,11},{8,4},{9... | collective-permute-start | bytes 798728 | tf_op jit(solution)/shard_map/ppermute | solution.py:598
  134.4 12.7 %collective-permute-start.27 = (f32[520,128]{1,0:T(8,128)S(1)}, f32[520,128]{1,0:T(8,128)S(1)}, u32[]{:S(2)}, u32[]{:S(2)}) collective-permute-start(f32[520,128]{1,0:T(8,128)S(1)} %collective-permute-done.21.rest_9_.rest_11_), channel_id=1, source_target_pairs={{0,124},{1,125},{2,126},{3,127},{4,8},{5,9},{6,10},{7,11},{8,4},{9... | collective-permute-start | bytes 798728 | tf_op jit(solution)/shard_map/ppermute | solution.py:598
  138.6 1.2 collective-permute-start.22
  139.7 4.8 %collective-permute-start.23 = (f32[8,128]{1,0:T(8,128)S(1)}, f32[8,128]{1,0:T(8,128)S(1)}, u32[]{:S(2)}, u32[]{:S(2)}) collective-permute-start(f32[8,128]{1,0:T(8,128)S(1)} %add.41), channel_id=1, source_target_pairs={{0,8},{1,9},{2,10},{3,11},{4,12},{5,13},{6,14},{7,15},{8,0},{9,1},... | collective-permute-start | bytes 12296 | tf_op jit(solution)/shard_map/ppermute | solution.py:598
  147.1 29.6 %copy-start.2 = (bf16[4,1024,512]{2,1,0:T(8,128)(2,1)S(1)}, bf16[4,1024,512]{2,1,0:T(8,128)(2,1)}, u32[]{:S(2)}) copy-start(bf16[4,1024,512]{2,1,0:T(8,128)(2,1)} %get-tuple-element.60.refs_4_.solved_ref) | copy-start | bytes 12582916
  150.0 8.7 %collective-permute-start.33 = (f32[520,128]{1,0:T(8,128)S(1)}, f32[520,128]{1,0:T(8,128)S(1)}, u32[]{:S(2)}, u32[]{:S(2)}) collective-permute-start(f32[520,128]{1,0:T(8,128)S(1)} %get-tuple-element.93.rest_6_), channel_id=1, source_target_pairs={{0,3},{1,0},{2,1},{3,2},{4,7},{5,4},{6,5},{7,6},{8,11},{9,8},{10,9... | collective-permute-start | bytes 798728 | tf_op jit(solution)/shard_map/ppermute | solution.py:594
  150.7 12.4 %collective-permute-start.32 = (f32[520,128]{1,0:T(8,128)S(1)}, f32[520,128]{1,0:T(8,128)S(1)}, u32[]{:S(2)}, u32[]{:S(2)}) collective-permute-start(f32[520,128]{1,0:T(8,128)S(1)} %get-tuple-element.93.rest_6_), channel_id=1, source_target_pairs={{0,1},{1,2},{2,3},{3,0},{4,5},{5,6},{6,7},{7,4},{8,9},{9,10},{10,1... | collective-permute-start | bytes 798728 | tf_op jit(solution)/shard_map/ppermute | solution.py:594
  152.0 11.1 %collective-permute-start.28 = (f32[520,128]{1,0:T(8,128)S(1)}, f32[520,128]{1,0:T(8,128)S(1)}, u32[]{:S(2)}, u32[]{:S(2)}) collective-permute-start(f32[520,128]{1,0:T(8,128)S(1)} %get-tuple-element.93.rest_6_), channel_id=1, source_target_pairs={{0,2},{1,3},{2,0},{3,1},{4,6},{5,7},{6,4},{7,5},{8,10},{9,11},{10,... | collective-permute-start | bytes 798728 | tf_op jit(solution)/shard_map/ppermute | solution.py:594
  163.2 17.0 %collective-permute-start.34 = (f32[2080,128]{1,0:T(8,128)S(1)}, f32[2080,128]{1,0:T(8,128)S(1)}, u32[]{:S(2)}, u32[]{:S(2)}) collective-permute-start(f32[2080,128]{1,0:T(8,128)S(1)} %pad_maximum_fusion.3), channel_id=1, source_target_pairs={{0,4},{1,5},{2,6},{3,7},{4,0},{5,1},{6,2},{7,3},{8,12},{9,13},{10,... | collective-permute-start | bytes 3194888 | tf_op jit(solution)/shard_map/ppermute | solution.py:598
  163.3 5.8 %collective-permute-start.29 = (f32[8,128]{1,0:T(8,128)S(1)}, f32[8,128]{1,0:T(8,128)S(1)}, u32[]{:S(2)}, u32[]{:S(2)}) collective-permute-start(f32[8,128]{1,0:T(8,128)S(1)} %add.42), channel_id=1, source_target_pairs={{0,16},{1,17},{2,18},{3,19},{4,20},{5,21},{6,22},{7,23},{8,24},{9,... | collective-permute-start | bytes 12296 | tf_op jit(solution)/shard_map/ppermute | solution.py:598
  166.0 14.2 %collective-permute-start.35 = (f32[520,128]{1,0:T(8,128)S(1)}, f32[520,128]{1,0:T(8,128)S(1)}, u32[]{:S(2)}, u32[]{:S(2)}) collective-permute-start(f32[520,128]{1,0:T(8,128)S(1)} %get-tuple-element.93.rest_6_), channel_id=1, source_target_pairs={{0,124},{1,125},{2,126},{3,127},{4,8},{5,9},{6,10},{7,11},{8,4},{9... | collective-permute-start | bytes 798728 | tf_op jit(solution)/shard_map/ppermute | solution.py:598
  169.1 6.0 %collective-permute-start.30 = (f32[8,128]{1,0:T(8,128)S(1)}, f32[8,128]{1,0:T(8,128)S(1)}, u32[]{:S(2)}, u32[]{:S(2)}) collective-permute-start(f32[8,128]{1,0:T(8,128)S(1)} %add.43), channel_id=1, source_target_pairs={{0,32},{1,33},{2,34},{3,35},{4,36},{5,37},{6,38},{7,39},{8,40},{9,... | collective-permute-start | bytes 12296 | tf_op jit(solution)/shard_map/ppermute | solution.py:598
  169.9 15.0 %collective-permute-start.36 = (f32[1040,128]{1,0:T(8,128)S(1)}, f32[1040,128]{1,0:T(8,128)S(1)}, u32[]{:S(2)}, u32[]{:S(2)}) collective-permute-start(f32[1040,128]{1,0:T(8,128)S(1)} %pad_maximum_fusion.6), channel_id=1, source_target_pairs={{0,124},{1,125},{2,126},{3,127},{4,8},{5,9},{6,10},{7,11},{8,4},{9... | collective-permute-start | bytes 1597448 | tf_op jit(solution)/shard_map/ppermute | solution.py:598
  173.2 11.7 %collective-permute-start.37 = (f32[520,128]{1,0:T(8,128)S(1)}, f32[520,128]{1,0:T(8,128)S(1)}, u32[]{:S(2)}, u32[]{:S(2)}) collective-permute-start(f32[520,128]{1,0:T(8,128)S(1)} %collective-permute-done.28.rest_9_), channel_id=1, source_target_pairs={{0,124},{1,125},{2,126},{3,127},{4,8},{5,9},{6,10},{7,11},{8,4},{9... | collective-permute-start | bytes 798728 | tf_op jit(solution)/shard_map/ppermute | solution.py:598
  175.1 5.1 %collective-permute-start.31 = (f32[8,128]{1,0:T(8,128)S(1)}, f32[8,128]{1,0:T(8,128)S(1)}, u32[]{:S(2)}, u32[]{:S(2)}) collective-permute-start(f32[8,128]{1,0:T(8,128)S(1)} %add.44), channel_id=1, source_target_pairs={{0,64},{1,65},{2,66},{3,67},{4,68},{5,69},{6,70},{7,71},{8,72},{9,... | collective-permute-start | bytes 12296 | tf_op jit(solution)/shard_map/ppermute | solution.py:598
  176.6 8.3 %copy-start.3 = (f32[4,512,128]{2,1,0:T(8,128)S(1)}, f32[4,512,128]{2,1,0:T(8,128)}, u32[]{:S(2)}) copy-start(f32[4,512,128]{2,1,0:T(8,128)} %get-tuple-element.96.reduced_ref) | copy-start | bytes 3145732
